TPU v7x, 32 devices: a whole 2x2x4 slice. The times are simulated.
32 devices in a mesh: expert: 16 (over z, y, x), tensor: 2 (over core).
Axes of the slice: x: 2, y: 2, z: 4, core: 2. Of those that a mesh axis runs over, the one named last changes fastest.
Arguments:
- layer_input: bfloat16 [3, 1024, 2048], P(None, 'expert'), may hold values from -6 to 6
- norm_first: float32 [2048], replicated, may hold values from 0.5 to 1.5
- query_weight: bfloat16 [2048, 4096], P(None, 'tensor'), may hold values from -0.125 to 0.125
- key_weight: bfloat16 [2048, 512], P(None, 'tensor'), may hold values from -0.125 to 0.125
- value_weight: bfloat16 [2048, 512], P(None, 'tensor'), may hold values from -0.125 to 0.125
- mixing_weight: bfloat16 [4096, 2048], P('tensor'), may hold values from -2 to 2
- query_gain: float32 [128], replicated, may hold values from 0.5 to 1.5
- key_gain: float32 [128], replicated, may hold values from 0.5 to 1.5
- norm_second: float32 [2048], replicated, may hold values from 0.5 to 1.5
- router_weight: bfloat16 [2048, 16], replicated, may hold values from -0.0625 to 0.0625
- gate_weight: bfloat16 [16, 2048, 768], P('expert', None, 'tensor'), may hold values from -0.125 to 0.125
- up_weight: bfloat16 [16, 2048, 768], P('expert', None, 'tensor'), may hold values from -0.125 to 0.125
- down_weight: bfloat16 [16, 768, 2048], P('expert', 'tensor'), may hold values from -0.625 to 0.625
- routes: int32 [3, 1024, 8], P(None, 'expert'), may hold values from 0 to 15, all different within a row
- fill_order: int32 [3, 1024], P(None, 'expert'), may hold values from 0 to 3071, as said below
- cotangent: bfloat16 [3, 1024, 2048], P(None, 'expert'), may hold values from -6 to 6
Outputs:
- layer_output: bfloat16 [3, 1024, 2048], P(None, 'expert', 'tensor')
- input_grad: float32 [3, 1024, 2048], P(None, 'expert')
- first_grad: float32 [2048], replicated
- query_grad: float32 [2048, 4096], P('expert', 'tensor')
- key_grad: float32 [2048, 512], P('expert', 'tensor')
- value_grad: float32 [2048, 512], P('expert', 'tensor')
- mixing_grad: float32 [4096, 2048], P('tensor', 'expert')
- querygain_grad: float32 [128], replicated
- keygain_grad: float32 [128], replicated
- second_grad: float32 [2048], replicated
- router_grad: float32 [2048, 16], replicated
- gate_grad: float32 [16, 2048, 768], P('expert', None, 'tensor')
- up_grad: float32 [16, 2048, 768], P('expert', None, 'tensor')
- down_grad: float32 [16, 768, 2048], P('expert', 'tensor')
Inputs may be any that keep to these rules, and one draw needn't show every extreme that they name: `routes`: each token names 8 different experts. `fill_order`: holds each whole number below 3072 once; a smaller number takes a slot first.
All inputs are finite; a program needn't handle non-finite values.
Results may differ from a plain program's by a relative error of at most 0.023.
Values may be sent and summed in bfloat16 or wider, within the bound.
A program may use at most 320 MiB of HBM per device.

v0:
```python
import jax
import jax.numpy as jnp
from jax import lax
from jax.sharding import PartitionSpec as P

BLOCK = 256


epsilon = 1e-06
rope_base = 1000000.0
far_below = -1e30


def rms_scaled(values, gain_vec):
    return (
        values * lax.rsqrt(jnp.mean(values * values, axis=-1, keepdims=True) + epsilon) * gain_vec
    )


def rotary_tables(positions, head_dim):
    halfway = head_dim // 2
    exponents = jnp.arange(halfway, dtype=jnp.float32) * (2.0 / head_dim)
    inverse = jnp.exp(-exponents * jnp.log(jnp.float32(rope_base)))
    angles = positions.astype(jnp.float32)[:, None] * inverse[None, :]
    return (jnp.cos(angles), jnp.sin(angles))


def rotate(values, cosine, sine_table):
    halfway = values.shape[-1] // 2
    first = values[..., :halfway]
    latter = values[..., halfway:]
    return jnp.concatenate(
        [first * cosine - latter * sine_table, latter * cosine + first * sine_table], axis=-1
    )


def glu_value(gate_act, up_act):
    return jax.nn.silu(gate_act) * up_act


def on_device(
    layer_input,
    norm_first,
    query_weight,
    key_weight,
    value_weight,
    mixing_weight,
    query_gain,
    key_gain,
    norm_second,
    router_weight,
    gate_weight,
    up_weight,
    down_weight,
    routes,
    fill_order,
    cotangent,
):
    seq_count, seg_len, model_width = layer_input.shape
    expert_count = lax.axis_size("expert")
    tensor_count = lax.axis_size("tensor")
    expert_idx = lax.axis_index("expert")
    tensor_idx = lax.axis_index("tensor")
    head_dim = query_gain.shape[0]
    local_queries = query_weight.shape[1] // head_dim
    local_keys = key_weight.shape[1] // head_dim
    group_size = local_queries // local_keys
    seq_length = seg_len * expert_count
    top_count = routes.shape[2]
    token_count = seq_count * seg_len
    capacity = 5 * token_count * top_count // (4 * expert_count)
    half_width = model_width // tensor_count
    factor = head_dim ** (-0.5)
    inputs = layer_input.astype(jnp.float32)
    normed_f, first_back = jax.vjp(rms_scaled, inputs, norm_first)
    normed = normed_f.astype(jnp.bfloat16)
    positions = expert_idx * seg_len + jnp.arange(seg_len, dtype=jnp.int32)
    cosine, sine_table = rotary_tables(positions, head_dim)
    cosine = cosine[:, None, :]
    sine_table = sine_table[:, None, :]

    def rope_norm(raw_heads, gain_vec):
        return rotate(rms_scaled(raw_heads, gain_vec), cosine, sine_table)

    query_raw = jnp.dot(normed, query_weight, preferred_element_type=jnp.float32).reshape(
        seq_count, seg_len, local_queries, head_dim
    )
    key_raw = jnp.dot(normed, key_weight, preferred_element_type=jnp.float32).reshape(
        seq_count, seg_len, local_keys, head_dim
    )
    value_local = jnp.dot(normed, value_weight, preferred_element_type=jnp.float32).astype(
        jnp.bfloat16
    )
    query_rot, query_back = jax.vjp(rope_norm, query_raw, query_gain)
    key_rot, key_back = jax.vjp(rope_norm, key_raw, key_gain)
    key_local = key_rot.astype(jnp.bfloat16).reshape(seq_count, seg_len, local_keys * head_dim)
    key_all, value_all = (
        lax.all_gather(key_local, "expert", axis=1, tiled=True),
        lax.all_gather(value_local, "expert", axis=1, tiled=True),
    )
    key_tiles = key_all.reshape(seq_count, seq_length, local_keys, head_dim)
    value_tiles = value_all.reshape(seq_count, seq_length, local_keys, head_dim)
    query_rows = query_rot.astype(jnp.bfloat16).reshape(
        seq_count, seg_len, local_keys, group_size, head_dim
    )
    query_rows = query_rows.transpose(0, 2, 3, 1, 4).reshape(
        seq_count, local_keys, group_size * seg_len, head_dim
    )
    row_block = (
        expert_idx * seg_len + jnp.arange(group_size * seg_len, dtype=jnp.int32) % seg_len
    ) // BLOCK
    tile_len = min(512, seq_length)
    reach_end = jnp.minimum(((expert_idx + 1) * seg_len - 1) // BLOCK * BLOCK + BLOCK, seq_length)
    tile_count = (reach_end + tile_len - 1) // tile_len

    def tile_scores(tile_idx):
        offset = tile_idx * tile_len
        key_part = lax.dynamic_slice_in_dim(key_tiles, offset, tile_len, 1)
        scores = (
            jnp.einsum("shrd,skhd->shrk", query_rows, key_part, preferred_element_type=jnp.float32)
            * factor
        )
        key_block = (offset + jnp.arange(tile_len, dtype=jnp.int32)) // BLOCK
        allowed = key_block[None, :] <= row_block[:, None]
        return (scores, allowed, offset)

    stat_shape = (seq_count, local_keys, group_size * seg_len)

    def stats_step(tile_idx, state_pair):
        running_max, running_sum = state_pair
        scores, allowed, offset = tile_scores(tile_idx)
        masked = jnp.where(allowed, scores, far_below)
        new_max = jnp.maximum(running_max, jnp.max(masked, axis=-1))
        exp_terms = jnp.where(allowed, jnp.exp(masked - new_max[..., None]), 0.0)
        return (new_max, running_sum * jnp.exp(running_max - new_max) + jnp.sum(exp_terms, axis=-1))

    row_max, row_sum = lax.fori_loop(
        0,
        tile_count,
        stats_step,
        (jnp.full(stat_shape, far_below, jnp.float32), jnp.zeros(stat_shape, jnp.float32)),
    )
    log_total = row_max + jnp.log(row_sum)

    def probabilities(tile_idx):
        scores, allowed, offset = tile_scores(tile_idx)
        return (jnp.where(allowed, jnp.exp(scores - log_total[..., None]), 0.0), offset)

    def context_step(tile_idx, context_sum):
        prob_tile, offset = probabilities(tile_idx)
        value_part = lax.dynamic_slice_in_dim(value_tiles, offset, tile_len, 1)
        return context_sum + jnp.einsum(
            "shrk,skhd->shrd",
            prob_tile.astype(jnp.bfloat16),
            value_part,
            preferred_element_type=jnp.float32,
        )

    context_f = lax.fori_loop(0, tile_count, context_step, jnp.zeros(query_rows.shape, jnp.float32))
    shaped = context_f.reshape(seq_count, local_keys, group_size, seg_len, head_dim).transpose(
        0, 3, 1, 2, 4
    )
    context = shaped.reshape(seq_count, seg_len, local_queries * head_dim).astype(jnp.bfloat16)
    head_part = jnp.dot(context, mixing_weight, preferred_element_type=jnp.float32)
    residual = inputs + lax.psum(head_part.astype(jnp.bfloat16), "tensor").astype(jnp.float32)
    second_f, second_back = jax.vjp(rms_scaled, residual, norm_second)
    second = second_f.astype(jnp.bfloat16).reshape(token_count, model_width)
    logits = jnp.dot(second, router_weight, preferred_element_type=jnp.float32)
    flat_routes = routes.reshape(token_count, top_count)
    picked = (flat_routes[:, :, None] == jnp.arange(expert_count, dtype=jnp.int32)).astype(
        jnp.float32
    )
    gates = jax.nn.softmax(jnp.sum(picked * logits[:, None, :], axis=-1), axis=-1)
    usages = jnp.sum(picked, axis=1)
    ranking = fill_order.reshape(token_count)
    before = (ranking[None, :] < ranking[:, None]).astype(jnp.bfloat16)
    counts = jnp.dot(before, usages.astype(jnp.bfloat16), preferred_element_type=jnp.float32)
    slot_ids = jnp.sum(picked * counts[:, None, :], axis=-1).astype(jnp.int32)
    kept_mask = slot_ids < capacity
    kept_float = kept_mask.astype(jnp.float32)
    weighted = gates * kept_float
    places = jnp.where(kept_mask, flat_routes * capacity + slot_ids, -1)
    slot_grid = jnp.arange(expert_count * capacity, dtype=jnp.int32)
    assign = (places[:, :, None] == slot_grid).astype(jnp.bfloat16)
    placed = jnp.sum(assign, axis=1)
    combine = jnp.sum(weighted[:, :, None] * assign.astype(jnp.float32), axis=1)
    send_rows = jnp.einsum("tp,td->pd", placed, second, preferred_element_type=jnp.float32).astype(
        jnp.bfloat16
    )
    arrived = lax.all_to_all(
        send_rows.reshape(expert_count, capacity, model_width),
        "expert",
        split_axis=0,
        concat_axis=0,
        tiled=True,
    )
    arrived = arrived.reshape(expert_count * capacity, model_width)
    gate_one = gate_weight[0]
    up_one = up_weight[0]
    down_one = down_weight[0]
    gate_act = jnp.dot(arrived, gate_one, preferred_element_type=jnp.float32)
    up_act = jnp.dot(arrived, up_one, preferred_element_type=jnp.float32)
    hidden_val, glu_back = jax.vjp(glu_value, gate_act, up_act)
    hidden = hidden_val.astype(jnp.bfloat16)
    expert_part = jnp.dot(hidden, down_one, preferred_element_type=jnp.float32)
    summed = lax.psum(expert_part.astype(jnp.bfloat16), "tensor")
    returned = lax.all_to_all(
        summed.reshape(expert_count, capacity, model_width),
        "expert",
        split_axis=0,
        concat_axis=0,
        tiled=True,
    )
    returned = returned.reshape(expert_count * capacity, model_width)
    per_route = (
        jnp.take(returned, jnp.maximum(places, 0), axis=0).astype(jnp.float32)
        * kept_float[:, :, None]
    )
    mixture = residual.reshape(token_count, model_width) + jnp.sum(
        weighted[:, :, None] * per_route, axis=1
    )
    layer_output = lax.dynamic_slice_in_dim(mixture, tensor_idx * half_width, half_width, 1)
    layer_output = layer_output.astype(jnp.bfloat16).reshape(seq_count, seg_len, half_width)
    upstream = cotangent.astype(jnp.float32).reshape(token_count, model_width)
    gate_grads = jnp.sum(upstream[:, None, :] * per_route, axis=-1) * kept_float
    send_grads = jnp.einsum(
        "tp,td->pd",
        combine,
        upstream,
        precision=lax.Precision.HIGHEST,
        preferred_element_type=jnp.float32,
    ).astype(jnp.bfloat16)
    grads_in = lax.all_to_all(
        send_grads.reshape(expert_count, capacity, model_width),
        "expert",
        split_axis=0,
        concat_axis=0,
        tiled=True,
    )
    grads_in = grads_in.reshape(expert_count * capacity, model_width)
    hidden_grad = lax.dot_general(
        grads_in, down_one, (((1,), (1,)), ((), ())), preferred_element_type=jnp.float32
    )
    down_grad = jnp.einsum("rf,rd->fd", hidden, grads_in, preferred_element_type=jnp.float32)
    gate_d, up_d = glu_back(hidden_grad)
    gate_d = gate_d.astype(jnp.bfloat16)
    up_d = up_d.astype(jnp.bfloat16)
    gate_grad = jnp.einsum("rd,rf->df", arrived, gate_d, preferred_element_type=jnp.float32)
    up_grad = jnp.einsum("rd,rf->df", arrived, up_d, preferred_element_type=jnp.float32)
    row_part = lax.dot_general(
        gate_d, gate_one, (((1,), (1,)), ((), ())), preferred_element_type=jnp.float32
    )
    row_part = row_part + lax.dot_general(
        up_d, up_one, (((1,), (1,)), ((), ())), preferred_element_type=jnp.float32
    )
    row_share = lax.psum_scatter(
        row_part.reshape(expert_count, capacity, model_width).astype(jnp.bfloat16),
        "tensor",
        scatter_dimension=2,
        tiled=True,
    )
    row_home = lax.all_to_all(row_share, "expert", split_axis=0, concat_axis=0, tiled=True).reshape(
        expert_count * capacity, half_width
    )
    second_half = jnp.dot(placed, row_home, preferred_element_type=jnp.float32)
    route_grads = gates * (gate_grads - jnp.sum(gates * gate_grads, axis=-1, keepdims=True))
    logit_grads = jnp.sum(picked * route_grads[:, :, None], axis=1).astype(jnp.bfloat16)
    router_grad = jnp.einsum("td,te->de", second, logit_grads, preferred_element_type=jnp.float32)
    router_back = lax.dot_general(
        logit_grads, router_weight, (((1,), (1,)), ((), ())), preferred_element_type=jnp.float32
    )
    own_part = second_half + lax.dynamic_slice_in_dim(
        router_back, tensor_idx * half_width, half_width, 1
    )
    second_part = lax.dynamic_update_slice_in_dim(
        jnp.zeros((token_count, model_width), jnp.float32), own_part, tensor_idx * half_width, 1
    )
    residual_part, norm_part = second_back(second_part.reshape(seq_count, seg_len, model_width))
    residual_grad, second_grad = (
        lax.psum(residual_part.astype(jnp.bfloat16), "tensor").astype(jnp.float32),
        lax.psum(norm_part.astype(jnp.bfloat16), "tensor").astype(jnp.float32),
    )
    residual_grad = residual_grad + upstream.reshape(seq_count, seg_len, model_width)
    head_in = residual_grad.astype(jnp.bfloat16)
    mixing_part = jnp.einsum("std,stc->dc", head_in, context, preferred_element_type=jnp.float32)
    context_grad = lax.dot_general(
        head_in, mixing_weight, (((2,), (1,)), ((), ())), preferred_element_type=jnp.float32
    ).astype(jnp.bfloat16)
    grad_rows = context_grad.reshape(
        seq_count, seg_len, local_keys, group_size, head_dim
    ).transpose(0, 2, 3, 1, 4)
    grad_rows = grad_rows.reshape(query_rows.shape)
    delta_rows = jnp.sum(grad_rows.astype(jnp.float32) * context_f, axis=-1)
    key_shape = (seq_count, seq_length, local_keys, head_dim)

    def gradient_step(tile_idx, state_trio):
        query_acc, key_acc, value_acc = state_trio
        prob_tile, offset = probabilities(tile_idx)
        key_part = lax.dynamic_slice_in_dim(key_tiles, offset, tile_len, 1)
        value_part = lax.dynamic_slice_in_dim(value_tiles, offset, tile_len, 1)
        prob_low = prob_tile.astype(jnp.bfloat16)
        prob_grad = jnp.einsum(
            "shrd,skhd->shrk", grad_rows, value_part, preferred_element_type=jnp.float32
        )
        score_grad = (prob_tile * (prob_grad - delta_rows[..., None])).astype(jnp.bfloat16)
        query_acc = query_acc + jnp.einsum(
            "shrk,skhd->shrd", score_grad, key_part, preferred_element_type=jnp.float32
        )
        key_tile = jnp.einsum(
            "shrk,shrd->skhd", score_grad, query_rows, preferred_element_type=jnp.float32
        )
        value_tile = jnp.einsum(
            "shrk,shrd->skhd", prob_low, grad_rows, preferred_element_type=jnp.float32
        )
        key_acc = lax.dynamic_update_slice_in_dim(key_acc, key_tile, offset, 1)
        value_acc = lax.dynamic_update_slice_in_dim(value_acc, value_tile, offset, 1)
        return (query_acc, key_acc, value_acc)

    start_state = (
        jnp.zeros(query_rows.shape, jnp.float32),
        jnp.zeros(key_shape, jnp.float32),
        jnp.zeros(key_shape, jnp.float32),
    )
    query_acc, key_acc, value_acc = lax.fori_loop(0, tile_count, gradient_step, start_state)
    key_grad_all, value_grad_all = (
        lax.psum_scatter(
            (key_acc * factor).reshape(seq_count, seq_length, local_keys * head_dim),
            "expert",
            scatter_dimension=1,
            tiled=True,
        ),
        lax.psum_scatter(
            value_acc.reshape(seq_count, seq_length, local_keys * head_dim),
            "expert",
            scatter_dimension=1,
            tiled=True,
        ),
    )
    key_raw_grad, keygain_part = key_back(
        key_grad_all.reshape(seq_count, seg_len, local_keys, head_dim)
    )
    query_shaped = (
        (query_acc * factor)
        .reshape(seq_count, local_keys, group_size, seg_len, head_dim)
        .transpose(0, 3, 1, 2, 4)
    )
    query_raw_grad, querygain_part = query_back(
        query_shaped.reshape(seq_count, seg_len, local_queries, head_dim)
    )
    query_low = query_raw_grad.astype(jnp.bfloat16).reshape(
        seq_count, seg_len, local_queries * head_dim
    )
    key_low = key_raw_grad.astype(jnp.bfloat16).reshape(seq_count, seg_len, local_keys * head_dim)
    value_low = value_grad_all.astype(jnp.bfloat16)
    query_sum = jnp.einsum("std,stc->dc", normed, query_low, preferred_element_type=jnp.float32)
    keys_sum = jnp.einsum("std,stc->dc", normed, key_low, preferred_element_type=jnp.float32)
    values_sum = jnp.einsum("std,stc->dc", normed, value_low, preferred_element_type=jnp.float32)
    query_grad, key_grad, value_grad, mixing_rows = (
        lax.psum_scatter(query_sum, "expert", scatter_dimension=0, tiled=True),
        lax.psum_scatter(keys_sum, "expert", scatter_dimension=0, tiled=True),
        lax.psum_scatter(values_sum, "expert", scatter_dimension=0, tiled=True),
        lax.psum_scatter(mixing_part, "expert", scatter_dimension=0, tiled=True),
    )
    mixing_grad = mixing_rows.T
    normed_part = lax.dot_general(
        query_low, query_weight, (((2,), (1,)), ((), ())), preferred_element_type=jnp.float32
    )
    normed_part = normed_part + lax.dot_general(
        key_low, key_weight, (((2,), (1,)), ((), ())), preferred_element_type=jnp.float32
    )
    normed_part = normed_part + lax.dot_general(
        value_low, value_weight, (((2,), (1,)), ((), ())), preferred_element_type=jnp.float32
    )
    normed_grad, querygain_grad, keygain_grad = (
        lax.psum(normed_part.astype(jnp.bfloat16), "tensor").astype(jnp.float32),
        lax.psum(querygain_part.astype(jnp.bfloat16), "tensor").astype(jnp.float32),
        lax.psum(keygain_part.astype(jnp.bfloat16), "tensor").astype(jnp.float32),
    )
    input_part, first_grad = first_back(normed_grad)
    input_grad = residual_grad + input_part
    first_grad, second_grad, querygain_grad, keygain_grad, router_grad = lax.psum(
        (first_grad, second_grad, querygain_grad, keygain_grad, router_grad), "expert"
    )
    return (
        layer_output,
        input_grad,
        first_grad,
        query_grad,
        key_grad,
        value_grad,
        mixing_grad,
        querygain_grad,
        keygain_grad,
        second_grad,
        router_grad,
        gate_grad[None],
        up_grad[None],
        down_grad[None],
    )


def solution(mesh):
    return jax.shard_map(
        on_device,
        mesh=mesh,
        in_specs=(
            P(None, "expert", None),
            P(),
            P(None, "tensor"),
            P(None, "tensor"),
            P(None, "tensor"),
            P("tensor", None),
            P(),
            P(),
            P(),
            P(),
            P("expert", None, "tensor"),
            P("expert", None, "tensor"),
            P("expert", "tensor", None),
            P(None, "expert", None),
            P(None, "expert"),
            P(None, "expert", None),
        ),
        out_specs=(
            P(None, "expert", "tensor"),
            P(None, "expert", None),
            P(),
            P("expert", "tensor"),
            P("expert", "tensor"),
            P("expert", "tensor"),
            P("tensor", "expert"),
            P(),
            P(),
            P(),
            P(),
            P("expert", None, "tensor"),
            P("expert", None, "tensor"),
            P("expert", "tensor", None),
        ),
        check_vma=False,
    )
```

profile of v0, /device:TPU:8, one launch (start us, length us, event | category | flops | bytes accessed | tf_op | source)
XLA Modules:
  0.0 2149.5 jit_solution(16232758752108309662)
XLA Ops:
  31.4 41.7 %all-gather.3.cloned.1.call-done = bf16[3,1024,256]{2,1,0:T(8,128)(2,1)} async-done(((bf16[3,64,256]{2,1,0:T(8,128)(2,1)}), bf16[3,1024,256]{2,1,0:T(8,128)(2,1)}) %all-gather.3.cloned.1.call-update) | async-done | bytes 1572880 | tf_op jit(solution)/shard_map/all_gather | solution.py:98
  82.5 51.2 %all-gather.5.cloned.1.call-done = bf16[3,1024,256]{2,1,0:T(8,128)(2,1)} async-done(((bf16[3,64,256]{2,1,0:T(8,128)(2,1)}), bf16[3,1024,256]{2,1,0:T(8,128)(2,1)}) %all-gather.5.cloned.1.call-update) | async-done | bytes 1572880 | tf_op jit(solution)/shard_map/all_gather | solution.py:99
  155.6 24.8 %all-reduce.16.cloned.1.call-done = bf16[3,64,2048]{2,1,0:T(8,128)(2,1)} async-done(((bf16[3,64,2048]{2,1,0:T(8,128)(2,1)}), bf16[3,64,2048]{2,1,0:T(8,128)(2,1)}) %all-reduce.16.cloned.1.call-update) | async-done | bytes 786448 | tf_op jit(solution)/shard_map/psum | solution.py:165
  217.8 156.9 %all-to-all-done = bf16[16,120,2048]{2,1,0:T(8,128)(2,1)} async-done(((bf16[16,120,2048]{2,1,0:T(8,128)(2,1)}), bf16[16,120,2048]{2,1,0:T(8,128)(2,1)}, u32[]{:S(2)}, u32[]{:S(2)}) %all-to-all-start) | async-done | bytes 7864352 | tf_op jit(solution)/shard_map/all_to_all | solution.py:190
  374.7 15.2 all-to-all-start.2
  389.9 9.6 fusion.112
  407.8 150.8 %all-to-all-done.2 = bf16[16,120,2048]{2,1,0:T(8,128)(2,1)} async-done(((bf16[16,120,2048]{2,1,0:T(8,128)(2,1)}), bf16[16,120,2048]{2,1,0:T(8,128)(2,1)}, u32[]{:S(2)}, u32[]{:S(2)}) %all-to-all-start.2) | async-done | bytes 7864352 | tf_op jit(solution)/shard_map/all_to_all | solution.py:233
  558.7 12.0 multiply_convert_fusion
  587.9 12.3 add_convert_fusion
  600.2 20.0 all-reduce.18.cloned.1.call-done
  627.2 12.8 reduce-scatter.6.cloned.1.call-done
  640.0 157.1 %all-to-all-done.1 = bf16[16,120,2048]{2,1,0:T(8,128)(2,1)} async-done(((bf16[16,120,2048]{2,1,0:T(8,128)(2,1)}), bf16[16,120,2048]{2,1,0:T(8,128)(2,1)}, u32[]{:S(2)}, u32[]{:S(2)}) %all-to-all-start.1) | async-done | bytes 7864352 | tf_op jit(solution)/shard_map/all_to_all | solution.py:207
  797.2 15.2 all-to-all-start.3
  814.3 17.1 gather_fusion
  843.0 53.4 %all-to-all-done.3 = bf16[16,120,1024]{2,1,0:T(8,128)(2,1)} async-done(((bf16[16,120,1024]{2,1,0:T(8,128)(2,1)}), bf16[16,120,1024]{2,1,0:T(8,128)(2,1)}, u32[]{:S(2)}, u32[]{:S(2)}) %all-to-all-start.3) | async-done | bytes 3932192 | tf_op jit(solution)/shard_map/all_to_all | solution.py:262
  908.1 17.9 all-reduce.20.cloned.1.call-done
  939.9 24.0 %while.47 = (s32[]{:T(128)}, f32[3,2,512,128]{3,2,1,0:T(8,128)}, f32[3,1024,2,128]{1,3,2,0:T(8,128)}, f32[3,1024,2,128]{1,3,2,0:T(8,128)}, s32[]{:T(128)}, /*ind...) while((s32[]{:T(128)}, f32[3,2,512,128]{3,2,1,0:T(8,128)}, ...), condition=%wide.region_28.29_spmd.clone, body=%wide.region_27.28_spmd.clone.sunk | while | flops 2029669376 | bytes 75542880 | solution.py:324
  984.4 219.0 %all-reduce.25 = bf16[3,1024,256]{2,0,1:T(4,128)(2,1)S(1)} all-reduce(f32[3,1024,256]{2,0,1:T(4,128)} %copy.227), channel_id=4, replica_groups=mesh['expert'=16,'tensor'=2] {'expert'}, use_global_device_ids=true, to_apply=%region_32.33.clone | all-reduce | flops 786432 | bytes 4718592
  1210.9 38.0 %all-reduce.24.cloned.1.call-done = (f32[3,1024,256]{2,0,1:T(4,128)}, f32[2048,16]{0,1:T(8,128)}) async-done(((f32[3,1024,256]{2,0,1:T(4,128)}, f32[2048,16]{0,1:T(8,128)}), (f32[3,1024,256]{2,0,1:T(4,128)}, f32[2048,16]{0,1:T(8,128)})) %all-reduce.24.cloned.1.call-update) | async-done | bytes 3276816
  1312.8 70.8 %all-reduce.6 = (f32[2048]{0:T(1024)}, f32[128]{0:T(128)}, f32[128]{0:T(128)}, f32[2048]{0:T(1024)}) all-reduce(f32[2048]{0:T(1024)S(1)} %get-tuple-element.726, bf16[128]{0:T(256)(128)(2,1)S(1)} %get-tuple-element.792, bf16[128]{0:T(256)(128)(2,1)S(1)} %get-tuple-element.793, ...), channel_id=1, replica_groups=mesh['expert'=16,'tensor'=2] {'expert'}, use_global_device_ids=true, to_apply=%region_36.37 | all-reduce | flops 4352 | bytes 30208 | tf_op jit(solution)/shard_map/psum | solution.py:381
  1387.0 238.9 %reduce-scatter.14.cloned.1.call-done = f32[128,2048]{1,0:T(8,128)} async-done(((f32[2048,2048]{1,0:T(8,128)}), f32[128,2048]{1,0:T(8,128)}) %reduce-scatter.14.cloned.1.call-update) | async-done | bytes 1048592 | tf_op jit(solution)/shard_map/reduce_scatter | solution.py:362
  1628.4 80.0 %reduce-scatter.12.cloned.1.call-done = f32[128,256]{1,0:T(8,128)} async-done(((f32[2048,256]{1,0:T(8,128)}), f32[128,256]{1,0:T(8,128)}) %reduce-scatter.12.cloned.1.call-update) | async-done | bytes 131088 | tf_op jit(solution)/shard_map/reduce_scatter | solution.py:361
  1708.5 80.8 %reduce-scatter.10.cloned.1.call-done = f32[128,256]{1,0:T(8,128)} async-done(((f32[2048,256]{1,0:T(8,128)}), f32[128,256]{1,0:T(8,128)}) %reduce-scatter.10.cloned.1.call-update) | async-done | bytes 131088 | tf_op jit(solution)/shard_map/reduce_scatter | solution.py:360
  1789.2 352.4 %reduce-scatter.8.cloned.1.call-done = f32[128,2048]{1,0:T(8,128)} async-done(((f32[2048,2048]{1,0:T(8,128)}), f32[128,2048]{1,0:T(8,128)}) %reduce-scatter.8.cloned.1.call-update) | async-done | bytes 1048592 | tf_op jit(solution)/shard_map/reduce_scatter | solution.py:359
  (341 shorter events, 295.0 us)
Async XLA Ops:
  7.2 551.5 %copy-start = (bf16[1,384,2048]{2,1,0:T(8,128)(2,1)S(1)}, bf16[1,384,2048]{2,1,0:T(8,128)(2,1)}, u32[]{:S(2)}) copy-start(bf16[1,384,2048]{2,1,0:T(8,128)(2,1)} %param.34) | copy-start | bytes 4718596
  7.2 65.9 %all-gather.3.cloned.1.call-start = ((), (), s32[]{:S(2)}) async-start(), calls=%async_computation.9 | async-start | bytes 1671168 | tf_op jit(solution)/shard_map/all_gather | solution.py:98
  14.3 119.4 %all-gather.5.cloned.1.call-start = ((), (), s32[]{:S(2)}) async-start(), calls=%async_computation.10 | async-start | bytes 1671168 | tf_op jit(solution)/shard_map/all_gather | solution.py:99
  16.7 163.6 %all-reduce.16.cloned.1.call-start = ((), (), s32[]{:S(2)}) async-start(), calls=%async_computation.11 | async-start | bytes 1572864 | tf_op jit(solution)/shard_map/psum | solution.py:165
  197.8 176.9 %all-to-all-start = ((bf16[16,120,2048]{2,1,0:T(8,128)(2,1)}), bf16[16,120,2048]{2,1,0:T(8,128)(2,1)}, u32[]{:S(2)}, u32[]{:S(2)}) async-start(bf16[16,120,2048]{2,1,0:T(8,128)(2,1)} %bitcast.255), calls=%async_computation | async-start | bytes 15728640 | tf_op jit(solution)/shard_map/all_to_all | solution.py:190
  374.7 184.0 %all-to-all-start.2 = ((bf16[16,120,2048]{2,1,0:T(8,128)(2,1)}), bf16[16,120,2048]{2,1,0:T(8,128)(2,1)}, u32[]{:S(2)}, u32[]{:S(2)}) async-start(bf16[16,120,2048]{2,1,0:T(8,128)(2,1)} %bitcast.260), calls=%async_computation.2 | async-start | bytes 15728640 | tf_op jit(solution)/shard_map/all_to_all | solution.py:233
  389.8 230.4 %all-reduce.18.cloned.1.call-start = ((), (), s32[]{:S(2)}) async-start(), calls=%async_computation.12 | async-start | bytes 15728640 | tf_op jit(solution)/shard_map/psum | solution.py:206
  577.1 62.9 %reduce-scatter.6.cloned.1.call-start = ((), (), s32[]{:S(2)}) async-start(), calls=%async_computation.13 | async-start | bytes 11796480 | tf_op jit(solution)/shard_map/reduce_scatter | solution.py:256
  620.2 176.9 %all-to-all-start.1 = ((bf16[16,120,2048]{2,1,0:T(8,128)(2,1)}), bf16[16,120,2048]{2,1,0:T(8,128)(2,1)}, u32[]{:S(2)}, u32[]{:S(2)}) async-start(bf16[16,120,2048]{2,1,0:T(8,128)(2,1)} %all-reduce.18.cloned.1.call-done), calls=%async_computation.1 | async-start | bytes 15728640 | tf_op jit(solution)/shard_map/all_to_all | solution.py:207
  627.2 185.2 %copy-start.16 = (bf16[3,64,2048]{2,1,0:T(8,128)(2,1)S(1)}, bf16[3,64,2048]{2,1,0:T(8,128)(2,1)}, u32[]{:S(2)}) copy-start(bf16[3,64,2048]{2,1,0:T(8,128)(2,1)} %param.37) | copy-start | bytes 2359300
  797.2 99.3 %all-to-all-start.3 = ((bf16[16,120,1024]{2,1,0:T(8,128)(2,1)}), bf16[16,120,1024]{2,1,0:T(8,128)(2,1)}, u32[]{:S(2)}, u32[]{:S(2)}) async-start(bf16[16,120,1024]{2,1,0:T(8,128)(2,1)} %reduce-scatter.6.cloned.1.call-done), calls=%async_computation.4 | async-start | bytes 7864320 | tf_op jit(solution)/shard_map/all_to_all | solution.py:262
  812.3 113.7 %all-reduce.20.cloned.1.call-start = ((), (), s32[]{:S(2)}) async-start(), calls=%async_computation.14 | async-start | bytes 1572864 | tf_op jit(solution)/shard_map/psum | solution.py:280
  904.3 344.5 %all-reduce.24.cloned.1.call-start = ((), (), s32[]{:S(2)}) async-start(), calls=%async_computation.20 | async-start | bytes 8650752
  984.3 219.1 %copy-start.29 = (bf16[3,64,2048]{2,1,0:T(8,128)(2,1)S(1)}, bf16[3,64,2048]{2,1,0:T(8,128)(2,1)}, u32[]{:S(2)}) copy-start(bf16[3,64,2048]{2,1,0:T(8,128)(2,1)} %reshape.492) | copy-start | bytes 2359300
  984.3 326.6 %all-reduce.22.cloned.1.call-start = ((), (), s32[]{:S(2)}) async-start(), calls=%async_computation.15 | async-start | bytes 1572864 | tf_op jit(solution)/shard_map/psum | solution.py:375
  1210.9 39.7 %copy-start.22 = (f32[3,64,2,128]{3,2,1,0:T(2,128)S(1)}, f32[3,64,2,128]{3,2,1,0:T(2,128)}, u32[]{:S(2)}) copy-start(f32[3,64,2,128]{3,2,1,0:T(2,128)} %copy-done.21) | copy-start | bytes 589828
  1210.9 39.7 %copy-start.39 = (f32[3,64,2]{2,1,0:T(8,128)S(1)}, f32[3,64,2]{2,1,0:T(8,128)}, u32[]{:S(2)}) copy-start(f32[3,64,2]{2,1,0:T(8,128)} %copy-done.38) | copy-start | bytes 4612
  1255.5 370.3 %reduce-scatter.14.cloned.1.call-start = ((), (), s32[]{:S(2)}) async-start(), calls=%async_computation.19 | async-start | bytes 17825792 | tf_op jit(solution)/shard_map/reduce_scatter | solution.py:362
  1265.1 443.3 %reduce-scatter.12.cloned.1.call-start = ((), (), s32[]{:S(2)}) async-start(), calls=%async_computation.18 | async-start | bytes 2228224 | tf_op jit(solution)/shard_map/reduce_scatter | solution.py:361
  1268.1 521.1 %reduce-scatter.10.cloned.1.call-start = ((), (), s32[]{:S(2)}) async-start(), calls=%async_computation.17 | async-start | bytes 2228224 | tf_op jit(solution)/shard_map/reduce_scatter | solution.py:360
  1270.1 871.6 %reduce-scatter.8.cloned.1.call-start = ((), (), s32[]{:S(2)}) async-start(), calls=%async_computation.16 | async-start | bytes 17825792 | tf_op jit(solution)/shard_map/reduce_scatter | solution.py:359
  1307.6 76.0 %copy-start.67 = (f32[3,64]{1,0:T(4,128)S(1)}, f32[3,64]{1,0:T(4,128)}, u32[]{:S(2)}) copy-start(f32[3,64]{1,0:T(4,128)} %copy-done.66) | copy-start | bytes 2308
  1383.6 758.7 %copy-start.1 = (bf16[1,384,2048]{2,1,0:T(8,128)(2,1)S(1)}, bf16[1,384,2048]{2,1,0:T(8,128)(2,1)}, u32[]{:S(2)}) copy-start(bf16[1,384,2048]{2,1,0:T(8,128)(2,1)} %param.34) | copy-start | bytes 4718596
  1387.0 754.7 %copy-start.54 = (f32[2048,16]{0,1:T(8,128)S(1)}, f32[2048,16]{0,1:T(8,128)}, u32[]{:S(2)}) copy-start(f32[2048,16]{0,1:T(8,128)} %get-tuple-element.1136) | copy-start | bytes 393220
  (72 other events, 350.1 us)
Sparse Core Ops, SparseCore 0:
  14.5 58.5 all-gather.2
  76.4 57.2 all-gather.4
  155.3 25.0 all-reduce.15
  577.2 42.9 all-reduce.17
  622.4 17.6 reduce-scatter.5
  904.4 21.5 all-reduce.19
  984.4 264.4 all-reduce.23
  1255.6 17.8 all-reduce.21
  1275.9 349.9 reduce-scatter.13
  1628.7 79.7 reduce-scatter.11
  1711.4 77.7 reduce-scatter.9
  1792.1 349.5 reduce-scatter.7
where the time goes:
time: 2160 us; the launch traced here: 2150 us
  waiting for transfers between devices  1480 us (69%)
  blocking collectives  292 us (14%)
  matrix products  184 us (9%)
  local copies, waits for them, and re-layouts  78.4 us (4%)
  other arithmetic  55.8 us (3%)
  starting transfers between devices  45.4 us (2%)
    reduce_scatter x1, waiting for transfers between devices, on_device(): lax.psum_scatter(query_sum, 'expert', scatter_dimension=0, tiled=True)  352 us
    reduce_scatter x1, waiting for transfers between devices, on_device(): lax.psum_scatter(mixing_part, 'expert', scatter_dimension=0, tiled=True)  239 us
    unnamed x1, blocking collectives  219 us
    all_to_all x1, waiting for transfers between devices, on_device(): lax.all_to_all(summed.reshape(expert_count, capacity, model_width), 'expe...  157 us
    all_to_all x1, waiting for transfers between devices, on_device(): lax.all_to_all(send_rows.reshape(expert_count, capacity, model_width), 'e...  157 us
    all_to_all x1, waiting for transfers between devices, on_device(): lax.all_to_all(send_grads.reshape(expert_count, capacity, model_width), '...  151 us
    reduce_scatter x1, waiting for transfers between devices, on_device(): lax.psum_scatter(keys_sum, 'expert', scatter_dimension=0, tiled=True)  80.8 us
    reduce_scatter x1, waiting for transfers between devices, on_device(): lax.psum_scatter(values_sum, 'expert', scatter_dimension=0, tiled=True)  80 us
  transfers between devices with their start and end apart: 16, of which 15 were waited for; matrix products, arithmetic and copies ran while one was open for 8% of the time, Pallas kernels for 0%

commit v1 on v0

--- a/solution.py
+++ b/solution.py
@@ -1,9 +1,1435 @@
+import functools
+
 import jax
 import jax.numpy as jnp
 from jax import lax
+from jax.experimental import pallas as pl
+from jax.experimental.pallas import tpu as pltpu
 from jax.sharding import PartitionSpec as P
 
 BLOCK = 256
+MESH = pl.DeviceIdType.MESH
+ROOM = 56 * 2**20
+
+
+class Spot:
+    def __init__(self):
+        self.e = lax.axis_index("expert")
+        self.t = lax.axis_index("tensor")
+        self.a = lax.div(self.e, 4)
+        y = lax.rem(lax.div(self.e, 2), 2)
+        x = lax.rem(self.e, 2)
+        self.b = x + self.t * (y - x)
+        self.c = y + self.t * (x - y)
+
+    def index(self, a, b, c):
+        y = c + self.t * (b - c)
+        x = b + self.t * (c - b)
+        return a * 4 + y * 2 + x
+
+    def at(self, a, b, c):
+        return (self.index(a, b, c), self.t)
+
+    def core(self):
+        return (self.e, 1 - self.t)
+
+    def greet(self, planes, chain, flat, share):
+        barrier = pltpu.get_barrier_semaphore()
+        total = 0
+
+        def call(who):
+            pl.semaphore_signal(barrier, inc=1, device_id=who, device_id_type=MESH)
+
+        if share:
+            call(self.core())
+            total = total + 1
+        if flat:
+            call(self.at(self.a, 1 - self.b, self.c))
+            call(self.at(self.a, self.b, 1 - self.c))
+            total = total + 2
+        if chain:
+            up = self.a + 1 < planes
+            down = self.a > 0
+
+            @pl.when(up)
+            def _():
+                call(self.at(self.a + 1, self.b, self.c))
+
+            @pl.when(down)
+            def _():
+                call(self.at(self.a - 1, self.b, self.c))
+
+            total = total + up.astype(jnp.int32) + down.astype(jnp.int32)
+        pl.semaphore_wait(barrier, total)
+
+
+def push(src, dst, send_sem, recv_sem, who):
+    return pltpu.make_async_remote_copy(
+        src_ref=src, dst_ref=dst, send_sem=send_sem, recv_sem=recv_sem, device_id=who, device_id_type=MESH
+    )
+
+
+def offsets(planes):
+    out = [0]
+    for step in range(1, planes):
+        out += [step, -step]
+    return out
+
+
+def gather_kernel(planes, share, x_ref, o_ref, ssem, rsem, csem, lsem):
+    me = Spot()
+    rows = x_ref.shape[0]
+    half = rows // 2 if share else rows
+    start = pl.multiple_of(me.t * half, half) if share else 0
+    span = pl.ds(start, half)
+    own = me.index(me.a, me.b, me.c)
+
+    def copy(idx, kind, src=None):
+        who = {
+            0: me.at(me.a + 1, me.b, me.c),
+            1: me.at(me.a - 1, me.b, me.c),
+            2: me.at(me.a, 1 - me.b, me.c),
+            3: me.at(me.a, me.b, 1 - me.c),
+            4: me.core(),
+        }[kind]
+        there = o_ref.at[idx, span]
+        landed = csem if kind == 4 else rsem
+        return push(there if src is None else src, there, ssem.at[idx, kind], landed.at[idx], who)
+
+    local = pltpu.make_async_copy(x_ref, o_ref.at[own], lsem)
+    local.start()
+    me.greet(planes, True, True, share)
+
+    def each(act):
+        for da in offsets(planes):
+            sa = me.a + da
+
+            @pl.when((sa >= 0) & (sa < planes))
+            def _(da=da, sa=sa):
+                idx = me.index(sa, me.b, me.c)
+                src = x_ref.at[span] if da == 0 else None
+                if da != 0 and act == "start":
+                    copy(idx, 2).wait_recv()
+                if da <= 0:
+
+                    @pl.when(me.a + 1 < planes)
+                    def _():
+                        run(copy(idx, 0, src))
+
+                if da >= 0:
+
+                    @pl.when(me.a > 0)
+                    def _():
+                        run(copy(idx, 1, src))
+
+                run(copy(idx, 3, src))
+                run(copy(idx, 2, src))
+                if share and da != 0:
+                    run(copy(idx, 4))
+                idx = me.index(sa, 1 - me.b, me.c)
+                if act == "start":
+                    copy(idx, 2).wait_recv()
+                run(copy(idx, 3))
+                if share:
+                    run(copy(idx, 4))
+
+        for da in offsets(planes):
+            sa = me.a + da
+
+            @pl.when((sa >= 0) & (sa < planes))
+            def _(da=da, sa=sa):
+                for sb in (me.b, 1 - me.b):
+                    idx = me.index(sa, sb, 1 - me.c)
+                    if act == "start":
+                        copy(idx, 2).wait_recv()
+                    if share:
+                        run(copy(idx, 4))
+
+    def run(c):
+        c.start() if mode[0] == "start" else c.wait_send()
+
+    mode = ["start"]
+    each("start")
+    mode[0] = "wait"
+    each("wait")
+    if share:
+        other = pl.ds(pl.multiple_of((1 - me.t) * half, half), half)
+        for da in offsets(planes):
+            sa = me.a + da
+
+            @pl.when((sa >= 0) & (sa < planes))
+            def _(da=da, sa=sa):
+                for sb in (me.b, 1 - me.b):
+                    for sc in (me.c, 1 - me.c):
+                        if da == 0 and sb is me.b and sc is me.c:
+                            continue
+                        idx = me.index(sa, sb, sc)
+                        there = o_ref.at[idx, other]
+                        push(there, there, ssem.at[idx, 4], csem.at[idx], me.core()).wait_recv()
+    local.wait()
+
+
+def gather_rows(x, planes, share, cid, name):
+    count = planes * 4
+    return pl.pallas_call(
+        functools.partial(gather_kernel, planes, share),
+        out_shape=jax.ShapeDtypeStruct((count,) + x.shape, x.dtype),
+        in_specs=[pl.BlockSpec(memory_space=pl.ANY)],
+        out_specs=pl.BlockSpec(memory_space=pl.ANY),
+        scratch_shapes=[
+            pltpu.SemaphoreType.DMA((count, 5)),
+            pltpu.SemaphoreType.DMA((count,)),
+            pltpu.SemaphoreType.DMA((count,)),
+            pltpu.SemaphoreType.DMA,
+        ],
+        compiler_params=pltpu.CompilerParams(collective_id=cid, has_side_effects=True),
+        name=name,
+    )(x)
+
+
+def add_rows(target, parts):
+    rows = target.shape[0]
+    step = 32 if rows % 32 == 0 else 16
+
+    def body(i, carry):
+        at = pl.ds(pl.multiple_of(i * step, step), step)
+        total = parts[0][at, :].astype(jnp.float32)
+        for part in parts[1:]:
+            total = total + part[at, :].astype(jnp.float32)
+        target[at, :] = total.astype(target.dtype)
+        return carry
+
+    lax.fori_loop(0, rows // step, body, 0)
+
+
+def far_first(a, planes, i):
+    last = planes - 1
+    low = jnp.where(i < last - a, last - i, jnp.where(i < last, i - (last - a), a))
+    high = jnp.where(i < a, i, jnp.where(i < last, last - (i - a), a))
+    return jnp.where(2 * a < last, low, high)
+
+
+def scatter_kernel(
+    planes, flat, share, p_ref, o_ref, mine, land0, landc, landb, landa, lsem, csem, rsem, ssem, esem
+):
+    me = Spot()
+    rows = p_ref.shape[1]
+    half = rows // 2 if share else rows
+    ours = pl.ds(pl.multiple_of(me.t * half, half), half) if share else pl.ds(0, half)
+    other = pl.ds(pl.multiple_of((1 - me.t) * half, half), half)
+    order = [far_first(me.a, planes, i) for i in range(planes)]
+
+    def block(sa, sb, sc):
+        return me.index(sa, sb, sc) if flat else sa
+
+    def load(idx):
+        return pltpu.make_async_copy(p_ref.at[idx, ours], mine.at[idx], lsem.at[idx])
+
+    def trade(idx):
+        return push(p_ref.at[idx, other], land0.at[idx], ssem.at[0, idx], csem.at[idx], me.core())
+
+    spots = [(sb, sc) for sc in (1 - me.c, me.c) for sb in (1 - me.b, me.b)] if flat else [(me.b, me.c)]
+    for sa in order:
+        for sb, sc in spots:
+            load(block(sa, sb, sc)).start()
+    me.greet(planes, True, flat, share)
+    if share:
+        for sa in order:
+            for sb, sc in spots:
+                trade(block(sa, sb, sc)).start()
+
+    def send_c(sa, sb):
+        slot = sa * 2 + sb
+        return push(
+            mine.at[me.index(sa, sb, 1 - me.c)],
+            landc.at[slot],
+            ssem.at[1, slot],
+            rsem.at[0, slot],
+            me.at(me.a, me.b, 1 - me.c),
+        )
+
+    def send_b(sa):
+        return push(
+            mine.at[me.index(sa, 1 - me.b, me.c)],
+            landb.at[sa],
+            ssem.at[2, sa],
+            rsem.at[1, sa],
+            me.at(me.a, 1 - me.b, me.c),
+        )
+
+    def send_a(sa, up):
+        arrive = me.a + 1 if up else me.a - 1
+        slot = sa if up else jnp.where(sa == arrive, planes, sa)
+        return push(
+            mine.at[block(sa, me.b, me.c)],
+            landa.at[slot],
+            ssem.at[3, sa],
+            rsem.at[2, slot],
+            me.at(arrive, me.b, me.c),
+        )
+
+    if flat:
+        for sa in order:
+            for sb, sc in spots:
+                idx = me.index(sa, sb, sc)
+                load(idx).wait()
+                if share:
+                    trade(idx).wait_recv()
+                    add_rows(mine.at[idx], [mine.at[idx], land0.at[idx]])
+                if sc is spots[0][1]:
+                    send_c(sa, sb).start()
+
+    def from_c(sa):
+        for sb in (1 - me.b, me.b):
+            slot = sa * 2 + sb
+            push(landc.at[slot], landc.at[slot], ssem.at[1, slot], rsem.at[0, slot], me.at(me.a, me.b, 1 - me.c)).wait_recv()
+            idx = me.index(sa, sb, me.c)
+            add_rows(mine.at[idx], [mine.at[idx], landc.at[slot]])
+            if sb is not me.b:
+                send_b(sa).start()
+
+    def along(i, sa):
+        idx = block(sa, me.b, me.c)
+        parts = [mine.at[idx]]
+        if flat:
+            push(landb.at[sa], landb.at[sa], ssem.at[2, sa], rsem.at[1, sa], me.at(me.a, 1 - me.b, me.c)).wait_recv()
+            parts = parts + [landb.at[sa]]
+        else:
+            load(idx).wait()
+
+        def landed(slot):
+            push(landa.at[slot], landa.at[slot], ssem.at[3, 0], rsem.at[2, slot], me.at(me.a, me.b, me.c)).wait_recv()
+
+        if i < planes - 1:
+            up = sa > me.a
+            inner = (up & (me.a > 0)) | (jnp.logical_not(up) & (me.a + 1 < planes))
+
+            @pl.when(inner)
+            def _():
+                landed(sa)
+                add_rows(mine.at[idx], parts + [landa.at[sa]])
+
+            if len(parts) > 1:
+
+                @pl.when(jnp.logical_not(inner))
+                def _():
+                    add_rows(mine.at[idx], parts)
+
+            @pl.when(up)
+            def _():
+                send_a(sa, True).start()
+
+            @pl.when(jnp.logical_not(up))
+            def _():
+                send_a(sa, False).start()
+
+        else:
+            target = o_ref.at[ours] if share else o_ref
+
+            @pl.when(me.a > 0)
+            def _():
+                landed(me.a)
+
+            @pl.when(me.a + 1 < planes)
+            def _():
+                landed(planes)
+
+            @pl.when((me.a > 0) & (me.a + 1 < planes))
+            def _():
+                add_rows(target, parts + [landa.at[me.a], landa.at[planes]])
+
+            @pl.when(me.a == 0)
+            def _():
+                add_rows(target, parts + [landa.at[planes]])
+
+            @pl.when(me.a + 1 == planes)
+            def _():
+                add_rows(target, parts + [landa.at[me.a]])
+
+    for i in range(planes + 1):
+        if flat and i < planes:
+            from_c(order[i])
+        if i > 0:
+            along(i - 1, order[i - 1])
+    if share:
+        done = push(o_ref.at[ours], o_ref.at[ours], esem.at[0], esem.at[1], me.core())
+        done.start()
+    for i, sa in enumerate(order):
+        if flat:
+            for sb, sc in spots:
+                if share:
+                    trade(me.index(sa, sb, sc)).wait_send()
+            for sb in (1 - me.b, me.b):
+                send_c(sa, sb).wait_send()
+            send_b(sa).wait_send()
+        if i < planes - 1:
+            send_a(sa, False).wait_send()
+    if share:
+        done.wait_send()
+        push(o_ref.at[other], o_ref.at[other], esem.at[0], esem.at[1], me.core()).wait_recv()
+
+
+def scatter_sum(p, planes, flat, share, out_type, cid, name):
+    count, rows, width = p.shape
+    half = rows // 2 if share else rows
+    one = (16, width)
+
+    def space(use, slots):
+        return pltpu.VMEM((slots, half, width), p.dtype) if use else pltpu.VMEM((1,) + one, p.dtype)
+
+    return pl.pallas_call(
+        functools.partial(scatter_kernel, planes, flat, share),
+        out_shape=jax.ShapeDtypeStruct((rows, width), out_type),
+        in_specs=[pl.BlockSpec(memory_space=pl.ANY)],
+        out_specs=pl.BlockSpec(memory_space=pltpu.VMEM),
+        scratch_shapes=[
+            space(True, count),
+            space(share, count),
+            space(flat, 2 * planes),
+            space(flat, planes),
+            space(True, planes + 1),
+            pltpu.SemaphoreType.DMA((count,)),
+            pltpu.SemaphoreType.DMA((count,)),
+            pltpu.SemaphoreType.DMA((3, max(2 * planes, planes + 1))),
+            pltpu.SemaphoreType.DMA((4, max(count, 2 * planes))),
+            pltpu.SemaphoreType.DMA((2,)),
+        ],
+        compiler_params=pltpu.CompilerParams(collective_id=cid, has_side_effects=True, vmem_limit_bytes=ROOM),
+        name=name,
+    )(p)
+
+
+def swap_kernel(x_ref, o_ref, sems):
+    me = Spot()
+    me.greet(1, False, False, True)
+    c = push(x_ref, o_ref, sems.at[0], sems.at[1], me.core())
+    c.start()
+    c.wait()
+
+
+def swap_cores(x, cid, name):
+    return pl.pallas_call(
+        swap_kernel,
+        out_shape=jax.ShapeDtypeStruct(x.shape, x.dtype),
+        in_specs=[pl.BlockSpec(memory_space=pl.ANY)],
+        out_specs=pl.BlockSpec(memory_space=pl.ANY),
+        scratch_shapes=[pltpu.SemaphoreType.DMA((2,))],
+        compiler_params=pltpu.CompilerParams(collective_id=cid, has_side_effects=True),
+        name=name,
+    )(x)
+
+
+def plane_kernel(g_ref, s_ref, go_ref, so_ref, ssem, rsem, lsem):
+    me = Spot()
+    q = lax.rem(me.e, 4)
+    base = me.e - q
+
+    def spot(b, c):
+        return me.index(0, b, c)
+
+    near = [(1 - me.b, me.c), (me.b, 1 - me.c), (1 - me.b, 1 - me.c)]
+    barrier = pltpu.get_barrier_semaphore()
+    for b, c in near:
+        pl.semaphore_signal(barrier, inc=1, device_id=(base + spot(b, c), me.t), device_id_type=MESH)
+    keep = [
+        pltpu.make_async_copy(g_ref, go_ref.at[q], lsem.at[0]),
+        pltpu.make_async_copy(s_ref.at[q], so_ref.at[q], lsem.at[1]),
+    ]
+    for k in keep:
+        k.start()
+    pl.semaphore_wait(barrier, 3)
+    whole = [
+        push(g_ref, go_ref.at[q], ssem.at[i], rsem.at[i], (base + spot(*near[i]), me.t)) for i in range(2)
+    ]
+    parts = [
+        push(s_ref.at[spot(*near[i])], so_ref.at[q], ssem.at[3 + i], rsem.at[3 + i], (base + spot(*near[i]), me.t))
+        for i in range(3)
+    ]
+    for k in whole + parts:
+        k.start()
+    whole[0].wait_recv()
+    source = spot(*near[0])
+    relay = push(go_ref.at[source], go_ref.at[source], ssem.at[2], rsem.at[2], (base + spot(*near[1]), me.t))
+    relay.start()
+    whole[0].wait_send()
+    whole[1].wait()
+    for k in parts:
+        k.wait()
+    relay.wait()
+    for k in keep:
+        k.wait()
+
+
+def plane_exchange(g, s, cid, name):
+    return pl.pallas_call(
+        plane_kernel,
+        out_shape=[jax.ShapeDtypeStruct((4,) + g.shape, g.dtype), jax.ShapeDtypeStruct(s.shape, s.dtype)],
+        in_specs=[pl.BlockSpec(memory_space=pl.ANY)] * 2,
+        out_specs=[pl.BlockSpec(memory_space=pl.ANY)] * 2,
+        scratch_shapes=[
+            pltpu.SemaphoreType.DMA((6,)),
+            pltpu.SemaphoreType.DMA((6,)),
+            pltpu.SemaphoreType.DMA((2,)),
+        ],
+        compiler_params=pltpu.CompilerParams(collective_id=cid, has_side_effects=True),
+        name=name,
+    )(g, s)
+
+
+def total_kernel(count, x_ref, o_ref, land, send, ssem, rsem):
+    me = Spot()
+    rows = x_ref.shape[0]
+    half = rows // 2
+    ours = pl.ds(pl.multiple_of(me.t * half, half), half)
+    other = pl.ds(pl.multiple_of((1 - me.t) * half, half), half)
+    steps = []
+    bit = 1
+    while bit < count:
+        steps.append(me.e + bit * (1 - 2 * lax.rem(lax.div(me.e, bit), 2)))
+        bit *= 2
+    barrier = pltpu.get_barrier_semaphore()
+    for who in steps:
+        pl.semaphore_signal(barrier, inc=1, device_id=(who, me.t), device_id_type=MESH)
+    pl.semaphore_signal(barrier, inc=1, device_id=me.core(), device_id_type=MESH)
+    pl.semaphore_wait(barrier, len(steps) + 1)
+    send[0] = x_ref[ours, :]
+    copies = []
+    for i, who in enumerate(steps):
+        c = push(send.at[i], land.at[i], ssem.at[i], rsem.at[i], (who, me.t))
+        c.start()
+        copies.append(c)
+        c.wait_recv()
+        if i + 1 < len(steps):
+            send[i + 1] = send[i] + land[i]
+        else:
+            o_ref[ours, :] = send[i] + land[i]
+    last = push(o_ref.at[ours], o_ref.at[ours], ssem.at[len(steps)], rsem.at[len(steps)], me.core())
+    last.start()
+    for c in copies:
+        c.wait_send()
+    last.wait_send()
+    push(o_ref.at[other], o_ref.at[other], ssem.at[len(steps)], rsem.at[len(steps)], me.core()).wait_recv()
+
+
+def total_over(x, count, cid, name):
+    steps = count.bit_length() - 1
+    half = (x.shape[0] // 2, x.shape[1])
+    return pl.pallas_call(
+        functools.partial(total_kernel, count),
+        out_shape=jax.ShapeDtypeStruct(x.shape, x.dtype),
+        in_specs=[pl.BlockSpec(memory_space=pltpu.VMEM)],
+        out_specs=pl.BlockSpec(memory_space=pltpu.VMEM),
+        scratch_shapes=[
+            pltpu.VMEM((steps,) + half, x.dtype),
+            pltpu.VMEM((steps,) + half, x.dtype),
+            pltpu.SemaphoreType.DMA((steps + 1,)),
+            pltpu.SemaphoreType.DMA((steps + 1,)),
+        ],
+        compiler_params=pltpu.CompilerParams(collective_id=cid, has_side_effects=True),
+        name=name,
+    )(x)
+
+
+def over(first, second, contract):
+    return lax.dot_general(first, second, (contract, ((), ())), preferred_element_type=jnp.float32)
+
+
+NN = ((1,), (0,))
+NT = ((1,), (1,))
+TN = ((0,), (0,))
+
+
+def experts_kernel(
+    planes,
+    parcel_ref,
+    up_ref,
+    gate_in,
+    lift_in,
+    down_in,
+    all_ref,
+    other_ref,
+    share_ref,
+    home_ref,
+    gate_sum,
+    lift_sum,
+    down_sum,
+    wide,
+    down,
+    wide_half,
+    down_half,
+    pbuf,
+    ubuf,
+    xbuf,
+    gbuf,
+    vbuf,
+    sbuf,
+    wbuf,
+    rbuf,
+    hbuf,
+    dbuf,
+    gates,
+    scores,
+    stage,
+    mine,
+    landc,
+    landb,
+    landa,
+    gsend,
+    grecv,
+    gcore,
+    usend,
+    urecv,
+    wsend,
+    wrecv,
+    wload,
+    hsend,
+    hrecv,
+    ssem,
+    rsem,
+    lsem,
+    osem,
+    esem,
+):
+    me = Spot()
+    f32, bf16 = jnp.float32, jnp.bfloat16
+    tokens, packed = parcel_ref.shape
+    hidden, width = down_in.shape
+    notes_width = packed - width
+    count = planes * 4
+    half = tokens // 2
+    side = width // 2
+    slots = sbuf.shape[2]
+    own = me.index(me.a, me.b, me.c)
+    ours = pl.ds(pl.multiple_of(me.t * half, half), half)
+    theirs = pl.ds(pl.multiple_of((1 - me.t) * half, half), half)
+    our_side = pl.ds(pl.multiple_of(me.t * side, side), side)
+    their_side = pl.ds(pl.multiple_of((1 - me.t) * side, side), side)
+    spots = [(sb, sc) for sc in (1 - me.c, me.c) for sb in (1 - me.b, me.b)]
+
+    def near(i):
+        return far_first(me.a, planes, planes - 1 - i)
+
+
+    def carry(idx, kind, src=None):
+        who = {
+            0: me.at(me.a + 1, me.b, me.c),
+            1: me.at(me.a - 1, me.b, me.c),
+            2: me.at(me.a, 1 - me.b, me.c),
+            3: me.at(me.a, me.b, 1 - me.c),
+            4: me.core(),
+        }[kind]
+        there = all_ref.at[idx, ours]
+        landed = gcore if kind == 4 else grecv
+        return push(there if src is None else src, there, gsend.at[idx, kind], landed.at[idx], who)
+
+    def relay(sa, act, first):
+        idx = me.index(sa, me.b, me.c)
+        src = parcel_ref.at[ours] if first else None
+        if act and not first:
+            carry(idx, 2).wait_recv()
+        run = (lambda c: c.start()) if act else (lambda c: c.wait_send())
+
+        @pl.when((sa <= me.a) & (me.a + 1 < planes))
+        def _():
+            run(carry(idx, 0, src))
+
+        @pl.when((sa >= me.a) & (me.a > 0))
+        def _():
+            run(carry(idx, 1, src))
+
+        run(carry(idx, 3, src))
+        run(carry(idx, 2, src))
+        if not first:
+            run(carry(idx, 4))
+        idx = me.index(sa, 1 - me.b, me.c)
+        if act:
+            carry(idx, 2).wait_recv()
+        run(carry(idx, 3))
+        run(carry(idx, 4))
+
+    def across(sa, act):
+        for sb in (me.b, 1 - me.b):
+            idx = me.index(sa, sb, 1 - me.c)
+            if act:
+                carry(idx, 2).wait_recv()
+                carry(idx, 4).start()
+            else:
+                carry(idx, 4).wait_send()
+
+    def from_core(sa):
+        for sb, sc in spots:
+            idx = me.index(sa, sb, sc)
+
+            @pl.when(idx != own)
+            def _(idx=idx):
+                there = all_ref.at[idx, theirs]
+                push(there, there, gsend.at[idx, 4], gcore.at[idx], me.core()).wait_recv()
+
+    def upstream(sa):
+        group = pl.ds(sa * 4, 4)
+        return push(up_ref.at[group], other_ref.at[group], usend.at[sa], urecv.at[sa], me.core())
+
+
+    def part(ref, base, size):
+        return ref.at[:, pl.ds(pl.multiple_of(base, 128), size)]
+
+    down_rows = down_half.at[pl.ds(pl.multiple_of(me.t * hidden, 128), hidden)]
+    wide_cols = [part(wide_half, me.t * 2 * hidden + i * hidden, hidden) for i in range(2)]
+    sources = [gate_in, lift_in]
+    loads = [pltpu.make_async_copy(sources[i], wide.at[:, i * hidden : (i + 1) * hidden], wload.at[i]) for i in range(2)]
+    loads += [pltpu.make_async_copy(sources[i].at[our_side], wide_cols[i], wload.at[2 + i]) for i in range(2)]
+    loads += [
+        pltpu.make_async_copy(down_in, down, wload.at[4]),
+        pltpu.make_async_copy(down_in.at[:, our_side], down_rows, wload.at[5]),
+    ]
+    pushes = [push(sources[i].at[their_side], wide_cols[i], wsend.at[i], wrecv.at[i], me.core()) for i in range(2)]
+    pushes += [push(down_in.at[:, their_side], down_rows, wsend.at[2], wrecv.at[2], me.core())]
+
+
+    def send_c(sa, sb):
+        slot = sa * 2 + sb
+        src = mine.at[me.index(sa, sb, 1 - me.c)]
+        return push(src, landc.at[slot], ssem.at[0, slot], rsem.at[0, slot], me.at(me.a, me.b, 1 - me.c))
+
+    def send_b(sa):
+        src = mine.at[me.index(sa, 1 - me.b, me.c)]
+        return push(src, landb.at[sa], ssem.at[1, sa], rsem.at[1, sa], me.at(me.a, 1 - me.b, me.c))
+
+    def send_a(sa, up):
+        arrive = me.a + 1 if up else me.a - 1
+        slot = sa if up else jnp.where(sa == arrive, planes, sa)
+        src = mine.at[me.index(sa, me.b, me.c)]
+        return push(src, landa.at[slot], ssem.at[2, sa], rsem.at[2, slot], me.at(arrive, me.b, me.c))
+
+    def from_c(sa):
+        for sb in (1 - me.b, me.b):
+            slot = sa * 2 + sb
+            push(landc.at[slot], landc.at[slot], ssem.at[0, slot], rsem.at[0, slot], me.at(me.a, me.b, 1 - me.c)).wait_recv()
+            idx = me.index(sa, sb, me.c)
+            add_rows(mine.at[idx], [mine.at[idx], landc.at[slot]])
+            if sb is not me.b:
+                send_b(sa).start()
+
+    def along(i, sa):
+        idx = me.index(sa, me.b, me.c)
+        push(landb.at[sa], landb.at[sa], ssem.at[1, sa], rsem.at[1, sa], me.at(me.a, 1 - me.b, me.c)).wait_recv()
+        parts = [mine.at[idx], landb.at[sa]]
+
+        def landed(slot):
+            push(landa.at[slot], landa.at[slot], ssem.at[2, 0], rsem.at[2, slot], me.at(me.a, me.b, me.c)).wait_recv()
+
+        if i < planes - 1:
+            up = sa > me.a
+            inner = (up & (me.a > 0)) | (jnp.logical_not(up) & (me.a + 1 < planes))
+
+            @pl.when(inner)
+            def _():
+                landed(sa)
+                add_rows(mine.at[idx], parts + [landa.at[sa]])
+
+            @pl.when(jnp.logical_not(inner))
+            def _():
+                add_rows(mine.at[idx], parts)
+
+            @pl.when(up)
+            def _():
+                send_a(sa, True).start()
+
+            @pl.when(jnp.logical_not(up))
+            def _():
+                send_a(sa, False).start()
+
+        else:
+            target = home_ref.at[me.t]
+
+            @pl.when(me.a > 0)
+            def _():
+                landed(me.a)
+
+            @pl.when(me.a + 1 < planes)
+            def _():
+                landed(planes)
+
+            @pl.when((me.a > 0) & (me.a + 1 < planes))
+            def _():
+                add_rows(target, parts + [landa.at[me.a], landa.at[planes]])
+
+            @pl.when(me.a == 0)
+            def _():
+                add_rows(target, parts + [landa.at[planes]])
+
+            @pl.when(me.a + 1 == planes)
+            def _():
+                add_rows(target, parts + [landa.at[me.a]])
+
+
+    def load_rows(sa, q):
+        return pltpu.make_async_copy(all_ref.at[sa * 4 + q], pbuf.at[q], lsem.at[q])
+
+    def load_up(sa):
+        group = pl.ds(sa * 4, 4)
+        return [
+            pltpu.make_async_copy(up_ref.at[group], ubuf.at[:, ours], lsem.at[4]),
+            pltpu.make_async_copy(other_ref.at[group], ubuf.at[:, theirs], lsem.at[5]),
+        ]
+
+    def fetch_up(sa):
+        there = other_ref.at[pl.ds(sa * 4, 4)]
+        push(there, there, usend.at[sa], urecv.at[sa], me.core()).wait_recv()
+        for k in load_up(sa):
+            k.start()
+
+    def lanes(rows):
+        return lax.broadcasted_iota(jnp.int32, (rows, notes_width), 1)
+
+    def pick_rows(q, sa):
+        load_rows(sa, q).wait()
+        notes = pbuf[q, :, width:].astype(f32)
+        slot_of = jnp.sum(jnp.where(lanes(tokens) == me.e, notes, 0.0), axis=1, keepdims=True)
+        chosen = slot_of == lax.broadcasted_iota(jnp.int32, (tokens, slots), 1).astype(f32)
+        chosen = jnp.where(chosen, 1.0, 0.0).astype(bf16)
+        sbuf[q] = chosen
+        at = pl.ds(pl.multiple_of(q * slots, slots), slots)
+        there = over(chosen, pbuf[q, :, width:], TN)
+        mark = lanes(slots)
+        gate = jnp.sum(jnp.where((mark == count + me.e) | (mark == 2 * count + me.e), there, 0.0), axis=1, keepdims=True)
+        gates[at, :] = jnp.broadcast_to(gate, (slots, 128))
+        for n in range(0, width, 512):
+            cut = slice(n, n + 512)
+            xbuf[at, cut] = over(chosen, pbuf[q, :, cut], TN).astype(bf16)
+            picked = over(chosen, ubuf[q, :, cut], TN)
+            gbuf[at, cut] = (picked * gate).astype(bf16)
+        for n in range(0, side, 512):
+            cut = pl.ds(pl.multiple_of(me.t * side + n, 512), 512)
+            vbuf[at, n : n + 512] = over(chosen, ubuf[q, :, cut], TN).astype(bf16)
+        return sa
+
+    def hidden_cols(p):
+        return pl.ds(pl.multiple_of(p * hidden, 128), hidden)
+
+    def both_cols(p):
+        return pl.ds(pl.multiple_of(p * 2 * hidden, 128), 2 * hidden)
+
+    def hidden_rows(r, slot):
+        at = pl.ds(pl.multiple_of(r * 256, 256), 256)
+        acts = over(xbuf[at, :], wide[...], NN)
+        gate_act, up_act = acts[:, :hidden], acts[:, hidden:]
+        sig = 1.0 / (1.0 + jnp.exp(-gate_act))
+        silu = gate_act * sig
+        hbuf[slot, at, hidden_cols(me.t)] = (silu * up_act).astype(bf16)
+        back = over(gbuf[at, :], down[...], NT)
+        gate_d = (back * up_act * (sig * (1.0 + gate_act * (1.0 - sig)))).astype(bf16)
+        dbuf[slot, at, pl.ds(pl.multiple_of(me.t * 2 * hidden, 128), hidden)] = gate_d
+        dbuf[slot, at, pl.ds(pl.multiple_of(me.t * 2 * hidden + hidden, 128), hidden)] = (back * silu).astype(bf16)
+        return slot
+
+    def trades(slot):
+        h_part = hbuf.at[slot, :, hidden_cols(me.t)]
+        d_part = dbuf.at[slot, :, both_cols(me.t)]
+        return [
+            push(h_part, h_part, hsend.at[0], hrecv.at[slot, 0], me.core()),
+            push(d_part, d_part, hsend.at[1], hrecv.at[slot, 1], me.core()),
+        ]
+
+    def traded(slot):
+        h_part = hbuf.at[slot, :, hidden_cols(1 - me.t)]
+        d_part = dbuf.at[slot, :, both_cols(1 - me.t)]
+        push(h_part, h_part, hsend.at[0], hrecv.at[slot, 0], me.core()).wait_recv()
+        push(d_part, d_part, hsend.at[1], hrecv.at[slot, 1], me.core()).wait_recv()
+
+    def weight_sums(n, slot):
+        cut = pl.ds(pl.multiple_of(n * 512, 512), 512)
+        own_d = dbuf[slot, :, both_cols(me.t)]
+        gate_sum[cut, :] += over(xbuf[:, cut], own_d[:, :hidden], TN)
+        lift_sum[cut, :] += over(xbuf[:, cut], own_d[:, hidden:], TN)
+        down_sum[:, cut] += over(hbuf[slot, :, hidden_cols(me.t)], gbuf[:, cut], TN)
+        return slot
+
+    def out_rows(n, slot):
+        cut = pl.ds(pl.multiple_of(n * 512, 512), 512)
+        for r in range(0, 4 * slots, 256):
+            at = slice(r, r + 256)
+            out = over(hbuf[slot, at, :], down_half[:, cut], NN)
+            wbuf[at, cut] = (out * gates[at, :1]).astype(bf16)
+            total = jnp.sum(out * vbuf[at, cut].astype(f32), axis=1, keepdims=True)
+            scores[at, :] += jnp.broadcast_to(total, (256, 128))
+            rbuf[at, cut] = over(dbuf[slot, at, :], wide_half[cut, :], NT).astype(bf16)
+        return slot
+
+    def note_scores():
+        mark = lanes(4 * slots)
+        total = scores[...]
+        high = total.astype(bf16).astype(f32)
+        row = jnp.where(mark == me.e, high, jnp.where(mark == me.e + count, total - high, 0.0))
+        rbuf[:, side:] = row.astype(bf16)
+
+    def store(idx, q):
+        return pltpu.make_async_copy(stage.at[lax.rem(q, 2)], share_ref.at[idx], osem.at[lax.rem(q, 2)])
+
+    def spread_rows(q, sa):
+        at = pl.ds(pl.multiple_of(q * slots, slots), slots)
+        idx = sa * 4 + q
+
+        @pl.when(q >= 2)
+        def _():
+            store(idx, q).wait()
+
+        for n in range(0, side, 512):
+            cut = slice(n, n + 512)
+            mine[idx, :, cut] = over(sbuf[q], rbuf[at, cut], NN).astype(bf16)
+            stage[lax.rem(q, 2), :, cut] = over(sbuf[q], wbuf[at, cut], NN).astype(bf16)
+        mine[idx, :, side:] = over(sbuf[q], rbuf[at, side:], NN).astype(bf16)
+        store(idx, q).start()
+        return sa
+
+    local = pltpu.make_async_copy(parcel_ref, all_ref.at[own], lsem.at[6])
+    local.start()
+    me.greet(planes, True, True, True)
+    relay(me.a, True, True)
+    for i in list(range(1, planes)) + [0]:
+        upstream(near(i)).start()
+    for k in loads + pushes:
+        k.start()
+    relay(near(1), True, False)
+    gate_sum[...] = jnp.zeros_like(gate_sum)
+    lift_sum[...] = jnp.zeros_like(lift_sum)
+    down_sum[...] = jnp.zeros_like(down_sum)
+    across(me.a, True)
+    fetch_up(near(1))
+    for k in loads + pushes:
+        k.wait()
+    local.wait()
+
+    def step(i, c):
+        last = i == planes - 1
+        sa = jnp.where(last, me.a, near(i + 1))
+        slot = lax.rem(i, 2)
+
+        @pl.when(i + 2 < planes)
+        def _():
+            relay(near(i + 2), True, False)
+
+        @pl.when(jnp.logical_not(last))
+        def _():
+            across(sa, True)
+
+        from_core(sa)
+        for q in range(4):
+            load_rows(sa, q).start()
+        for k in load_up(sa):
+            k.wait()
+        scores[...] = jnp.zeros_like(scores)
+        lax.fori_loop(0, 4, pick_rows, sa)
+
+        @pl.when(jnp.logical_not(last))
+        def _():
+            fetch_up(jnp.where(i + 1 == planes - 1, me.a, near(i + 2)))
+
+        @pl.when(i > 0)
+        def _():
+            for k in trades(slot):
+                k.wait_send()
+
+        lax.fori_loop(0, 4 * slots // 256, hidden_rows, slot)
+        for k in trades(slot):
+            k.start()
+        lax.fori_loop(0, width // 512, weight_sums, slot)
+        traded(slot)
+        lax.fori_loop(0, side // 512, out_rows, slot)
+        note_scores()
+        lax.fori_loop(0, 4, spread_rows, sa)
+        for sb in (1 - me.b, me.b):
+            send_c(sa, sb).start()
+        store(0, 0).wait()
+        store(0, 1).wait()
+
+        @pl.when(i > 0)
+        def _():
+            from_c(near(i))
+
+        return c
+
+    lax.fori_loop(0, planes, step, 0)
+    for i in range(planes - 1):
+        along(i, far_first(me.a, planes, i))
+    from_c(me.a)
+    along(planes - 1, me.a)
+    done = push(home_ref.at[me.t], home_ref.at[me.t], esem.at[0], esem.at[1], me.core())
+    done.start()
+
+    relay(me.a, False, True)
+
+    def settle(i, c):
+        sa = near(i)
+
+        @pl.when(i > 0)
+        def _():
+            relay(sa, False, False)
+            send_a(sa, False).wait_send()
+
+        across(sa, False)
+        for sb in (1 - me.b, me.b):
+            send_c(sa, sb).wait_send()
+        send_b(sa).wait_send()
+        upstream(sa).wait_send()
+        return c
+
+    lax.fori_loop(0, planes, settle, 0)
+    for k in trades(0):
+        k.wait_send()
+    done.wait_send()
+    other = home_ref.at[1 - me.t]
+    push(other, other, esem.at[0], esem.at[1], me.core()).wait_recv()
+
+
+def run_experts(parcel, upstream, gate, lift_w, down, planes, slots, cid):
+    f32, bf16 = jnp.float32, jnp.bfloat16
+    tokens, packed = parcel.shape
+    hidden, width = down.shape
+    count = planes * 4
+    half = tokens // 2
+    side = width // 2
+    block = side + packed - width
+    rows = 4 * slots
+    anywhere = pl.BlockSpec(memory_space=pl.ANY)
+    inside = pl.BlockSpec(memory_space=pltpu.VMEM)
+    return pl.pallas_call(
+        functools.partial(experts_kernel, planes),
+        out_shape=[
+            jax.ShapeDtypeStruct((count, tokens, packed), bf16),
+            jax.ShapeDtypeStruct((count, half, width), bf16),
+            jax.ShapeDtypeStruct((count, tokens, side), bf16),
+            jax.ShapeDtypeStruct((2, tokens, block), bf16),
+            jax.ShapeDtypeStruct((width, hidden), f32),
+            jax.ShapeDtypeStruct((width, hidden), f32),
+            jax.ShapeDtypeStruct((hidden, width), f32),
+        ],
+        in_specs=[anywhere] * 5,
+        out_specs=[anywhere] * 3 + [inside] * 4,
+        scratch_shapes=[
+            pltpu.VMEM((width, 2 * hidden), bf16),
+            pltpu.VMEM((hidden, width), bf16),
+            pltpu.VMEM((side, 4 * hidden), bf16),
+            pltpu.VMEM((2 * hidden, side), bf16),
+            pltpu.VMEM((4, tokens, packed), bf16),
+            pltpu.VMEM((4, tokens, width), bf16),
+            pltpu.VMEM((rows, width), bf16),
+            pltpu.VMEM((rows, width), bf16),
+            pltpu.VMEM((rows, side), bf16),
+            pltpu.VMEM((4, tokens, slots), bf16),
+            pltpu.VMEM((rows, side), bf16),
+            pltpu.VMEM((rows, block), bf16),
+            pltpu.VMEM((2, rows, 2 * hidden), bf16),
+            pltpu.VMEM((2, rows, 4 * hidden), bf16),
+            pltpu.VMEM((rows, 128), f32),
+            pltpu.VMEM((rows, 128), f32),
+            pltpu.VMEM((2, tokens, side), bf16),
+            pltpu.VMEM((count, tokens, block), bf16),
+            pltpu.VMEM((2 * planes, tokens, block), bf16),
+            pltpu.VMEM((planes, tokens, block), bf16),
+            pltpu.VMEM((planes + 1, tokens, block), bf16),
+            pltpu.SemaphoreType.DMA((count, 5)),
+            pltpu.SemaphoreType.DMA((count,)),
+            pltpu.SemaphoreType.DMA((count,)),
+            pltpu.SemaphoreType.DMA((planes,)),
+            pltpu.SemaphoreType.DMA((planes,)),
+            pltpu.SemaphoreType.DMA((3,)),
+            pltpu.SemaphoreType.DMA((3,)),
+            pltpu.SemaphoreType.DMA((6,)),
+            pltpu.SemaphoreType.DMA((2,)),
+            pltpu.SemaphoreType.DMA((2, 2)),
+            pltpu.SemaphoreType.DMA((3, 2 * planes)),
+            pltpu.SemaphoreType.DMA((3, 2 * planes)),
+            pltpu.SemaphoreType.DMA((7,)),
+            pltpu.SemaphoreType.DMA((2,)),
+            pltpu.SemaphoreType.DMA((2,)),
+        ],
+        compiler_params=pltpu.CompilerParams(
+            collective_id=cid, has_side_effects=True, vmem_limit_bytes=62 * 2**20
+        ),
+        name="experts",
+    )(parcel, upstream, gate, lift_w, down)
+
+
+def stack_heads(target, source, group):
+    items, rows, size = target.shape
+    seg = rows // group
+    keys = source.shape[1] // (group * size)
+    for s in range(items // keys):
+        for k in range(keys):
+            for h in range(group):
+                at = (k * group + h) * size
+                part = source[s * seg : (s + 1) * seg, at : at + size]
+                target[s * keys + k, h * seg : (h + 1) * seg, :] = part.astype(target.dtype)
+
+
+def spread_heads(target, item, value, group, keys):
+    rows, size = value.shape
+    seg = rows // group
+    s, k = item // keys, item % keys
+    for h in range(group):
+        at = (k * group + h) * size
+        target[s * seg : (s + 1) * seg, at : at + size] = value[h * seg : (h + 1) * seg, :].astype(target.dtype)
+
+
+def block_heads(ref, plane, item, keys, size, part):
+    seg = BLOCK // 4
+    s, k = lax.div(item, keys), lax.rem(item, keys)
+    rows = pl.ds(pl.multiple_of(s * seg, seg), seg)
+    cols = pl.ds(pl.multiple_of((part * keys + k) * size, size), size)
+    return [ref.at[plane * 4 + q, rows, cols] for q in range(4)]
+
+
+def joined(refs):
+    return jnp.concatenate([ref[...] for ref in refs], axis=0)
+
+
+def attend_kernel(
+    planes, group, q_ref, x_ref, context_ref, all_ref, log_ref, qs, top, total, acc, ssem, rsem, lsem
+):
+    me = Spot()
+    f32, bf16 = jnp.float32, jnp.bfloat16
+    items, rows, size = qs.shape
+    keys = x_ref.shape[1] // (2 * size)
+    factor = size ** (-0.5)
+    own = me.index(me.a, me.b, me.c)
+
+    def carry(idx, kind, src=None):
+        who = {
+            0: me.at(me.a + 1, me.b, me.c),
+            2: me.at(me.a, 1 - me.b, me.c),
+            3: me.at(me.a, me.b, 1 - me.c),
+        }[kind]
+        there = all_ref.at[idx]
+        return push(there if src is None else src, there, ssem.at[idx, kind], rsem.at[idx], who)
+
+    def relay(sa, act, first):
+        idx = me.index(sa, me.b, me.c)
+        src = x_ref if first else None
+        if act and not first:
+            carry(idx, 2).wait_recv()
+        run = (lambda c: c.start()) if act else (lambda c: c.wait_send())
+
+        @pl.when(me.a + 1 < planes)
+        def _():
+            run(carry(idx, 0, src))
+
+        run(carry(idx, 3, src))
+        run(carry(idx, 2, src))
+        idx = me.index(sa, 1 - me.b, me.c)
+        if act:
+            carry(idx, 2).wait_recv()
+        run(carry(idx, 3))
+
+    def block(item, sa):
+        scores = over(qs[item], joined(block_heads(all_ref, sa, item, keys, size, 0)), NT) * factor
+        values = joined(block_heads(all_ref, sa, item, keys, size, 1))
+        before = top[item]
+        high = jnp.maximum(before, jnp.broadcast_to(jnp.max(scores, axis=1, keepdims=True), before.shape))
+        shrink = jnp.exp(before - high)
+        terms = jnp.exp(scores - high[:, :1])
+        top[item] = high
+        total[item] = total[item] * shrink + jnp.broadcast_to(jnp.sum(terms, axis=1, keepdims=True), before.shape)
+        acc[item] = acc[item] * shrink + over(terms.astype(bf16), values, NN)
+        return sa
+
+    local = pltpu.make_async_copy(x_ref, all_ref.at[own], lsem)
+    local.start()
+    me.greet(planes, True, True, False)
+    relay(me.a, True, True)
+    stack_heads(qs, q_ref, group)
+    top[...] = jnp.full(top.shape, far_below, f32)
+    total[...] = jnp.zeros_like(total)
+    acc[...] = jnp.zeros_like(acc)
+    local.wait()
+
+    def step(i, c):
+        sa = me.a - i
+
+        @pl.when(sa > 0)
+        def _():
+            relay(sa - 1, True, False)
+
+        for sb in (me.b, 1 - me.b):
+            carry(me.index(sa, sb, 1 - me.c), 2).wait_recv()
+        lax.fori_loop(0, items, block, sa)
+        return c
+
+    lax.fori_loop(0, me.a + 1, step, 0)
+    for item in range(items):
+        spread_heads(context_ref, item, acc[item] / total[item], group, keys)
+    log_ref[...] = top[...] + jnp.log(total[...])
+    relay(me.a, False, True)
+
+    def settle(i, c):
+        relay(me.a - i, False, False)
+        return c
+
+    lax.fori_loop(1, me.a + 1, settle, 0)
+
+
+def attend(query, pairs, planes, group, size, cid):
+    f32, bf16 = jnp.float32, jnp.bfloat16
+    tokens, width = query.shape
+    count = planes * 4
+    items = (tokens * 4 // BLOCK) * (width // (group * size))
+    state = (items, group * BLOCK // 4, size)
+    inside = pl.BlockSpec(memory_space=pltpu.VMEM)
+    return pl.pallas_call(
+        functools.partial(attend_kernel, planes, group),
+        out_shape=[
+            jax.ShapeDtypeStruct((tokens, width), bf16),
+            jax.ShapeDtypeStruct((count,) + pairs.shape, bf16),
+            jax.ShapeDtypeStruct(state, f32),
+        ],
+        in_specs=[inside] * 2,
+        out_specs=[inside] * 3,
+        scratch_shapes=[
+            pltpu.VMEM(state, bf16),
+            pltpu.VMEM(state, f32),
+            pltpu.VMEM(state, f32),
+            pltpu.VMEM(state, f32),
+            pltpu.SemaphoreType.DMA((count, 4)),
+            pltpu.SemaphoreType.DMA((count,)),
+            pltpu.SemaphoreType.DMA,
+        ],
+        compiler_params=pltpu.CompilerParams(collective_id=cid, has_side_effects=True, vmem_limit_bytes=ROOM),
+        name="attend",
+    )(query, pairs)
+
+
+def attend_back_kernel(
+    planes,
+    group,
+    q_ref,
+    g_ref,
+    o_ref,
+    all_ref,
+    log_ref,
+    cut_ref,
+    query_grad,
+    pair_grad,
+    plane_o,
+    plane_cut,
+    qs,
+    gs,
+    delta,
+    qacc,
+    mine,
+    landc,
+    landb,
+    landa,
+    ssem,
+    rsem,
+    psend,
+    precv,
+    lsem,
+):
+    me = Spot()
+    f32, bf16 = jnp.float32, jnp.bfloat16
+    items, rows, size = qs.shape
+    keys = all_ref.shape[2] // (2 * size)
+    factor = size ** (-0.5)
+    place = lax.rem(me.e, 4)
+    base = me.e - place
+
+    def spot(b, c):
+        return me.index(0, b, c)
+
+    near = [(1 - me.b, me.c), (me.b, 1 - me.c), (1 - me.b, 1 - me.c)]
+    keep = [
+        pltpu.make_async_copy(o_ref, plane_o.at[place], lsem.at[0]),
+        pltpu.make_async_copy(cut_ref.at[place], plane_cut.at[place], lsem.at[1]),
+    ]
+    for k in keep:
+        k.start()
+    barrier = pltpu.get_barrier_semaphore()
+    for b, c in near:
+        pl.semaphore_signal(barrier, inc=1, device_id=(base + spot(b, c), me.t), device_id_type=MESH)
+    up, down = me.a + 1 < planes, me.a > 0
+
+    @pl.when(up)
+    def _():
+        pl.semaphore_signal(barrier, inc=1, device_id=me.at(me.a + 1, me.b, me.c), device_id_type=MESH)
+
+    @pl.when(down)
+    def _():
+        pl.semaphore_signal(barrier, inc=1, device_id=me.at(me.a - 1, me.b, me.c), device_id_type=MESH)
+
+    pl.semaphore_wait(barrier, 3 + up.astype(jnp.int32) + down.astype(jnp.int32))
+    parts = [
+        push(cut_ref.at[spot(*near[i])], plane_cut.at[place], psend.at[3 + i], precv.at[3 + i], (base + spot(*near[i]), me.t))
+        for i in range(3)
+    ]
+    whole = [push(o_ref, plane_o.at[place], psend.at[i], precv.at[i], (base + spot(*near[i]), me.t)) for i in range(2)]
+    for k in parts + whole:
+        k.start()
+
+    stack_heads(qs, q_ref, group)
+    stack_heads(gs, g_ref, group)
+    stack_heads(qacc, o_ref, group)
+
+    def prepare(item, c):
+        part = jnp.sum(gs[item].astype(f32) * qacc[item], axis=1, keepdims=True)
+        delta[item] = jnp.broadcast_to(part, delta.shape[1:])
+        qacc[item] = jnp.zeros(qacc.shape[1:], f32)
+        return c
+
+    lax.fori_loop(0, items, prepare, 0)
+
+    def block(item, sa):
+        keys_here = joined(block_heads(all_ref, sa, item, keys, size, 0))
+        values = joined(block_heads(all_ref, sa, item, keys, size, 1))
+        queries, grads = qs[item], gs[item]
+        scores = over(queries, keys_here, NT) * factor
+        probs = jnp.exp(scores - log_ref[item][:, :1])
+        prob_grads = over(grads, values, NT)
+        score_grads = (probs * (prob_grads - delta[item][:, :1])).astype(bf16)
+        qacc[item] += over(score_grads, keys_here, NN)
+        key_part = (over(score_grads, queries, TN) * factor).astype(bf16)
+        value_part = over(probs.astype(bf16), grads, TN).astype(bf16)
+        seg = key_part.shape[0] // 4
+        for part, value in ((0, key_part), (1, value_part)):
+            for q, ref in enumerate(block_heads(mine, sa, item, keys, size, part)):
+                ref[...] = value[q * seg : (q + 1) * seg, :]
+        return sa
+
+    def send_c(sa, sb):
+        slot = sa * 2 + sb
+        src = mine.at[me.index(sa, sb, 1 - me.c)]
+        return push(src, landc.at[slot], ssem.at[0, slot], rsem.at[0, slot], me.at(me.a, me.b, 1 - me.c))
+
+    def send_b(sa):
+        src = mine.at[me.index(sa, 1 - me.b, me.c)]
+        return push(src, landb.at[sa], ssem.at[1, sa], rsem.at[1, sa], me.at(me.a, 1 - me.b, me.c))
+
+    def send_a(sa):
+        src = mine.at[me.index(sa, me.b, me.c)]
+        return push(src, landa.at[sa], ssem.at[2, sa], rsem.at[2, sa], me.at(me.a - 1, me.b, me.c))
+
+    def from_c(sa):
+        for sb in (1 - me.b, me.b):
+            slot = sa * 2 + sb
+            push(landc.at[slot], landc.at[slot], ssem.at[0, slot], rsem.at[0, slot], me.at(me.a, me.b, 1 - me.c)).wait_recv()
+            idx = me.index(sa, sb, me.c)
+            add_rows(mine.at[idx], [mine.at[idx], landc.at[slot]])
+            if sb is not me.b:
+                send_b(sa).start()
+
+    def along(sa):
+        idx = me.index(sa, me.b, me.c)
+        push(landb.at[sa], landb.at[sa], ssem.at[1, sa], rsem.at[1, sa], me.at(me.a, 1 - me.b, me.c)).wait_recv()
+
+        def finish(target):
+            @pl.when(me.a + 1 < planes)
+            def _():
+                push(landa.at[sa], landa.at[sa], ssem.at[2, sa], rsem.at[2, sa], me.at(me.a, me.b, me.c)).wait_recv()
+                add_rows(target, [mine.at[idx], landb.at[sa], landa.at[sa]])
+
+            @pl.when(me.a + 1 == planes)
+            def _():
+                add_rows(target, [mine.at[idx], landb.at[sa]])
+
+        @pl.when(sa < me.a)
+        def _():
+            finish(mine.at[idx])
+            send_a(sa).start()
+
+        @pl.when(sa == me.a)
+        def _():
+            finish(pair_grad)
+
+    source = spot(*near[0])
+    relay = push(plane_o.at[source], plane_o.at[source], psend.at[2], precv.at[2], (base + spot(*near[1]), me.t))
+
+    def step(sa, c):
+        lax.fori_loop(0, items, block, sa)
+        for sb in (1 - me.b, me.b):
+            send_c(sa, sb).start()
+
+        @pl.when(sa == 0)
+        def _():
+            whole[0].wait_recv()
+            relay.start()
+
+        @pl.when(sa >= 1)
+        def _():
+            from_c(sa - 1)
+
+        @pl.when(sa >= 2)
+        def _():
+            along(sa - 2)
+
+        return c
+
+    lax.fori_loop(0, me.a + 1, step, 0)
+    for item in range(items):
+        spread_heads(query_grad, item, qacc[item] * factor, group, keys)
+    from_c(me.a)
+
+    @pl.when(me.a > 0)
+    def _():
+        along(me.a - 1)
+
+    along(me.a)
+
+    def settle(sa, c):
+        for sb in (1 - me.b, me.b):
+            send_c(sa, sb).wait_send()
+        send_b(sa).wait_send()
+
+        @pl.when(sa < me.a)
+        def _():
+            send_a(sa).wait_send()
+
+        return c
+
+    lax.fori_loop(0, me.a + 1, settle, 0)
+    whole[0].wait_send()
+    whole[1].wait()
+    for k in parts:
+        k.wait()
+    relay.wait()
+    for k in keep:
+        k.wait()
+
+
+def attend_back(query, grads, context, pairs_all, logs, cut, planes, group, size, cid):
+    f32, bf16 = jnp.float32, jnp.bfloat16
+    tokens, width = query.shape
+    items = logs.shape[0]
+    state = logs.shape
+    block = pairs_all.shape[1:]
+    inside = pl.BlockSpec(memory_space=pltpu.VMEM)
+    anywhere = pl.BlockSpec(memory_space=pl.ANY)
+    return pl.pallas_call(
+        functools.partial(attend_back_kernel, planes, group),
+        out_shape=[
+            jax.ShapeDtypeStruct((tokens, width), f32),
+            jax.ShapeDtypeStruct(block, f32),
+            jax.ShapeDtypeStruct((4,) + context.shape, bf16),
+            jax.ShapeDtypeStruct(cut.shape, bf16),
+        ],
+        in_specs=[inside] * 5 + [anywhere],
+        out_specs=[inside, inside, anywhere, anywhere],
+        scratch_shapes=[
+            pltpu.VMEM(state, bf16),
+            pltpu.VMEM(state, bf16),
+            pltpu.VMEM(state, f32),
+            pltpu.VMEM(state, f32),
+            pltpu.VMEM((4 * planes,) + block, bf16),
+            pltpu.VMEM((2 * planes,) + block, bf16),
+            pltpu.VMEM((planes,) + block, bf16),
+            pltpu.VMEM((planes,) + block, bf16),
+            pltpu.SemaphoreType.DMA((3, 2 * planes)),
+            pltpu.SemaphoreType.DMA((3, 2 * planes)),
+            pltpu.SemaphoreType.DMA((6,)),
+            pltpu.SemaphoreType.DMA((6,)),
+            pltpu.SemaphoreType.DMA((2,)),
+        ],
+        compiler_params=pltpu.CompilerParams(collective_id=cid, has_side_effects=True, vmem_limit_bytes=ROOM),
+        name="attend_back",
+    )(query, grads, context, pairs_all, logs, cut)
 
 
 epsilon = 1e-06
@@ -398,10 +1824,199 @@
         down_grad[None],
     )
 
+def lift(values, wide):
+    high = lax.reduce_precision(values, 8, 7)
+    both = jnp.concatenate([high, values - high], axis=-1).astype(jnp.bfloat16)
+    return jnp.pad(both, ((0, 0), (0, wide - both.shape[-1])))
+
+
+def on_chips(
+    layer_input,
+    norm_first,
+    query_weight,
+    key_weight,
+    value_weight,
+    mixing_weight,
+    query_gain,
+    key_gain,
+    norm_second,
+    router_weight,
+    gate_weight,
+    up_weight,
+    down_weight,
+    routes,
+    fill_order,
+    cotangent,
+):
+    seq_count, seg_len, model_width = layer_input.shape
+    expert_count = lax.axis_size("expert")
+    planes = expert_count // 4
+    expert_idx = lax.axis_index("expert")
+    tensor_idx = lax.axis_index("tensor")
+    head_dim = query_gain.shape[0]
+    local_queries = query_weight.shape[1] // head_dim
+    local_keys = key_weight.shape[1] // head_dim
+    key_width = local_keys * head_dim
+    group_size = local_queries // local_keys
+    top_count = routes.shape[2]
+    token_count = seq_count * seg_len
+    capacity = 5 * token_count * top_count // (4 * expert_count)
+    slots = -(-capacity // 32) * 32
+    half_width = model_width // 2
+    share_width = model_width // expert_count
+    f32, bf16 = jnp.float32, jnp.bfloat16
+    inputs = layer_input.astype(f32)
+    normed_f, first_back = jax.vjp(rms_scaled, inputs, norm_first)
+    normed = normed_f.astype(bf16)
+    positions = expert_idx * seg_len + jnp.arange(seg_len, dtype=jnp.int32)
+    cosine, sine_table = rotary_tables(positions, head_dim)
+    cosine = cosine[:, None, :]
+    sine_table = sine_table[:, None, :]
+
+    def rope_norm(raw_heads, gain_vec):
+        return rotate(rms_scaled(raw_heads, gain_vec), cosine, sine_table)
+
+    query_raw = jnp.dot(normed, query_weight, preferred_element_type=f32).reshape(
+        seq_count, seg_len, local_queries, head_dim
+    )
+    key_raw = jnp.dot(normed, key_weight, preferred_element_type=f32).reshape(
+        seq_count, seg_len, local_keys, head_dim
+    )
+    value_local = jnp.dot(normed, value_weight, preferred_element_type=f32).astype(bf16)
+    query_rot, query_back = jax.vjp(rope_norm, query_raw, query_gain)
+    key_rot, key_back = jax.vjp(rope_norm, key_raw, key_gain)
+    key_local = key_rot.astype(bf16).reshape(token_count, key_width)
+    pairs = jnp.concatenate([key_local, value_local.reshape(token_count, key_width)], axis=1)
+    upstream_low = cotangent.reshape(token_count, model_width)
+    half_tokens = token_count // 2
+    upstream_half = lax.dynamic_slice_in_dim(upstream_low, tensor_idx * half_tokens, half_tokens, 0)
+    upstream_mine = lax.all_gather(upstream_half, "expert")
+    query_rows = query_rot.astype(bf16).reshape(token_count, local_queries * head_dim)
+    context, pairs_all, logs = attend(query_rows, pairs, planes, group_size, head_dim, 1)
+    head_part = jnp.dot(context, mixing_weight, preferred_element_type=f32)
+    head_low = head_part.astype(bf16)
+    head_other = swap_cores(head_low, 3, "swap_heads")
+    residual = inputs.reshape(token_count, model_width) + (head_low.astype(f32) + head_other.astype(f32))
+    second_f, second_back = jax.vjp(rms_scaled, residual, norm_second)
+    second = second_f.astype(bf16)
+    logits = jnp.dot(second, router_weight, preferred_element_type=f32)
+    flat_routes = routes.reshape(token_count, top_count)
+    picked = (flat_routes[:, :, None] == jnp.arange(expert_count, dtype=jnp.int32)).astype(f32)
+    gates = jax.nn.softmax(jnp.sum(picked * logits[:, None, :], axis=-1), axis=-1)
+    usages = jnp.sum(picked, axis=1)
+    ranking = fill_order.reshape(token_count)
+    before = (ranking[None, :] < ranking[:, None]).astype(bf16)
+    counts = jnp.dot(before, usages.astype(bf16), preferred_element_type=f32)
+    here = (usages > 0.0) & (counts < capacity)
+    slot_table = jnp.where(here, counts, -1.0)
+    gate_table = jnp.where(here, jnp.sum(picked * gates[:, :, None], axis=1), 0.0)
+    slot_hi = lift(slot_table, 2 * expert_count)[:, :expert_count]
+    notes = jnp.concatenate([slot_hi, lift(gate_table, 128 - expert_count)], axis=1)
+    parcel = jnp.concatenate([second, notes], axis=1)
+    _, _, out_share, row_home, gate_grad, up_grad, down_grad = run_experts(
+        parcel, upstream_mine, gate_weight[0], up_weight[0], down_weight[0], planes, slots, 4
+    )
+    out_home = lax.psum_scatter(out_share, "expert", scatter_dimension=0, tiled=True)[0]
+    residual_half = lax.dynamic_slice_in_dim(residual, tensor_idx * half_width, half_width, 1)
+    layer_output = (residual_half + out_home.astype(f32)).astype(bf16).reshape(seq_count, seg_len, half_width)
+    home_scores = jnp.sum(row_home[:, :, half_width:].astype(f32), axis=0)
+    home_scores = home_scores[:, :expert_count] + home_scores[:, expert_count : 2 * expert_count]
+    gate_grads = jnp.sum(picked * home_scores[:, None, :], axis=-1)
+    route_grads = gates * (gate_grads - jnp.sum(gates * gate_grads, axis=-1, keepdims=True))
+    logit_grads = jnp.sum(picked * route_grads[:, :, None], axis=1).astype(bf16)
+    router_grad = jnp.einsum("td,te->ed", second, logit_grads, preferred_element_type=f32)
+    router_back = lax.dot_general(
+        logit_grads, router_weight, (((1,), (1,)), ((), ())), preferred_element_type=f32
+    )
+    second_rows = jnp.concatenate([row_home[0, :, :half_width], row_home[1, :, :half_width]], axis=1)
+    second_in = second_rows.astype(f32) + router_back
+    residual_part, second_grad = second_back(second_in)
+    residual_grad = residual_part + upstream_low.astype(f32)
+    head_in = residual_grad.astype(bf16)
+
+    def slices(rows):
+        cut = rows.reshape(token_count, planes, 4, share_width)
+        return cut.transpose(2, 0, 1, 3).reshape(4, token_count, planes * share_width)
+
+    context_grad = lax.dot_general(
+        head_in, mixing_weight, (((1,), (1,)), ((), ())), preferred_element_type=f32
+    ).astype(bf16)
+    query_rot_grad, pair_home, context_plane, head_plane = attend_back(
+        query_rows, context_grad, context, pairs_all, logs, slices(head_in), planes, group_size, head_dim, 7
+    )
+    mixing_part = jnp.einsum("gtd,gtc->dc", head_plane, context_plane, preferred_element_type=f32)
+    mixing_part = mixing_part.astype(bf16).reshape(planes, share_width, local_queries * head_dim)
+    mixing_rows = scatter_sum(mixing_part, planes, False, False, f32, 8, "scatter_mixing")
+    mixing_grad = mixing_rows.T
+    key_raw_grad, keygain_part = key_back(
+        pair_home[:, :key_width].reshape(seq_count, seg_len, local_keys, head_dim)
+    )
+    query_raw_grad, querygain_part = query_back(
+        query_rot_grad.reshape(seq_count, seg_len, local_queries, head_dim)
+    )
+    query_low = query_raw_grad.astype(bf16).reshape(token_count, local_queries * head_dim)
+    key_low = key_raw_grad.astype(bf16).reshape(token_count, key_width)
+    value_low = pair_home[:, key_width:].astype(bf16)
+    all_low = jnp.concatenate([query_low, key_low, value_low], axis=1)
+    flat_normed = normed.reshape(token_count, model_width)
+    low_plane, normed_plane = plane_exchange(all_low, slices(flat_normed), 10, "plane_queries")
+    weight_part = jnp.einsum("gtd,gtc->dc", normed_plane, low_plane, preferred_element_type=f32)
+    weight_part = weight_part.astype(bf16).reshape(planes, share_width, all_low.shape[1])
+    weight_rows = scatter_sum(weight_part, planes, False, False, f32, 11, "scatter_queries")
+    query_width = local_queries * head_dim
+    query_grad = weight_rows[:, :query_width]
+    key_grad = weight_rows[:, query_width : query_width + key_width]
+    value_grad = weight_rows[:, query_width + key_width :]
+    normed_part = lax.dot_general(
+        query_low, query_weight, (((1,), (1,)), ((), ())), preferred_element_type=f32
+    )
+    normed_part = normed_part + lax.dot_general(
+        key_low, key_weight, (((1,), (1,)), ((), ())), preferred_element_type=f32
+    )
+    normed_part = normed_part + lax.dot_general(
+        value_low, value_weight, (((1,), (1,)), ((), ())), preferred_element_type=f32
+    )
+    gain_row = jnp.pad(
+        jnp.concatenate([querygain_part, keygain_part])[None], ((0, 15), (0, model_width - 2 * head_dim))
+    )
+    normed_low = jnp.concatenate([normed_part, gain_row], axis=0).astype(bf16)
+    normed_sum = normed_low.astype(f32) + swap_cores(normed_low, 12, "swap_normed").astype(f32)
+    normed_grad = normed_sum[:token_count].reshape(seq_count, seg_len, model_width)
+    input_part, first_grad = first_back(normed_grad)
+    input_grad = residual_grad.reshape(seq_count, seg_len, model_width) + input_part
+    small = jnp.concatenate(
+        [
+            first_grad[None],
+            second_grad[None],
+            normed_sum[token_count : token_count + 1],
+            jnp.zeros((13, model_width), f32),
+            router_grad,
+        ],
+        axis=0,
+    )
+    small = total_over(small, expert_count, 13, "total_small")
+    return (
+        layer_output,
+        input_grad,
+        small[0],
+        query_grad,
+        key_grad,
+        value_grad,
+        mixing_grad,
+        small[2, :head_dim],
+        small[2, head_dim : 2 * head_dim],
+        small[1],
+        small[16:].T,
+        gate_grad[None],
+        up_grad[None],
+        down_grad[None],
+    )
+
 
 def solution(mesh):
+    chips = mesh.shape["expert"] == 16 and mesh.shape["tensor"] == 2
     return jax.shard_map(
-        on_device,
+        on_chips if chips else on_device,
         mesh=mesh,
         in_specs=(
             P(None, "expert", None),

time: 2160 us -> 662 us (0.31)
  waiting for transfers between devices: 1480 us -> 34.9 us
  Pallas kernels: 0 us -> 471 us
  blocking collectives: 292 us -> 0 us
  matrix products: 184 us -> 38.6 us
  starting transfers between devices: 45.4 us -> 0.08 us
  other arithmetic: 55.8 us -> 32.8 us
  local copies, waits for them, and re-layouts: 78.4 us -> 56.7 us
    reduce_scatter x5 -> x1, waiting for transfers between devices: 765 us -> 0.01 us  [on_chips(): lax.psum_scatter(out_share, 'expert', scatter_dimension=0, tiled=True)[0]]
    all_to_all x4 -> x0, waiting for transfers between devices: 518 us -> none  [the longest x1 157 us: on_device(): lax.all_to_all(summed.reshape(expert_count, capacity, model_width), 'expe...]
    pallas_call x0 -> x9, Pallas kernels: none -> 471 us  [the longest x1 185 us: run_experts(): pl.pallas_call(functools.partial(experts_kernel, planes), out_shape=[jax....]
    unnamed x1 -> x0, blocking collectives: 219 us -> none
    dot_general x35 -> x14, matrix products: 184 us -> 38.6 us  [the longest x1 7.52 us: on_chips(): lax.dot_general(head_in, mixing_weight, (((1,), (1,)), ((), ())), preferr...]
    psum x2 -> x0, blocking collectives: 73.3 us -> none  [the longest x1 70.8 us: on_device(): lax.psum((first_grad, second_grad, querygain_grad, keygain_grad, router_g...]
    psum x4 -> x0, waiting for transfers between devices: 62.7 us -> none  [the longest x1 24.8 us: on_device(): lax.psum(head_part.astype(jnp.bfloat16), 'tensor').astype(jnp.float32)]
    all_gather x2 -> x1, waiting for transfers between devices: 92.9 us -> 34.8 us  [on_chips(): upstream_mine = lax.all_gather(upstream_half, 'expert')]
  transfers between devices with their start and end apart: 16 -> 2, of which waited for: 15 -> 1; matrix products, arithmetic and copies ran while one was open for 8% -> 17% of each run, Pallas kernels for 0% -> 44%
where the time goes in v1:
time: 662 us; the launch traced here: 650 us
  Pallas kernels  471 us (71%)
  local copies, waits for them, and re-layouts  56.7 us (9%)
  matrix products  38.6 us (6%)
  waiting for transfers between devices  34.9 us (5%)
  other arithmetic  32.8 us (5%)
  between operations  15.5 us (2%)
    pallas_call x1, Pallas kernels, run_experts(): pl.pallas_call(functools.partial(experts_kernel, planes), out_shape=[jax....  185 us
    pallas_call x2, Pallas kernels, scatter_sum(): pl.pallas_call(functools.partial(scatter_kernel, planes, flat, share), ou...  92.2 us
    pallas_call x1, Pallas kernels, attend_back(): pl.pallas_call(functools.partial(attend_back_kernel, planes, group), out_...  87.1 us
    pallas_call x1, Pallas kernels, plane_exchange(): pl.pallas_call(plane_kernel, out_shape=[jax.ShapeDtypeStruct((4,) + g.sha...  42.9 us
    all_gather x1, waiting for transfers between devices, on_chips(): upstream_mine = lax.all_gather(upstream_half, 'expert')  34.8 us
    pallas_call x1, Pallas kernels, attend(): pl.pallas_call(functools.partial(attend_kernel, planes, group), out_shape...  33.3 us
    unnamed x133, local copies, waits for them, and re-layouts  24.6 us
    pallas_call x1, Pallas kernels, total_over(): pl.pallas_call(functools.partial(total_kernel, count), out_shape=jax.Shap...  23 us
  transfers between devices with their start and end apart: 2, of which 1 were waited for; matrix products, arithmetic and copies ran while one was open for 17% of the time, Pallas kernels for 44%

profile of v1, /device:TPU:8, one launch (start us, length us, event | category | flops | bytes accessed | tf_op | source)
XLA Modules:
  0.0 649.7 jit_solution(6759936967829562475)
XLA Ops:
  7.3 1.9 constant_dynamic-slice_fusion
  13.6 5.2 fusion
  29.3 33.3 %attend.1 = (bf16[192,2048]{1,0:T(8,128)(2,1)}, bf16[16,192,512]{2,1,0:T(8,128)(2,1)}, f32[6,512,128]{2,1,0:T(8,128)}) custom-call(bf16[192,2048]{1,0:T(8,128)(2,1)} %bitcast.132, bf16[192,512]{1,0:T(8,128)(2,1)} %pad_maximum_fusion.2.x_ref), custom_call_target="tpu_custom_call" | custom-call | tf_op jit(solution)/shard_map/attend/pallas_call | solution.py:1178
  62.6 6.3 convolution_convert_fusion.1.x_ref
  68.9 4.6 swap_heads.1
  80.9 34.8 %all-gather.3.cloned.1.call-done = bf16[1536,2048]{1,0:T(8,128)(2,1)} async-done(((bf16[96,2048]{1,0:T(8,128)(2,1)}), bf16[1536,2048]{1,0:T(8,128)(2,1)}) %all-gather.3.cloned.1.call-update) | async-done | bytes 6291472 | tf_op jit(solution)/shard_map/all_gather | solution.py:1893
  115.7 185.3 %experts.1 = (bf16[16,192,2176]{2,1,0:T(8,128)(2,1)}, bf16[16,96,2048]{2,1,0:T(8,128)(2,1)}, bf16[16,192,1024]{2,1,0:T(8,128)(2,1)}, bf16[2,192,1152]{2,1,0:T(8,...) custom-call(bf16[192,2176]{1,0:T(8,128)(2,1)} %concatenate.41.parcel_ref, ...), custom_call_target="tpu_custom_call" | custom-call | tf_op jit(solution)/shard_map/experts/pallas_call | solution.py:996
  315.1 7.5 %convolution_convert_fusion.g_ref = bf16[192,2048]{1,0:T(8,128)(2,1)} fusion(bf16[192,2048]{1,0:T(8,128)(2,1)} %copy-done.22, bf16[2048,2048]{1,0:T(8,128)(2,1)} %param.21), kind=kOutput, calls=%fused_computation.8 | convolution fusion | flops 1611005952 | bytes 9961472 | tf_op jit(solution)/shard_map/dot_general | solution.py:1941
  322.7 87.1 %attend_back.1 = (f32[192,2048]{1,0:T(8,128)}, f32[192,512]{1,0:T(8,128)}, bf16[4,192,2048]{2,1,0:T(8,128)(2,1)}, bf16[4,192,512]{2,1,0:T(8,128)(2,1)}) custom-call(bf16[192,2048]{1,0:T(8,128)(2,1)} %bitcast.133, bf16[192,2048]{1,0:T(8,128)(2,1)} %convolution_convert_fusion.g_ref, bf16[192,2048]{1,0:T(8,128)(2,1)} %get-tuple-element.28.o_ref, ...), custom_call_target="tpu_custom_call" | custom-call | tf_op jit(solution)/shard_map/attend_back/pallas_call | solution.py:1405
  420.8 3.1 fusion.5
  425.0 6.5 %fusion.34 = f32[192,2048]{1,0:T(8,128)S(1)} fusion(bf16[2048,2048]{1,0:T(8,128)(2,1)} %param.18, bf16[24,8,16,128]{3,2,1,0:T(8,128)(2,1)S(1)} %bitcast.146), kind=kOutput, calls=%fused_computation.125 | convolution fusion | flops 1610612736 | bytes 10747904 | tf_op jit(solution)/shard_map/dot_general | solution.py:1970
  434.3 2.7 swap_normed.1
  441.6 3.2 bitcast_convert_fusion.1
  444.8 43.9 %scatter_mixing.1 = f32[128,2048]{1,0:T(8,128)} custom-call(bf16[4,128,2048]{2,1,0:T(8,128)(2,1)} %bitcast.131), custom_call_target="tpu_custom_call" | custom-call | tf_op jit(solution)/shard_map/scatter_mixing/pallas_call | solution.py:380
  488.7 2.6 copy.105
  491.4 1.9 pad_maximum_fusion.g_ref
  493.3 42.9 %plane_queries.1 = (bf16[4,192,2560]{2,1,0:T(8,128)(2,1)}, bf16[4,192,512]{2,1,0:T(8,128)(2,1)}) custom-call(bf16[192,2560]{1,0:T(8,128)(2,1)} %pad_maximum_fusion.g_ref, bf16[4,192,512]{2,1,0:T(8,128)(2,1)} %reshape.337.s_ref), custom_call_target="tpu_custom_call" | custom-call | tf_op jit(solution)/shard_map/plane_queries/pallas_call | solution.py:464
  536.2 6.1 bitcast_convert_fusion
  542.3 48.3 %scatter_queries.1 = f32[128,2560]{1,0:T(8,128)} custom-call(bf16[4,128,2560]{2,1,0:T(8,128)(2,1)} %bitcast.147), custom_call_target="tpu_custom_call" | custom-call | tf_op jit(solution)/shard_map/scatter_queries/pallas_call | solution.py:380
  590.6 2.4 slice.82
  595.1 3.7 concatenate.45.x_ref
  598.8 23.0 %total_small.1 = f32[32,2048]{1,0:T(8,128)} custom-call(f32[32,2048]{1,0:T(8,128)} %concatenate.45.x_ref), custom_call_target="tpu_custom_call" | custom-call | tf_op jit(solution)/shard_map/total_small/pallas_call | solution.py:517
  628.5 3.4 fusion.6
  633.8 3.9 copy.155
  (228 shorter events, 70.5 us)
Async XLA Ops:
  7.2 3.1 copy-start
  7.2 2.8 copy-start.39
  7.2 108.5 %all-gather.3.cloned.1.call-start = ((), (), s32[]{:S(2)}) async-start(), calls=%async_computation.2 | async-start | bytes 6684672 | tf_op jit(solution)/shard_map/all_gather | solution.py:1893
  9.2 622.8 %reduce-scatter.2.cloned.1.call-start = ((), (), s32[]{:S(2)}) async-start(), calls=%async_computation.1 | async-start | bytes 6684672 | tf_op jit(solution)/shard_map/reduce_scatter | solution.py:1919
  10.8 7.9 %copy-start.14 = (f32[3,64,2,128]{3,2,1,0:T(2,128)}, f32[3,64,2,128]{3,2,1,0:T(2,128)S(1)}, u32[]{:S(2)}) copy-start(f32[3,64,2,128]{3,2,1,0:T(2,128)S(1)} %reshape.324) | copy-start | bytes 589828
  12.0 6.8 %copy-start.26 = (f32[64,64]{1,0:T(8,128)}, f32[64,64]{1,0:T(8,128)S(1)}, u32[]{:S(2)}) copy-start(f32[64,64]{1,0:T(8,128)S(1)} %get-tuple-element.173) | copy-start | bytes 49156
  19.1 7.0 %copy-start.3 = (f32[24,8,16,128]{3,2,1,0:T(8,128)}, f32[24,8,16,128]{3,2,1,0:T(8,128)S(1)}, u32[]{:S(2)}) copy-start(f32[24,8,16,128]{3,2,1,0:T(8,128)S(1)} %copy.131) | copy-start | bytes 4718596
  19.1 5.6 copy-start.58
  62.6 10.9 %copy-start.53 = (s32[3,64,8]{1,2,0:T(8,128)S(1)}, s32[3,64,8]{1,2,0:T(8,128)}, u32[]{:S(2)}) copy-start(s32[3,64,8]{1,2,0:T(8,128)} %param.29) | copy-start | bytes 18436
  68.9 6.0 copy-start.6
  68.9 6.0 copy-start.23
  302.0 5.1 copy-start.2
  303.3 3.8 copy-start.34
  303.3 3.8 copy-start.37
  303.3 3.8 copy-start.50
  409.7 3.9 copy-start.15
  409.7 3.9 copy-start.57
  409.7 4.7 copy-start.46
  437.0 3.2 copy-start.29
  438.5 3.1 copy-start.20
  542.3 50.8 %copy-start.12 = (bf16[192,2048]{1,0:T(8,128)(2,1)S(1)}, bf16[192,2048]{1,0:T(8,128)(2,1)}, u32[]{:S(2)}) copy-start(bf16[192,2048]{1,0:T(8,128)(2,1)} %copy-done.11) | copy-start | bytes 2359300
  542.3 50.8 %copy-start.42 = (bf16[192,16]{0,1:T(8,128)(2,1)S(1)}, bf16[192,16]{0,1:T(8,128)(2,1)}, u32[]{:S(2)}) copy-start(bf16[192,16]{0,1:T(8,128)(2,1)} %copy-done.41) | copy-start | bytes 18436
  633.8 3.9 copy-start.19
  637.7 3.0 copy-start.18
  (40 other events, 64.8 us)
Sparse Core Ops, SparseCore 0:
  11.4 104.2 all-gather.2
  301.2 153.7 reduce-scatter.1

commit v2 on v1

--- a/solution.py
+++ b/solution.py
@@ -33,7 +33,7 @@
     def core(self):
         return (self.e, 1 - self.t)
 
-    def greet(self, planes, chain, flat, share):
+    def greet(self, planes, chain, flat, share, far=False, corner=False):
         barrier = pltpu.get_barrier_semaphore()
         total = 0
 
@@ -47,7 +47,14 @@
             call(self.at(self.a, 1 - self.b, self.c))
             call(self.at(self.a, self.b, 1 - self.c))
             total = total + 2
-        if chain:
+        if corner:
+            call(self.at(self.a, 1 - self.b, 1 - self.c))
+            total = total + 1
+        if far:
+            for k in range(1, planes):
+                call(self.at(lax.rem(self.a + k, planes), self.b, self.c))
+            total = total + planes - 1
+        elif chain:
             up = self.a + 1 < planes
             down = self.a > 0
 
@@ -67,124 +74,6 @@
     return pltpu.make_async_remote_copy(
         src_ref=src, dst_ref=dst, send_sem=send_sem, recv_sem=recv_sem, device_id=who, device_id_type=MESH
     )
-
-
-def offsets(planes):
-    out = [0]
-    for step in range(1, planes):
-        out += [step, -step]
-    return out
-
-
-def gather_kernel(planes, share, x_ref, o_ref, ssem, rsem, csem, lsem):
-    me = Spot()
-    rows = x_ref.shape[0]
-    half = rows // 2 if share else rows
-    start = pl.multiple_of(me.t * half, half) if share else 0
-    span = pl.ds(start, half)
-    own = me.index(me.a, me.b, me.c)
-
-    def copy(idx, kind, src=None):
-        who = {
-            0: me.at(me.a + 1, me.b, me.c),
-            1: me.at(me.a - 1, me.b, me.c),
-            2: me.at(me.a, 1 - me.b, me.c),
-            3: me.at(me.a, me.b, 1 - me.c),
-            4: me.core(),
-        }[kind]
-        there = o_ref.at[idx, span]
-        landed = csem if kind == 4 else rsem
-        return push(there if src is None else src, there, ssem.at[idx, kind], landed.at[idx], who)
-
-    local = pltpu.make_async_copy(x_ref, o_ref.at[own], lsem)
-    local.start()
-    me.greet(planes, True, True, share)
-
-    def each(act):
-        for da in offsets(planes):
-            sa = me.a + da
-
-            @pl.when((sa >= 0) & (sa < planes))
-            def _(da=da, sa=sa):
-                idx = me.index(sa, me.b, me.c)
-                src = x_ref.at[span] if da == 0 else None
-                if da != 0 and act == "start":
-                    copy(idx, 2).wait_recv()
-                if da <= 0:
-
-                    @pl.when(me.a + 1 < planes)
-                    def _():
-                        run(copy(idx, 0, src))
-
-                if da >= 0:
-
-                    @pl.when(me.a > 0)
-                    def _():
-                        run(copy(idx, 1, src))
-
-                run(copy(idx, 3, src))
-                run(copy(idx, 2, src))
-                if share and da != 0:
-                    run(copy(idx, 4))
-                idx = me.index(sa, 1 - me.b, me.c)
-                if act == "start":
-                    copy(idx, 2).wait_recv()
-                run(copy(idx, 3))
-                if share:
-                    run(copy(idx, 4))
-
-        for da in offsets(planes):
-            sa = me.a + da
-
-            @pl.when((sa >= 0) & (sa < planes))
-            def _(da=da, sa=sa):
-                for sb in (me.b, 1 - me.b):
-                    idx = me.index(sa, sb, 1 - me.c)
-                    if act == "start":
-                        copy(idx, 2).wait_recv()
-                    if share:
-                        run(copy(idx, 4))
-
-    def run(c):
-        c.start() if mode[0] == "start" else c.wait_send()
-
-    mode = ["start"]
-    each("start")
-    mode[0] = "wait"
-    each("wait")
-    if share:
-        other = pl.ds(pl.multiple_of((1 - me.t) * half, half), half)
-        for da in offsets(planes):
-            sa = me.a + da
-
-            @pl.when((sa >= 0) & (sa < planes))
-            def _(da=da, sa=sa):
-                for sb in (me.b, 1 - me.b):
-                    for sc in (me.c, 1 - me.c):
-                        if da == 0 and sb is me.b and sc is me.c:
-                            continue
-                        idx = me.index(sa, sb, sc)
-                        there = o_ref.at[idx, other]
-                        push(there, there, ssem.at[idx, 4], csem.at[idx], me.core()).wait_recv()
-    local.wait()
-
-
-def gather_rows(x, planes, share, cid, name):
-    count = planes * 4
-    return pl.pallas_call(
-        functools.partial(gather_kernel, planes, share),
-        out_shape=jax.ShapeDtypeStruct((count,) + x.shape, x.dtype),
-        in_specs=[pl.BlockSpec(memory_space=pl.ANY)],
-        out_specs=pl.BlockSpec(memory_space=pl.ANY),
-        scratch_shapes=[
-            pltpu.SemaphoreType.DMA((count, 5)),
-            pltpu.SemaphoreType.DMA((count,)),
-            pltpu.SemaphoreType.DMA((count,)),
-            pltpu.SemaphoreType.DMA,
-        ],
-        compiler_params=pltpu.CompilerParams(collective_id=cid, has_side_effects=True),
-        name=name,
-    )(x)
 
 
 def add_rows(target, parts):
@@ -207,196 +96,6 @@
     low = jnp.where(i < last - a, last - i, jnp.where(i < last, i - (last - a), a))
     high = jnp.where(i < a, i, jnp.where(i < last, last - (i - a), a))
     return jnp.where(2 * a < last, low, high)
-
-
-def scatter_kernel(
-    planes, flat, share, p_ref, o_ref, mine, land0, landc, landb, landa, lsem, csem, rsem, ssem, esem
-):
-    me = Spot()
-    rows = p_ref.shape[1]
-    half = rows // 2 if share else rows
-    ours = pl.ds(pl.multiple_of(me.t * half, half), half) if share else pl.ds(0, half)
-    other = pl.ds(pl.multiple_of((1 - me.t) * half, half), half)
-    order = [far_first(me.a, planes, i) for i in range(planes)]
-
-    def block(sa, sb, sc):
-        return me.index(sa, sb, sc) if flat else sa
-
-    def load(idx):
-        return pltpu.make_async_copy(p_ref.at[idx, ours], mine.at[idx], lsem.at[idx])
-
-    def trade(idx):
-        return push(p_ref.at[idx, other], land0.at[idx], ssem.at[0, idx], csem.at[idx], me.core())
-
-    spots = [(sb, sc) for sc in (1 - me.c, me.c) for sb in (1 - me.b, me.b)] if flat else [(me.b, me.c)]
-    for sa in order:
-        for sb, sc in spots:
-            load(block(sa, sb, sc)).start()
-    me.greet(planes, True, flat, share)
-    if share:
-        for sa in order:
-            for sb, sc in spots:
-                trade(block(sa, sb, sc)).start()
-
-    def send_c(sa, sb):
-        slot = sa * 2 + sb
-        return push(
-            mine.at[me.index(sa, sb, 1 - me.c)],
-            landc.at[slot],
-            ssem.at[1, slot],
-            rsem.at[0, slot],
-            me.at(me.a, me.b, 1 - me.c),
-        )
-
-    def send_b(sa):
-        return push(
-            mine.at[me.index(sa, 1 - me.b, me.c)],
-            landb.at[sa],
-            ssem.at[2, sa],
-            rsem.at[1, sa],
-            me.at(me.a, 1 - me.b, me.c),
-        )
-
-    def send_a(sa, up):
-        arrive = me.a + 1 if up else me.a - 1
-        slot = sa if up else jnp.where(sa == arrive, planes, sa)
-        return push(
-            mine.at[block(sa, me.b, me.c)],
-            landa.at[slot],
-            ssem.at[3, sa],
-            rsem.at[2, slot],
-            me.at(arrive, me.b, me.c),
-        )
-
-    if flat:
-        for sa in order:
-            for sb, sc in spots:
-                idx = me.index(sa, sb, sc)
-                load(idx).wait()
-                if share:
-                    trade(idx).wait_recv()
-                    add_rows(mine.at[idx], [mine.at[idx], land0.at[idx]])
-                if sc is spots[0][1]:
-                    send_c(sa, sb).start()
-
-    def from_c(sa):
-        for sb in (1 - me.b, me.b):
-            slot = sa * 2 + sb
-            push(landc.at[slot], landc.at[slot], ssem.at[1, slot], rsem.at[0, slot], me.at(me.a, me.b, 1 - me.c)).wait_recv()
-            idx = me.index(sa, sb, me.c)
-            add_rows(mine.at[idx], [mine.at[idx], landc.at[slot]])
-            if sb is not me.b:
-                send_b(sa).start()
-
-    def along(i, sa):
-        idx = block(sa, me.b, me.c)
-        parts = [mine.at[idx]]
-        if flat:
-            push(landb.at[sa], landb.at[sa], ssem.at[2, sa], rsem.at[1, sa], me.at(me.a, 1 - me.b, me.c)).wait_recv()
-            parts = parts + [landb.at[sa]]
-        else:
-            load(idx).wait()
-
-        def landed(slot):
-            push(landa.at[slot], landa.at[slot], ssem.at[3, 0], rsem.at[2, slot], me.at(me.a, me.b, me.c)).wait_recv()
-
-        if i < planes - 1:
-            up = sa > me.a
-            inner = (up & (me.a > 0)) | (jnp.logical_not(up) & (me.a + 1 < planes))
-
-            @pl.when(inner)
-            def _():
-                landed(sa)
-                add_rows(mine.at[idx], parts + [landa.at[sa]])
-
-            if len(parts) > 1:
-
-                @pl.when(jnp.logical_not(inner))
-                def _():
-                    add_rows(mine.at[idx], parts)
-
-            @pl.when(up)
-            def _():
-                send_a(sa, True).start()
-
-            @pl.when(jnp.logical_not(up))
-            def _():
-                send_a(sa, False).start()
-
-        else:
-            target = o_ref.at[ours] if share else o_ref
-
-            @pl.when(me.a > 0)
-            def _():
-                landed(me.a)
-
-            @pl.when(me.a + 1 < planes)
-            def _():
-                landed(planes)
-
-            @pl.when((me.a > 0) & (me.a + 1 < planes))
-            def _():
-                add_rows(target, parts + [landa.at[me.a], landa.at[planes]])
-
-            @pl.when(me.a == 0)
-            def _():
-                add_rows(target, parts + [landa.at[planes]])
-
-            @pl.when(me.a + 1 == planes)
-            def _():
-                add_rows(target, parts + [landa.at[me.a]])
-
-    for i in range(planes + 1):
-        if flat and i < planes:
-            from_c(order[i])
-        if i > 0:
-            along(i - 1, order[i - 1])
-    if share:
-        done = push(o_ref.at[ours], o_ref.at[ours], esem.at[0], esem.at[1], me.core())
-        done.start()
-    for i, sa in enumerate(order):
-        if flat:
-            for sb, sc in spots:
-                if share:
-                    trade(me.index(sa, sb, sc)).wait_send()
-            for sb in (1 - me.b, me.b):
-                send_c(sa, sb).wait_send()
-            send_b(sa).wait_send()
-        if i < planes - 1:
-            send_a(sa, False).wait_send()
-    if share:
-        done.wait_send()
-        push(o_ref.at[other], o_ref.at[other], esem.at[0], esem.at[1], me.core()).wait_recv()
-
-
-def scatter_sum(p, planes, flat, share, out_type, cid, name):
-    count, rows, width = p.shape
-    half = rows // 2 if share else rows
-    one = (16, width)
-
-    def space(use, slots):
-        return pltpu.VMEM((slots, half, width), p.dtype) if use else pltpu.VMEM((1,) + one, p.dtype)
-
-    return pl.pallas_call(
-        functools.partial(scatter_kernel, planes, flat, share),
-        out_shape=jax.ShapeDtypeStruct((rows, width), out_type),
-        in_specs=[pl.BlockSpec(memory_space=pl.ANY)],
-        out_specs=pl.BlockSpec(memory_space=pltpu.VMEM),
-        scratch_shapes=[
-            space(True, count),
-            space(share, count),
-            space(flat, 2 * planes),
-            space(flat, planes),
-            space(True, planes + 1),
-            pltpu.SemaphoreType.DMA((count,)),
-            pltpu.SemaphoreType.DMA((count,)),
-            pltpu.SemaphoreType.DMA((3, max(2 * planes, planes + 1))),
-            pltpu.SemaphoreType.DMA((4, max(count, 2 * planes))),
-            pltpu.SemaphoreType.DMA((2,)),
-        ],
-        compiler_params=pltpu.CompilerParams(collective_id=cid, has_side_effects=True, vmem_limit_bytes=ROOM),
-        name=name,
-    )(p)
 
 
 def swap_kernel(x_ref, o_ref, sems):
@@ -419,117 +118,6 @@
     )(x)
 
 
-def plane_kernel(g_ref, s_ref, go_ref, so_ref, ssem, rsem, lsem):
-    me = Spot()
-    q = lax.rem(me.e, 4)
-    base = me.e - q
-
-    def spot(b, c):
-        return me.index(0, b, c)
-
-    near = [(1 - me.b, me.c), (me.b, 1 - me.c), (1 - me.b, 1 - me.c)]
-    barrier = pltpu.get_barrier_semaphore()
-    for b, c in near:
-        pl.semaphore_signal(barrier, inc=1, device_id=(base + spot(b, c), me.t), device_id_type=MESH)
-    keep = [
-        pltpu.make_async_copy(g_ref, go_ref.at[q], lsem.at[0]),
-        pltpu.make_async_copy(s_ref.at[q], so_ref.at[q], lsem.at[1]),
-    ]
-    for k in keep:
-        k.start()
-    pl.semaphore_wait(barrier, 3)
-    whole = [
-        push(g_ref, go_ref.at[q], ssem.at[i], rsem.at[i], (base + spot(*near[i]), me.t)) for i in range(2)
-    ]
-    parts = [
-        push(s_ref.at[spot(*near[i])], so_ref.at[q], ssem.at[3 + i], rsem.at[3 + i], (base + spot(*near[i]), me.t))
-        for i in range(3)
-    ]
-    for k in whole + parts:
-        k.start()
-    whole[0].wait_recv()
-    source = spot(*near[0])
-    relay = push(go_ref.at[source], go_ref.at[source], ssem.at[2], rsem.at[2], (base + spot(*near[1]), me.t))
-    relay.start()
-    whole[0].wait_send()
-    whole[1].wait()
-    for k in parts:
-        k.wait()
-    relay.wait()
-    for k in keep:
-        k.wait()
-
-
-def plane_exchange(g, s, cid, name):
-    return pl.pallas_call(
-        plane_kernel,
-        out_shape=[jax.ShapeDtypeStruct((4,) + g.shape, g.dtype), jax.ShapeDtypeStruct(s.shape, s.dtype)],
-        in_specs=[pl.BlockSpec(memory_space=pl.ANY)] * 2,
-        out_specs=[pl.BlockSpec(memory_space=pl.ANY)] * 2,
-        scratch_shapes=[
-            pltpu.SemaphoreType.DMA((6,)),
-            pltpu.SemaphoreType.DMA((6,)),
-            pltpu.SemaphoreType.DMA((2,)),
-        ],
-        compiler_params=pltpu.CompilerParams(collective_id=cid, has_side_effects=True),
-        name=name,
-    )(g, s)
-
-
-def total_kernel(count, x_ref, o_ref, land, send, ssem, rsem):
-    me = Spot()
-    rows = x_ref.shape[0]
-    half = rows // 2
-    ours = pl.ds(pl.multiple_of(me.t * half, half), half)
-    other = pl.ds(pl.multiple_of((1 - me.t) * half, half), half)
-    steps = []
-    bit = 1
-    while bit < count:
-        steps.append(me.e + bit * (1 - 2 * lax.rem(lax.div(me.e, bit), 2)))
-        bit *= 2
-    barrier = pltpu.get_barrier_semaphore()
-    for who in steps:
-        pl.semaphore_signal(barrier, inc=1, device_id=(who, me.t), device_id_type=MESH)
-    pl.semaphore_signal(barrier, inc=1, device_id=me.core(), device_id_type=MESH)
-    pl.semaphore_wait(barrier, len(steps) + 1)
-    send[0] = x_ref[ours, :]
-    copies = []
-    for i, who in enumerate(steps):
-        c = push(send.at[i], land.at[i], ssem.at[i], rsem.at[i], (who, me.t))
-        c.start()
-        copies.append(c)
-        c.wait_recv()
-        if i + 1 < len(steps):
-            send[i + 1] = send[i] + land[i]
-        else:
-            o_ref[ours, :] = send[i] + land[i]
-    last = push(o_ref.at[ours], o_ref.at[ours], ssem.at[len(steps)], rsem.at[len(steps)], me.core())
-    last.start()
-    for c in copies:
-        c.wait_send()
-    last.wait_send()
-    push(o_ref.at[other], o_ref.at[other], ssem.at[len(steps)], rsem.at[len(steps)], me.core()).wait_recv()
-
-
-def total_over(x, count, cid, name):
-    steps = count.bit_length() - 1
-    half = (x.shape[0] // 2, x.shape[1])
-    return pl.pallas_call(
-        functools.partial(total_kernel, count),
-        out_shape=jax.ShapeDtypeStruct(x.shape, x.dtype),
-        in_specs=[pl.BlockSpec(memory_space=pltpu.VMEM)],
-        out_specs=pl.BlockSpec(memory_space=pltpu.VMEM),
-        scratch_shapes=[
-            pltpu.VMEM((steps,) + half, x.dtype),
-            pltpu.VMEM((steps,) + half, x.dtype),
-            pltpu.SemaphoreType.DMA((steps + 1,)),
-            pltpu.SemaphoreType.DMA((steps + 1,)),
-        ],
-        compiler_params=pltpu.CompilerParams(collective_id=cid, has_side_effects=True),
-        name=name,
-    )(x)
-
-
 def over(first, second, contract):
     return lax.dot_general(first, second, (contract, ((), ())), preferred_element_type=jnp.float32)
 
@@ -546,10 +134,14 @@
     gate_in,
     lift_in,
     down_in,
+    context_ref,
+    cut_ref,
     all_ref,
     other_ref,
     share_ref,
     home_ref,
+    column_ref,
+    cut_all,
     gate_sum,
     lift_sum,
     down_sum,
@@ -571,6 +163,8 @@
     scores,
     stage,
     mine,
+    outgoing,
+    partner,
     landc,
     landb,
     landa,
@@ -589,6 +183,10 @@
     lsem,
     osem,
     esem,
+    xsend,
+    xrecv,
+    csend,
+    crecv,
 ):
     me = Spot()
     f32, bf16 = jnp.float32, jnp.bfloat16
@@ -622,7 +220,7 @@
         landed = gcore if kind == 4 else grecv
         return push(there if src is None else src, there, gsend.at[idx, kind], landed.at[idx], who)
 
-    def relay(sa, act, first):
+    def relay_a(sa, act, first):
         idx = me.index(sa, me.b, me.c)
         src = parcel_ref.at[ours] if first else None
         if act and not first:
@@ -641,7 +239,10 @@
         run(carry(idx, 2, src))
         if not first:
             run(carry(idx, 4))
+
+    def relay_b(sa, act):
         idx = me.index(sa, 1 - me.b, me.c)
+        run = (lambda c: c.start()) if act else (lambda c: c.wait_send())
         if act:
             carry(idx, 2).wait_recv()
         run(carry(idx, 3))
@@ -688,83 +289,89 @@
 
     def send_c(sa, sb):
         slot = sa * 2 + sb
-        src = mine.at[me.index(sa, sb, 1 - me.c)]
-        return push(src, landc.at[slot], ssem.at[0, slot], rsem.at[0, slot], me.at(me.a, me.b, 1 - me.c))
+        there = me.at(me.a, me.b, 1 - me.c)
+        return push(outgoing.at[slot], landc.at[slot], ssem.at[0, slot], rsem.at[0, slot], there)
 
     def send_b(sa):
-        src = mine.at[me.index(sa, 1 - me.b, me.c)]
+        src = mine.at[sa * 2 + 1 - me.b]
         return push(src, landb.at[sa], ssem.at[1, sa], rsem.at[1, sa], me.at(me.a, 1 - me.b, me.c))
 
-    def send_a(sa, up):
-        arrive = me.a + 1 if up else me.a - 1
-        slot = sa if up else jnp.where(sa == arrive, planes, sa)
-        src = mine.at[me.index(sa, me.b, me.c)]
-        return push(src, landa.at[slot], ssem.at[2, sa], rsem.at[2, slot], me.at(arrive, me.b, me.c))
+    def send_a(sa):
+        src = mine.at[sa * 2 + me.b]
+        return push(src, landa.at[me.a], ssem.at[2, sa], rsem.at[2, me.a], me.at(sa, me.b, me.c))
 
     def from_c(sa):
         for sb in (1 - me.b, me.b):
             slot = sa * 2 + sb
             push(landc.at[slot], landc.at[slot], ssem.at[0, slot], rsem.at[0, slot], me.at(me.a, me.b, 1 - me.c)).wait_recv()
-            idx = me.index(sa, sb, me.c)
-            add_rows(mine.at[idx], [mine.at[idx], landc.at[slot]])
+            for n in range(0, mine.shape[2], 384):
+                cut = slice(n, n + 384)
+                spread = over(partner[slot], landc[slot, :, cut], NN)
+                mine[slot, :, cut] = (mine[slot, :, cut].astype(f32) + spread).astype(bf16)
             if sb is not me.b:
                 send_b(sa).start()
 
-    def along(i, sa):
-        idx = me.index(sa, me.b, me.c)
+    def from_b(sa):
         push(landb.at[sa], landb.at[sa], ssem.at[1, sa], rsem.at[1, sa], me.at(me.a, 1 - me.b, me.c)).wait_recv()
-        parts = [mine.at[idx], landb.at[sa]]
-
-        def landed(slot):
-            push(landa.at[slot], landa.at[slot], ssem.at[2, 0], rsem.at[2, slot], me.at(me.a, me.b, me.c)).wait_recv()
-
-        if i < planes - 1:
-            up = sa > me.a
-            inner = (up & (me.a > 0)) | (jnp.logical_not(up) & (me.a + 1 < planes))
-
-            @pl.when(inner)
-            def _():
-                landed(sa)
-                add_rows(mine.at[idx], parts + [landa.at[sa]])
-
-            @pl.when(jnp.logical_not(inner))
-            def _():
-                add_rows(mine.at[idx], parts)
-
-            @pl.when(up)
-            def _():
-                send_a(sa, True).start()
-
-            @pl.when(jnp.logical_not(up))
-            def _():
-                send_a(sa, False).start()
-
-        else:
-            target = home_ref.at[me.t]
-
-            @pl.when(me.a > 0)
-            def _():
-                landed(me.a)
-
-            @pl.when(me.a + 1 < planes)
-            def _():
-                landed(planes)
-
-            @pl.when((me.a > 0) & (me.a + 1 < planes))
-            def _():
-                add_rows(target, parts + [landa.at[me.a], landa.at[planes]])
-
-            @pl.when(me.a == 0)
-            def _():
-                add_rows(target, parts + [landa.at[planes]])
-
-            @pl.when(me.a + 1 == planes)
-            def _():
-                add_rows(target, parts + [landa.at[me.a]])
+        return [mine.at[sa * 2 + me.b], landb.at[sa]]
+
+    def along(sa):
+        parts = from_b(sa)
+        add_rows(parts[0], parts)
+        send_a(sa).start()
+
+    def finish():
+        parts = from_b(me.a)
+        for k in range(1, planes):
+            far = lax.rem(me.a + k, planes)
+            push(landa.at[far], landa.at[far], ssem.at[2, far], rsem.at[2, far], me.at(far, me.b, me.c)).wait_recv()
+            parts = parts + [landa.at[far]]
+        add_rows(home_ref.at[me.t], parts)
+
+
+    def context_to(source, up, own_rows):
+        there = column_ref.at[source]
+        who = me.at(me.a + 1 if up else me.a - 1, me.b, me.c)
+        return push(context_ref if own_rows else there, there, xsend.at[source, int(up)], xrecv.at[source], who)
+
+    def context_pass(i, act):
+        for up in (True, False):
+            source = me.a - i if up else me.a + i
+            further = me.a + 1 < planes if up else me.a > 0
+            run = (lambda c: c.start()) if act else (lambda c: c.wait_send())
+
+            @pl.when((source >= 0) & (source < planes))
+            def _(source=source, up=up, further=further, run=run):
+                if act and i > 0:
+                    context_to(source, up, False).wait_recv()
+
+                @pl.when(further)
+                def _():
+                    run(context_to(source, up, i == 0))
+
+    place = lax.rem(me.e, 4)
+    peers = [me.index(0, b, c) for b, c in ((1 - me.b, me.c), (me.b, 1 - me.c), (1 - me.b, 1 - me.c))]
+
+    def cut_to(i):
+        there = (me.e - place + peers[i], me.t)
+        return push(cut_ref.at[peers[i]], cut_all.at[place], csend.at[i], crecv.at[i], there)
 
 
     def load_rows(sa, q):
         return pltpu.make_async_copy(all_ref.at[sa * 4 + q], pbuf.at[q], lsem.at[q])
+
+    def fetch_rows(sa):
+        from_core(sa)
+        for q in range(4):
+            mine_here = sa * 4 + q == own
+
+            @pl.when(mine_here)
+            def _(q=q):
+                pltpu.make_async_copy(parcel_ref, pbuf.at[q], lsem.at[q]).start()
+
+            @pl.when(jnp.logical_not(mine_here))
+            def _(q=q):
+                load_rows(sa, q).start()
 
     def load_up(sa):
         group = pl.ds(sa * 4, 4)
@@ -782,27 +389,42 @@
     def lanes(rows):
         return lax.broadcasted_iota(jnp.int32, (rows, notes_width), 1)
 
-    def pick_rows(q, sa):
+    def side_of(q):
+        y, x = lax.div(q, 2), lax.rem(q, 2)
+        return x + me.t * (y - x), y + me.t * (x - y)
+
+    def chosen_by(expert, notes):
+        slot_of = jnp.sum(jnp.where(lanes(tokens) == expert, notes, 0.0), axis=1, keepdims=True)
+        chosen = slot_of == lax.broadcasted_iota(jnp.int32, (tokens, slots), 1).astype(f32)
+        return jnp.where(chosen, 1.0, 0.0).astype(bf16)
+
+    def pick_rows(q, carried):
+        sa, slot = carried
         load_rows(sa, q).wait()
         notes = pbuf[q, :, width:].astype(f32)
-        slot_of = jnp.sum(jnp.where(lanes(tokens) == me.e, notes, 0.0), axis=1, keepdims=True)
-        chosen = slot_of == lax.broadcasted_iota(jnp.int32, (tokens, slots), 1).astype(f32)
-        chosen = jnp.where(chosen, 1.0, 0.0).astype(bf16)
+        sb, sc = side_of(q)
+
+        @pl.when(sc == me.c)
+        def _():
+            partner[sa * 2 + sb] = chosen_by(me.index(me.a, me.b, 1 - me.c), notes)
+
+        chosen = chosen_by(me.e, notes)
         sbuf[q] = chosen
+        pick = jnp.transpose(chosen.astype(f32)).astype(bf16)
         at = pl.ds(pl.multiple_of(q * slots, slots), slots)
-        there = over(chosen, pbuf[q, :, width:], TN)
+        there = over(pick, pbuf[q, :, width:], NN)
         mark = lanes(slots)
         gate = jnp.sum(jnp.where((mark == count + me.e) | (mark == 2 * count + me.e), there, 0.0), axis=1, keepdims=True)
         gates[at, :] = jnp.broadcast_to(gate, (slots, 128))
         for n in range(0, width, 512):
             cut = slice(n, n + 512)
-            xbuf[at, cut] = over(chosen, pbuf[q, :, cut], TN).astype(bf16)
-            picked = over(chosen, ubuf[q, :, cut], TN)
+            xbuf[at, cut] = over(pick, pbuf[q, :, cut], NN).astype(bf16)
+            picked = over(pick, ubuf[q, :, cut], NN)
             gbuf[at, cut] = (picked * gate).astype(bf16)
         for n in range(0, side, 512):
             cut = pl.ds(pl.multiple_of(me.t * side + n, 512), 512)
-            vbuf[at, n : n + 512] = over(chosen, ubuf[q, :, cut], TN).astype(bf16)
-        return sa
+            vbuf[at, n : n + 512] = over(pick, ubuf[q, :, cut], NN).astype(bf16)
+        return carried
 
     def hidden_cols(p):
         return pl.ds(pl.multiple_of(p * hidden, 128), hidden)
@@ -840,8 +462,9 @@
     def weight_sums(n, slot):
         cut = pl.ds(pl.multiple_of(n * 512, 512), 512)
         own_d = dbuf[slot, :, both_cols(me.t)]
-        gate_sum[cut, :] += over(xbuf[:, cut], own_d[:, :hidden], TN)
-        lift_sum[cut, :] += over(xbuf[:, cut], own_d[:, hidden:], TN)
+        rows = xbuf[:, cut]
+        gate_sum[cut, :] += over(rows, own_d[:, :hidden], TN)
+        lift_sum[cut, :] += over(rows, own_d[:, hidden:], TN)
         down_sum[:, cut] += over(hbuf[slot, :, hidden_cols(me.t)], gbuf[:, cut], TN)
         return slot
 
@@ -870,60 +493,64 @@
         at = pl.ds(pl.multiple_of(q * slots, slots), slots)
         idx = sa * 4 + q
 
-        @pl.when(q >= 2)
+        @pl.when((q >= 2) | (sa != near(1)))
         def _():
             store(idx, q).wait()
 
         for n in range(0, side, 512):
             cut = slice(n, n + 512)
-            mine[idx, :, cut] = over(sbuf[q], rbuf[at, cut], NN).astype(bf16)
             stage[lax.rem(q, 2), :, cut] = over(sbuf[q], wbuf[at, cut], NN).astype(bf16)
-        mine[idx, :, side:] = over(sbuf[q], rbuf[at, side:], NN).astype(bf16)
+        sb, sc = side_of(q)
+        slot = sa * 2 + sb
+
+        @pl.when(sc == me.c)
+        def _():
+            for n in range(0, mine.shape[2], 384):
+                cut = slice(n, n + 384)
+                mine[slot, :, cut] = over(sbuf[q], rbuf[at, cut], NN).astype(bf16)
+
+        @pl.when(sc != me.c)
+        def _():
+            outgoing[slot] = rbuf[at, :]
+            send_c(sa, sb).start()
+
         store(idx, q).start()
         return sa
 
-    local = pltpu.make_async_copy(parcel_ref, all_ref.at[own], lsem.at[6])
-    local.start()
-    me.greet(planes, True, True, True)
-    relay(me.a, True, True)
-    for i in list(range(1, planes)) + [0]:
+    me.greet(planes, True, True, True, True, True)
+    relay_a(me.a, True, True)
+    for i in range(planes):
         upstream(near(i)).start()
     for k in loads + pushes:
         k.start()
-    relay(near(1), True, False)
     gate_sum[...] = jnp.zeros_like(gate_sum)
     lift_sum[...] = jnp.zeros_like(lift_sum)
     down_sum[...] = jnp.zeros_like(down_sum)
+    fetch_up(near(1))
+    relay_b(me.a, True)
+    relay_a(near(1), True, False)
     across(me.a, True)
-    fetch_up(near(1))
+    for i in range(2, planes):
+        relay_a(near(i), True, False)
+        relay_b(near(i - 1), True)
+    across(near(1), True)
+    fetch_rows(near(1))
     for k in loads + pushes:
         k.wait()
-    local.wait()
 
     def step(i, c):
         last = i == planes - 1
         sa = jnp.where(last, me.a, near(i + 1))
+        after = jnp.where(i + 2 < planes, near(i + 2), me.a)
         slot = lax.rem(i, 2)
-
-        @pl.when(i + 2 < planes)
-        def _():
-            relay(near(i + 2), True, False)
-
-        @pl.when(jnp.logical_not(last))
-        def _():
-            across(sa, True)
-
-        from_core(sa)
-        for q in range(4):
-            load_rows(sa, q).start()
         for k in load_up(sa):
             k.wait()
         scores[...] = jnp.zeros_like(scores)
-        lax.fori_loop(0, 4, pick_rows, sa)
-
-        @pl.when(jnp.logical_not(last))
-        def _():
-            fetch_up(jnp.where(i + 1 == planes - 1, me.a, near(i + 2)))
+        lax.fori_loop(0, 4, pick_rows, (sa, slot))
+
+        @pl.when(i + 1 < planes)
+        def _():
+            fetch_up(after)
 
         @pl.when(i > 0)
         def _():
@@ -933,39 +560,63 @@
         lax.fori_loop(0, 4 * slots // 256, hidden_rows, slot)
         for k in trades(slot):
             k.start()
-        lax.fori_loop(0, width // 512, weight_sums, slot)
+
+        @pl.when(i == 0)
+        def _():
+            relay_b(near(planes - 1), True)
+            context_pass(0, True)
+            for k in range(3):
+                cut_to(k).start()
+
+        @pl.when(i > 0)
+        def _():
+            from_c(near(i))
+
         traded(slot)
         lax.fori_loop(0, side // 512, out_rows, slot)
         note_scores()
         lax.fori_loop(0, 4, spread_rows, sa)
-        for sb in (1 - me.b, me.b):
-            send_c(sa, sb).start()
-        store(0, 0).wait()
-        store(0, 1).wait()
+
+        @pl.when(i + 2 < planes)
+        def _():
+            across(after, True)
+
+        @pl.when(jnp.logical_not(last))
+        def _():
+            fetch_rows(after)
+
+        lax.fori_loop(0, width // 512, weight_sums, slot)
 
         @pl.when(i > 0)
         def _():
-            from_c(near(i))
+            along(near(i))
+
+        for k in range(1, planes):
+
+            @pl.when(i == k)
+            def _(k=k):
+                context_pass(k, True)
 
         return c
 
     lax.fori_loop(0, planes, step, 0)
-    for i in range(planes - 1):
-        along(i, far_first(me.a, planes, i))
     from_c(me.a)
-    along(planes - 1, me.a)
+    finish()
+    store(0, 0).wait()
+    store(0, 1).wait()
     done = push(home_ref.at[me.t], home_ref.at[me.t], esem.at[0], esem.at[1], me.core())
     done.start()
 
-    relay(me.a, False, True)
+    relay_a(me.a, False, True)
 
     def settle(i, c):
         sa = near(i)
+        relay_b(sa, False)
 
         @pl.when(i > 0)
         def _():
-            relay(sa, False, False)
-            send_a(sa, False).wait_send()
+            relay_a(sa, False, False)
+            send_a(sa).wait_send()
 
         across(sa, False)
         for sb in (1 - me.b, me.b):
@@ -977,12 +628,16 @@
     lax.fori_loop(0, planes, settle, 0)
     for k in trades(0):
         k.wait_send()
+    for k in range(planes):
+        context_pass(k, False)
+    for k in range(3):
+        cut_to(k).wait()
     done.wait_send()
     other = home_ref.at[1 - me.t]
     push(other, other, esem.at[0], esem.at[1], me.core()).wait_recv()
 
 
-def run_experts(parcel, upstream, gate, lift_w, down, planes, slots, cid):
+def run_experts(parcel, upstream, gate, lift_w, down, context, cut, planes, slots, cid):
     f32, bf16 = jnp.float32, jnp.bfloat16
     tokens, packed = parcel.shape
     hidden, width = down.shape
@@ -1000,12 +655,14 @@
             jax.ShapeDtypeStruct((count, half, width), bf16),
             jax.ShapeDtypeStruct((count, tokens, side), bf16),
             jax.ShapeDtypeStruct((2, tokens, block), bf16),
+            jax.ShapeDtypeStruct((planes,) + context.shape, bf16),
+            jax.ShapeDtypeStruct(cut.shape, bf16),
             jax.ShapeDtypeStruct((width, hidden), f32),
             jax.ShapeDtypeStruct((width, hidden), f32),
             jax.ShapeDtypeStruct((hidden, width), f32),
         ],
-        in_specs=[anywhere] * 5,
-        out_specs=[anywhere] * 3 + [inside] * 4,
+        in_specs=[anywhere] * 7,
+        out_specs=[anywhere] * 3 + [inside, anywhere, anywhere] + [inside] * 3,
         scratch_shapes=[
             pltpu.VMEM((width, 2 * hidden), bf16),
             pltpu.VMEM((hidden, width), bf16),
@@ -1024,10 +681,12 @@
             pltpu.VMEM((rows, 128), f32),
             pltpu.VMEM((rows, 128), f32),
             pltpu.VMEM((2, tokens, side), bf16),
-            pltpu.VMEM((count, tokens, block), bf16),
             pltpu.VMEM((2 * planes, tokens, block), bf16),
+            pltpu.VMEM((2 * planes, slots, block), bf16),
+            pltpu.VMEM((2 * planes, tokens, slots), bf16),
+            pltpu.VMEM((2 * planes, slots, block), bf16),
             pltpu.VMEM((planes, tokens, block), bf16),
-            pltpu.VMEM((planes + 1, tokens, block), bf16),
+            pltpu.VMEM((planes, tokens, block), bf16),
             pltpu.SemaphoreType.DMA((count, 5)),
             pltpu.SemaphoreType.DMA((count,)),
             pltpu.SemaphoreType.DMA((count,)),
@@ -1043,12 +702,16 @@
             pltpu.SemaphoreType.DMA((7,)),
             pltpu.SemaphoreType.DMA((2,)),
             pltpu.SemaphoreType.DMA((2,)),
+            pltpu.SemaphoreType.DMA((planes, 2)),
+            pltpu.SemaphoreType.DMA((planes,)),
+            pltpu.SemaphoreType.DMA((3,)),
+            pltpu.SemaphoreType.DMA((3,)),
         ],
         compiler_params=pltpu.CompilerParams(
             collective_id=cid, has_side_effects=True, vmem_limit_bytes=62 * 2**20
         ),
         name="experts",
-    )(parcel, upstream, gate, lift_w, down)
+    )(parcel, upstream, gate, lift_w, down, context, cut)
 
 
 def stack_heads(target, source, group):
@@ -1085,7 +748,7 @@
 
 
 def attend_kernel(
-    planes, group, q_ref, x_ref, context_ref, all_ref, log_ref, qs, top, total, acc, ssem, rsem, lsem
+    planes, group, q_ref, x_ref, context_ref, all_ref, log_ref, qs, top, total, acc, ssem, rsem
 ):
     me = Spot()
     f32, bf16 = jnp.float32, jnp.bfloat16
@@ -1133,22 +796,25 @@
         acc[item] = acc[item] * shrink + over(terms.astype(bf16), values, NN)
         return sa
 
-    local = pltpu.make_async_copy(x_ref, all_ref.at[own], lsem)
-    local.start()
     me.greet(planes, True, True, False)
     relay(me.a, True, True)
+    all_ref[own] = x_ref[...]
+
+    @pl.when(me.a > 0)
+    def _():
+        relay(me.a - 1, True, False)
+
     stack_heads(qs, q_ref, group)
     top[...] = jnp.full(top.shape, far_below, f32)
     total[...] = jnp.zeros_like(total)
     acc[...] = jnp.zeros_like(acc)
-    local.wait()
 
     def step(i, c):
         sa = me.a - i
 
-        @pl.when(sa > 0)
-        def _():
-            relay(sa - 1, True, False)
+        @pl.when(sa > 1)
+        def _():
+            relay(sa - 2, True, False)
 
         for sb in (me.b, 1 - me.b):
             carry(me.index(sa, sb, 1 - me.c), 2).wait_recv()
@@ -1191,7 +857,6 @@
             pltpu.VMEM(state, f32),
             pltpu.SemaphoreType.DMA((count, 4)),
             pltpu.SemaphoreType.DMA((count,)),
-            pltpu.SemaphoreType.DMA,
         ],
         compiler_params=pltpu.CompilerParams(collective_id=cid, has_side_effects=True, vmem_limit_bytes=ROOM),
         name="attend",
@@ -1207,10 +872,12 @@
     all_ref,
     log_ref,
     cut_ref,
+    column_ref,
     query_grad,
     pair_grad,
-    plane_o,
-    plane_cut,
+    mixing_ref,
+    cut_all,
+    column,
     qs,
     gs,
     delta,
@@ -1230,41 +897,29 @@
     items, rows, size = qs.shape
     keys = all_ref.shape[2] // (2 * size)
     factor = size ** (-0.5)
-    place = lax.rem(me.e, 4)
-    base = me.e - place
-
-    def spot(b, c):
-        return me.index(0, b, c)
-
-    near = [(1 - me.b, me.c), (me.b, 1 - me.c), (1 - me.b, 1 - me.c)]
-    keep = [
-        pltpu.make_async_copy(o_ref, plane_o.at[place], lsem.at[0]),
-        pltpu.make_async_copy(cut_ref.at[place], plane_cut.at[place], lsem.at[1]),
-    ]
-    for k in keep:
-        k.start()
-    barrier = pltpu.get_barrier_semaphore()
-    for b, c in near:
-        pl.semaphore_signal(barrier, inc=1, device_id=(base + spot(b, c), me.t), device_id_type=MESH)
-    up, down = me.a + 1 < planes, me.a > 0
-
-    @pl.when(up)
-    def _():
-        pl.semaphore_signal(barrier, inc=1, device_id=me.at(me.a + 1, me.b, me.c), device_id_type=MESH)
-
-    @pl.when(down)
-    def _():
-        pl.semaphore_signal(barrier, inc=1, device_id=me.at(me.a - 1, me.b, me.c), device_id_type=MESH)
-
-    pl.semaphore_wait(barrier, 3 + up.astype(jnp.int32) + down.astype(jnp.int32))
-    parts = [
-        push(cut_ref.at[spot(*near[i])], plane_cut.at[place], psend.at[3 + i], precv.at[3 + i], (base + spot(*near[i]), me.t))
-        for i in range(3)
-    ]
-    whole = [push(o_ref, plane_o.at[place], psend.at[i], precv.at[i], (base + spot(*near[i]), me.t)) for i in range(2)]
-    for k in parts + whole:
-        k.start()
-
+    me.greet(planes, False, True, False, True)
+
+    def cut_to(k):
+        far = lax.rem(me.a + k, planes)
+        return push(cut_ref.at[far], cut_all.at[me.a], psend.at[k], precv.at[me.a], me.at(far, me.b, me.c))
+
+    def cut_from(k):
+        far = lax.rem(me.a + k, planes)
+        there = cut_all.at[far]
+        push(there, there, psend.at[k], precv.at[far], me.at(far, me.b, me.c)).wait_recv()
+
+    for k in range(1, planes):
+        cut_to(k).start()
+    keep = pltpu.make_async_copy(cut_ref.at[me.a], cut_all.at[me.a], lsem.at[0])
+    keep.start()
+
+    def column_in(k):
+        far = lax.rem(me.a + k, planes)
+        return pltpu.make_async_copy(column_ref.at[far], column.at[far], lsem.at[k])
+
+    for k in range(1, planes):
+        column_in(k).start()
+    column[me.a] = o_ref[...]
     stack_heads(qs, q_ref, group)
     stack_heads(gs, g_ref, group)
     stack_heads(qacc, o_ref, group)
@@ -1305,7 +960,7 @@
 
     def send_a(sa):
         src = mine.at[me.index(sa, me.b, me.c)]
-        return push(src, landa.at[sa], ssem.at[2, sa], rsem.at[2, sa], me.at(me.a - 1, me.b, me.c))
+        return push(src, landa.at[me.a], ssem.at[2, sa], rsem.at[2, me.a], me.at(sa, me.b, me.c))
 
     def from_c(sa):
         for sb in (1 - me.b, me.b):
@@ -1316,42 +971,44 @@
             if sb is not me.b:
                 send_b(sa).start()
 
+    def from_b(sa):
+        push(landb.at[sa], landb.at[sa], ssem.at[1, sa], rsem.at[1, sa], me.at(me.a, 1 - me.b, me.c)).wait_recv()
+        idx = me.index(sa, me.b, me.c)
+        return mine.at[idx], [mine.at[idx], landb.at[sa]]
+
     def along(sa):
-        idx = me.index(sa, me.b, me.c)
-        push(landb.at[sa], landb.at[sa], ssem.at[1, sa], rsem.at[1, sa], me.at(me.a, 1 - me.b, me.c)).wait_recv()
-
-        def finish(target):
-            @pl.when(me.a + 1 < planes)
-            def _():
-                push(landa.at[sa], landa.at[sa], ssem.at[2, sa], rsem.at[2, sa], me.at(me.a, me.b, me.c)).wait_recv()
-                add_rows(target, [mine.at[idx], landb.at[sa], landa.at[sa]])
-
-            @pl.when(me.a + 1 == planes)
-            def _():
-                add_rows(target, [mine.at[idx], landb.at[sa]])
-
-        @pl.when(sa < me.a)
-        def _():
-            finish(mine.at[idx])
-            send_a(sa).start()
-
-        @pl.when(sa == me.a)
-        def _():
-            finish(pair_grad)
-
-    source = spot(*near[0])
-    relay = push(plane_o.at[source], plane_o.at[source], psend.at[2], precv.at[2], (base + spot(*near[1]), me.t))
+        target, parts = from_b(sa)
+        add_rows(target, parts)
+        send_a(sa).start()
+
+    def finish():
+        target, parts = from_b(me.a)
+        add_rows(pair_grad, parts)
+        for far in range(1, planes):
+
+            @pl.when(far > me.a)
+            def _(far=far):
+                push(landa.at[far], landa.at[far], ssem.at[2, far], rsem.at[2, far], me.at(far, me.b, me.c)).wait_recv()
+                add_rows(pair_grad, [pair_grad, landa.at[far]])
+
+    def mix():
+        share = mixing_ref.shape[1]
+        keep.wait()
+        for k in range(1, planes):
+            cut_from(k)
+            column_in(k).wait()
+        tokens = column.shape[0] * column.shape[1]
+        for n in range(0, column.shape[2], 512):
+            rows = column[:, :, n : n + 512].reshape(tokens, 512)
+            part = over(cut_all[...].reshape(tokens, 4 * share), rows, TN).astype(bf16)
+            for q in range(4):
+                mixing_ref[q, :, n : n + 512] = part[q * share : (q + 1) * share]
 
     def step(sa, c):
         lax.fori_loop(0, items, block, sa)
         for sb in (1 - me.b, me.b):
             send_c(sa, sb).start()
 
-        @pl.when(sa == 0)
-        def _():
-            whole[0].wait_recv()
-            relay.start()
-
         @pl.when(sa >= 1)
         def _():
             from_c(sa - 1)
@@ -1365,13 +1022,14 @@
     lax.fori_loop(0, me.a + 1, step, 0)
     for item in range(items):
         spread_heads(query_grad, item, qacc[item] * factor, group, keys)
+    mix()
     from_c(me.a)
 
     @pl.when(me.a > 0)
     def _():
         along(me.a - 1)
 
-    along(me.a)
+    finish()
 
     def settle(sa, c):
         for sb in (1 - me.b, me.b):
@@ -1385,21 +1043,17 @@
         return c
 
     lax.fori_loop(0, me.a + 1, settle, 0)
-    whole[0].wait_send()
-    whole[1].wait()
-    for k in parts:
-        k.wait()
-    relay.wait()
-    for k in keep:
-        k.wait()
-
-
-def attend_back(query, grads, context, pairs_all, logs, cut, planes, group, size, cid):
+    for k in range(1, planes):
+        cut_to(k).wait_send()
+
+
+def attend_back(query, grads, context, pairs_all, logs, cut, column, planes, group, size, cid):
     f32, bf16 = jnp.float32, jnp.bfloat16
     tokens, width = query.shape
     items = logs.shape[0]
     state = logs.shape
     block = pairs_all.shape[1:]
+    share = cut.shape[2] // 4
     inside = pl.BlockSpec(memory_space=pltpu.VMEM)
     anywhere = pl.BlockSpec(memory_space=pl.ANY)
     return pl.pallas_call(
@@ -1407,12 +1061,13 @@
         out_shape=[
             jax.ShapeDtypeStruct((tokens, width), f32),
             jax.ShapeDtypeStruct(block, f32),
-            jax.ShapeDtypeStruct((4,) + context.shape, bf16),
-            jax.ShapeDtypeStruct(cut.shape, bf16),
+            jax.ShapeDtypeStruct((4, share, width), bf16),
         ],
-        in_specs=[inside] * 5 + [anywhere],
-        out_specs=[inside, inside, anywhere, anywhere],
+        in_specs=[inside] * 5 + [anywhere] * 2,
+        out_specs=[inside] * 3,
         scratch_shapes=[
+            pltpu.VMEM(cut.shape, bf16),
+            pltpu.VMEM(column.shape, bf16),
             pltpu.VMEM(state, bf16),
             pltpu.VMEM(state, bf16),
             pltpu.VMEM(state, f32),
@@ -1423,13 +1078,350 @@
             pltpu.VMEM((planes,) + block, bf16),
             pltpu.SemaphoreType.DMA((3, 2 * planes)),
             pltpu.SemaphoreType.DMA((3, 2 * planes)),
-            pltpu.SemaphoreType.DMA((6,)),
-            pltpu.SemaphoreType.DMA((6,)),
-            pltpu.SemaphoreType.DMA((2,)),
+            pltpu.SemaphoreType.DMA((planes,)),
+            pltpu.SemaphoreType.DMA((planes,)),
+            pltpu.SemaphoreType.DMA((planes,)),
         ],
         compiler_params=pltpu.CompilerParams(collective_id=cid, has_side_effects=True, vmem_limit_bytes=ROOM),
         name="attend_back",
-    )(query, grads, context, pairs_all, logs, cut)
+    )(query, grads, context, pairs_all, logs, cut, column)
+
+
+def weights_kernel(
+    planes,
+    chunk,
+    low_ref,
+    cut_ref,
+    query_w,
+    key_w,
+    value_w,
+    input_ref,
+    gain_ref,
+    grad_ref,
+    small_ref,
+    mixing_part,
+    rows_ref,
+    input_grad,
+    total_ref,
+    mixing_rows,
+    low_all,
+    mixed,
+    mixc,
+    mixb,
+    weights,
+    sums,
+    landz,
+    normed,
+    normed_other,
+    gains_other,
+    send,
+    land,
+    wload,
+    lsend,
+    lrecv,
+    msend,
+    mrecv,
+    mload,
+    zsend,
+    zrecv,
+    nsend,
+    nrecv,
+    tsend,
+    trecv,
+):
+    me = Spot()
+    f32, bf16 = jnp.float32, jnp.bfloat16
+    tokens, packed = low_ref.shape
+    width = input_ref.shape[1]
+    chunks = packed // chunk
+    assert chunks == 10
+    place = lax.rem(me.e, 4)
+    base = me.e - place
+    share = sums.shape[1] // planes
+
+    def spot(b, c):
+        return me.index(0, b, c)
+
+    near = [(1 - me.b, me.c), (me.b, 1 - me.c), (1 - me.b, 1 - me.c)]
+    peers = [(base + spot(b, c), me.t) for b, c in near]
+    barrier = pltpu.get_barrier_semaphore()
+    for who in peers + [me.core()] + [me.at(lax.rem(me.a + k, planes), me.b, me.c) for k in range(1, planes)]:
+        pl.semaphore_signal(barrier, inc=1, device_id=who, device_id_type=MESH)
+    pl.semaphore_wait(barrier, 3 + planes)
+
+    def cols(k):
+        return pl.ds(pl.multiple_of(k * chunk, chunk), chunk)
+
+    def whole(i, k):
+        return push(low_ref.at[:, cols(k)], low_all.at[place, :, cols(k)], lsend.at[i, k], lrecv.at[i, k], peers[i])
+
+    first = spot(*near[0])
+
+    def relay(k):
+        there = low_all.at[first, :, cols(k)]
+        return push(there, there, lsend.at[2, k], lrecv.at[2, k], peers[1])
+
+    quarters = [spot(b, c) for b, c in ((1 - me.b, 1 - me.c), (me.b, 1 - me.c), (1 - me.b, me.c), (me.b, me.c))]
+
+    def mix_c(i):
+        return push(mixing_part.at[quarters[i]], mixc.at[i], msend.at[i], mrecv.at[i], peers[1])
+
+    def mix_b():
+        return push(mixed.at[0], mixb, msend.at[2], mrecv.at[2], peers[0])
+
+    mix_loads = [pltpu.make_async_copy(mixing_part.at[quarters[2 + i]], mixed.at[i], mload.at[i]) for i in range(2)]
+
+    def mix_round(k):
+        if k == chunks - 2:
+            for i in range(2):
+                mix_c(i).start()
+        if k == chunks:
+            for i in range(2):
+                mix_loads[i].wait()
+                mix_c(i).wait_recv()
+                add_rows(mixed.at[i], [mixed.at[i], mixc.at[i]])
+                if i == 0:
+                    mix_b().start()
+        if k == chunks + 1:
+            mix_b().wait_recv()
+            add_rows(mixing_rows, [mixed.at[1], mixb])
+
+    def send_low(k, c):
+        whole(0, k).start()
+        return c
+
+    lax.fori_loop(0, chunks, send_low, 0)
+    whole(1, 0).start()
+    whole(1, 1).start()
+    for k in mix_loads:
+        k.start()
+    query_width, key_width = query_w.shape[1], key_w.shape[1]
+    loads = [
+        pltpu.make_async_copy(query_w, weights.at[:, :query_width], wload.at[0]),
+        pltpu.make_async_copy(key_w, weights.at[:, query_width : query_width + key_width], wload.at[1]),
+        pltpu.make_async_copy(value_w, weights.at[:, query_width + key_width :], wload.at[2]),
+    ]
+    for k in loads:
+        k.start()
+    gains = push(small_ref.at[pl.ds(0, 8)], gains_other, nsend.at[4], nrecv.at[4], me.core())
+    gains.start()
+    low_all[place] = low_ref[...]
+    quarter = width // 4
+
+    def trade(n):
+        at = pl.ds(pl.multiple_of(n * quarter, quarter), quarter)
+        return push(normed.at[:, at], normed_other.at[:, at], nsend.at[n], nrecv.at[n], me.core())
+
+    def normed_cols(n, c):
+        at = pl.ds(pl.multiple_of(n * quarter, quarter), quarter)
+        normed[:, at] = over(low_ref[...], weights[at, :], NT).astype(bf16)
+        trade(n).start()
+        return c
+
+    def await_trade(n, c):
+        trade(n).wait_recv()
+        return c
+
+
+    def input_rows(r, total):
+        at = pl.ds(pl.multiple_of(r * 16, 16), 16)
+        grads = normed[at, :].astype(f32) + normed_other[at, :].astype(f32)
+        inputs = input_ref[at, :].astype(f32)
+        scale = lax.rsqrt(jnp.mean(inputs * inputs, axis=1, keepdims=True) + epsilon)
+        scaled = gain_ref[...] * grads
+        level = jnp.mean(scaled * inputs, axis=1, keepdims=True)
+        input_grad[at, :] = grad_ref[at, :] + scale * scaled - inputs * (scale * scale * scale * level)
+        return total + jnp.sum(grads * inputs * scale, axis=0, keepdims=True)
+
+    def norm_round(k):
+        if k == 0:
+            for copy in loads:
+                copy.wait()
+        if k < 4:
+            lax.fori_loop(k, k + 1, normed_cols, 0)
+        if k == 4:
+            gains.wait()
+            total_ref[...] = small_ref[...]
+            total_ref[0:8, :] += gains_other[...]
+            lax.fori_loop(0, 4, await_trade, 0)
+            total_ref[8:9, :] = lax.fori_loop(0, tokens // 16, input_rows, jnp.zeros((1, width), f32))
+            send[0] = total_ref[ours, :]
+
+    half = total_ref.shape[0] // 2
+    ours = pl.ds(pl.multiple_of(me.t * half, half), half)
+    others = pl.ds(pl.multiple_of((1 - me.t) * half, half), half)
+    bits = [1, 2, 4, 8]
+
+    def small(j):
+        bit = bits[j]
+        who = (me.e + bit * (1 - 2 * lax.rem(lax.div(me.e, bit), 2)), me.t)
+        return push(send.at[j], land.at[j], tsend.at[j], trecv.at[j], who)
+
+    share_back = push(send.at[4], land.at[4], tsend.at[4], trecv.at[4], me.core())
+
+    def small_round(j):
+        if j > 0:
+            small(j - 1).wait_recv()
+            if j < 4:
+                send[j] = send[j - 1] + land[j - 1]
+            else:
+                send[4] = send[3] + land[3]
+                share_back.start()
+        if j < 4:
+            small(j).start()
+
+
+    def block(k, d):
+        return sums.at[k, pl.ds(pl.multiple_of(d * share, share), share)]
+
+    def along(k, d, up):
+        arrive = me.a + 1 if up else me.a - 1
+        slot = d if up else jnp.where(d == arrive, planes, d)
+        return push(block(k, d), landz.at[k, slot], zsend.at[k, d], zrecv.at[k, slot], me.at(arrive, me.b, me.c))
+
+    def landed(k, slot):
+        push(landz.at[k, slot], landz.at[k, slot], zsend.at[k, 0], zrecv.at[k, slot], me.core()).wait_recv()
+
+    def chain(k, act, ends):
+        for i in range(planes - 1):
+            d = far_first(me.a, planes, i)
+            up = d > me.a
+            inner = (up & (me.a > 0)) | (jnp.logical_not(up) & (me.a + 1 < planes))
+
+            @pl.when(jnp.logical_not(inner) if ends else inner)
+            def _(d=d, up=up):
+                if act and not ends:
+                    landed(k, d)
+                    add_rows(block(k, d), [block(k, d), landz.at[k, d]])
+
+                @pl.when(up)
+                def _():
+                    along(k, d, True).start() if act else along(k, d, True).wait_send()
+
+                @pl.when(jnp.logical_not(up))
+                def _():
+                    along(k, d, False).start() if act else along(k, d, False).wait_send()
+
+    def finish(k):
+        target = rows_ref.at[:, cols(k)]
+        own = block(k, me.a)
+
+        @pl.when(me.a > 0)
+        def _():
+            landed(k, me.a)
+
+        @pl.when(me.a + 1 < planes)
+        def _():
+            landed(k, planes)
+
+        @pl.when((me.a > 0) & (me.a + 1 < planes))
+        def _():
+            add_rows(target, [own, landz.at[k, me.a], landz.at[k, planes]])
+
+        @pl.when(me.a == 0)
+        def _():
+            add_rows(target, [own, landz.at[k, planes]])
+
+        @pl.when(me.a + 1 == planes)
+        def _():
+            add_rows(target, [own, landz.at[k, me.a]])
+
+    def forward(k):
+        whole(0, k).wait_recv()
+        relay(k).start()
+        if k + 2 < chunks:
+            whole(1, k + 2).start()
+
+    for k in range(chunks + 2):
+        if k < chunks:
+            if k == 0:
+                forward(0)
+            if k + 1 < chunks:
+                forward(k + 1)
+            whole(1, k).wait_recv()
+            relay(k).wait_recv()
+            mixed_rows = low_all[:, :, k * chunk : (k + 1) * chunk].reshape(4 * tokens, chunk)
+            sums[k] = over(cut_ref[...], mixed_rows, NN).astype(bf16)
+            chain(k, True, True)
+        norm_round(k)
+        if k in (4, 6, 8, 10, 11):
+            small_round((4, 6, 8, 10, 11).index(k))
+        if 1 <= k <= chunks:
+            chain(k - 1, True, False)
+        if k >= 2:
+            finish(k - 2)
+        mix_round(k)
+
+    def settle(k, c):
+        for i in range(2):
+            whole(i, k).wait_send()
+        relay(k).wait_send()
+        chain(k, False, True)
+        chain(k, False, False)
+        return c
+
+    lax.fori_loop(0, chunks, settle, 0)
+    for k in (mix_c(0), mix_c(1), mix_b()):
+        k.wait_send()
+    for n in range(4):
+        trade(n).wait_send()
+        small(n).wait_send()
+    share_back.wait_send()
+    share_back.wait_recv()
+    total_ref[ours, :] = send[4]
+    total_ref[others, :] = land[4]
+
+
+def weight_grads(low, cut, query_w, key_w, value_w, inputs, gain, residual_grad, small, mixing, planes, cid):
+    f32, bf16 = jnp.float32, jnp.bfloat16
+    tokens, packed = low.shape
+    width = inputs.shape[1]
+    chunk = 256
+    chunks = packed // chunk
+    share = cut.shape[0] // planes
+    quarter = mixing.shape[1:]
+    inside = pl.BlockSpec(memory_space=pltpu.VMEM)
+    anywhere = pl.BlockSpec(memory_space=pl.ANY)
+    half = (small.shape[0] // 2, small.shape[1])
+    return pl.pallas_call(
+        functools.partial(weights_kernel, planes, chunk),
+        out_shape=[
+            jax.ShapeDtypeStruct((share, packed), f32),
+            jax.ShapeDtypeStruct((tokens, width), f32),
+            jax.ShapeDtypeStruct(small.shape, f32),
+            jax.ShapeDtypeStruct(quarter, f32),
+        ],
+        in_specs=[inside, inside, anywhere, anywhere, anywhere, inside, inside, inside, inside, anywhere],
+        out_specs=[inside] * 4,
+        scratch_shapes=[
+            pltpu.VMEM((4, tokens, packed), bf16),
+            pltpu.VMEM((2,) + quarter, bf16),
+            pltpu.VMEM((2,) + quarter, bf16),
+            pltpu.VMEM(quarter, bf16),
+            pltpu.VMEM((width, packed), bf16),
+            pltpu.VMEM((chunks, planes * share, chunk), bf16),
+            pltpu.VMEM((chunks, planes + 1, share, chunk), bf16),
+            pltpu.VMEM((tokens, width), bf16),
+            pltpu.VMEM((tokens, width), bf16),
+            pltpu.VMEM((8, width), f32),
+            pltpu.VMEM((5,) + half, f32),
+            pltpu.VMEM((5,) + half, f32),
+            pltpu.SemaphoreType.DMA((3,)),
+            pltpu.SemaphoreType.DMA((3, chunks)),
+            pltpu.SemaphoreType.DMA((3, chunks)),
+            pltpu.SemaphoreType.DMA((3,)),
+            pltpu.SemaphoreType.DMA((3,)),
+            pltpu.SemaphoreType.DMA((2,)),
+            pltpu.SemaphoreType.DMA((chunks, planes)),
+            pltpu.SemaphoreType.DMA((chunks, planes + 1)),
+            pltpu.SemaphoreType.DMA((5,)),
+            pltpu.SemaphoreType.DMA((5,)),
+            pltpu.SemaphoreType.DMA((5,)),
+            pltpu.SemaphoreType.DMA((5,)),
+        ],
+        compiler_params=pltpu.CompilerParams(collective_id=cid, has_side_effects=True, vmem_limit_bytes=ROOM),
+        name="weight_grads",
+    )(low, cut, query_w, key_w, value_w, inputs, gain, residual_grad, small, mixing)
 
 
 epsilon = 1e-06
@@ -1866,8 +1858,7 @@
     share_width = model_width // expert_count
     f32, bf16 = jnp.float32, jnp.bfloat16
     inputs = layer_input.astype(f32)
-    normed_f, first_back = jax.vjp(rms_scaled, inputs, norm_first)
-    normed = normed_f.astype(bf16)
+    normed = rms_scaled(inputs, norm_first).astype(bf16)
     positions = expert_idx * seg_len + jnp.arange(seg_len, dtype=jnp.int32)
     cosine, sine_table = rotary_tables(positions, head_dim)
     cosine = cosine[:, None, :]
@@ -1875,6 +1866,10 @@
 
     def rope_norm(raw_heads, gain_vec):
         return rotate(rms_scaled(raw_heads, gain_vec), cosine, sine_table)
+
+    def slices(rows):
+        cut = rows.reshape(token_count, planes, 4, share_width)
+        return cut.transpose(2, 0, 1, 3).reshape(4, token_count, planes * share_width)
 
     query_raw = jnp.dot(normed, query_weight, preferred_element_type=f32).reshape(
         seq_count, seg_len, local_queries, head_dim
@@ -1913,9 +1908,13 @@
     slot_hi = lift(slot_table, 2 * expert_count)[:, :expert_count]
     notes = jnp.concatenate([slot_hi, lift(gate_table, 128 - expert_count)], axis=1)
     parcel = jnp.concatenate([second, notes], axis=1)
-    _, _, out_share, row_home, gate_grad, up_grad, down_grad = run_experts(
-        parcel, upstream_mine, gate_weight[0], up_weight[0], down_weight[0], planes, slots, 4
-    )
+    normed_cut = slices(normed.reshape(token_count, model_width))
+    _, _, out_share, row_home, context_column, other_cuts, gate_grad, up_grad, down_grad = run_experts(
+        parcel, upstream_mine, gate_weight[0], up_weight[0], down_weight[0], context, normed_cut, planes, slots, 4
+    )
+    place = lax.rem(expert_idx, 4)
+    own_cut = lax.dynamic_index_in_dim(normed_cut, place, 0)
+    normed_cut = lax.dynamic_update_slice_in_dim(other_cuts, own_cut, place, 0)
     out_home = lax.psum_scatter(out_share, "expert", scatter_dimension=0, tiled=True)[0]
     residual_half = lax.dynamic_slice_in_dim(residual, tensor_idx * half_width, half_width, 1)
     layer_output = (residual_half + out_home.astype(f32)).astype(bf16).reshape(seq_count, seg_len, half_width)
@@ -1934,20 +1933,23 @@
     residual_grad = residual_part + upstream_low.astype(f32)
     head_in = residual_grad.astype(bf16)
 
-    def slices(rows):
-        cut = rows.reshape(token_count, planes, 4, share_width)
-        return cut.transpose(2, 0, 1, 3).reshape(4, token_count, planes * share_width)
-
     context_grad = lax.dot_general(
         head_in, mixing_weight, (((1,), (1,)), ((), ())), preferred_element_type=f32
     ).astype(bf16)
-    query_rot_grad, pair_home, context_plane, head_plane = attend_back(
-        query_rows, context_grad, context, pairs_all, logs, slices(head_in), planes, group_size, head_dim, 7
-    )
-    mixing_part = jnp.einsum("gtd,gtc->dc", head_plane, context_plane, preferred_element_type=f32)
-    mixing_part = mixing_part.astype(bf16).reshape(planes, share_width, local_queries * head_dim)
-    mixing_rows = scatter_sum(mixing_part, planes, False, False, f32, 8, "scatter_mixing")
-    mixing_grad = mixing_rows.T
+    head_cut = head_in.reshape(token_count, planes, 4 * share_width).transpose(1, 0, 2)
+    query_rot_grad, pair_home, mixing_part = attend_back(
+        query_rows,
+        context_grad,
+        context,
+        pairs_all,
+        logs,
+        head_cut,
+        context_column,
+        planes,
+        group_size,
+        head_dim,
+        7,
+    )
     key_raw_grad, keygain_part = key_back(
         pair_home[:, :key_width].reshape(seq_count, seg_len, local_keys, head_dim)
     )
@@ -1958,54 +1960,42 @@
     key_low = key_raw_grad.astype(bf16).reshape(token_count, key_width)
     value_low = pair_home[:, key_width:].astype(bf16)
     all_low = jnp.concatenate([query_low, key_low, value_low], axis=1)
-    flat_normed = normed.reshape(token_count, model_width)
-    low_plane, normed_plane = plane_exchange(all_low, slices(flat_normed), 10, "plane_queries")
-    weight_part = jnp.einsum("gtd,gtc->dc", normed_plane, low_plane, preferred_element_type=f32)
-    weight_part = weight_part.astype(bf16).reshape(planes, share_width, all_low.shape[1])
-    weight_rows = scatter_sum(weight_part, planes, False, False, f32, 11, "scatter_queries")
+    gain_row = jnp.pad(
+        jnp.concatenate([querygain_part, keygain_part])[None], ((0, 7), (0, model_width - 2 * head_dim))
+    )
+    small = jnp.concatenate(
+        [gain_row, jnp.pad(second_grad[None], ((1, 6), (0, 0))), router_grad], axis=0
+    )
+    weight_rows, input_grad, small, mixing_rows = weight_grads(
+        all_low,
+        normed_cut.reshape(4 * token_count, planes * share_width).T,
+        query_weight,
+        key_weight,
+        value_weight,
+        layer_input.reshape(token_count, model_width),
+        norm_first[None],
+        residual_grad,
+        small,
+        mixing_part,
+        planes,
+        10,
+    )
+    mixing_grad = mixing_rows.T
     query_width = local_queries * head_dim
     query_grad = weight_rows[:, :query_width]
     key_grad = weight_rows[:, query_width : query_width + key_width]
     value_grad = weight_rows[:, query_width + key_width :]
-    normed_part = lax.dot_general(
-        query_low, query_weight, (((1,), (1,)), ((), ())), preferred_element_type=f32
-    )
-    normed_part = normed_part + lax.dot_general(
-        key_low, key_weight, (((1,), (1,)), ((), ())), preferred_element_type=f32
-    )
-    normed_part = normed_part + lax.dot_general(
-        value_low, value_weight, (((1,), (1,)), ((), ())), preferred_element_type=f32
-    )
-    gain_row = jnp.pad(
-        jnp.concatenate([querygain_part, keygain_part])[None], ((0, 15), (0, model_width - 2 * head_dim))
-    )
-    normed_low = jnp.concatenate([normed_part, gain_row], axis=0).astype(bf16)
-    normed_sum = normed_low.astype(f32) + swap_cores(normed_low, 12, "swap_normed").astype(f32)
-    normed_grad = normed_sum[:token_count].reshape(seq_count, seg_len, model_width)
-    input_part, first_grad = first_back(normed_grad)
-    input_grad = residual_grad.reshape(seq_count, seg_len, model_width) + input_part
-    small = jnp.concatenate(
-        [
-            first_grad[None],
-            second_grad[None],
-            normed_sum[token_count : token_count + 1],
-            jnp.zeros((13, model_width), f32),
-            router_grad,
-        ],
-        axis=0,
-    )
-    small = total_over(small, expert_count, 13, "total_small")
     return (
         layer_output,
-        input_grad,
-        small[0],
+        input_grad.reshape(seq_count, seg_len, model_width),
+        small[8],
         query_grad,
         key_grad,
         value_grad,
         mixing_grad,
-        small[2, :head_dim],
-        small[2, head_dim : 2 * head_dim],
-        small[1],
+        small[0, :head_dim],
+        small[0, head_dim : 2 * head_dim],
+        small[9],
         small[16:].T,
         gate_grad[None],
         up_grad[None],

time: 662 us -> 525 us (0.79)
  Pallas kernels: 471 us -> 377 us
  matrix products: 38.6 us -> 21 us
  local copies, waits for them, and re-layouts: 56.7 us -> 44.1 us
  other arithmetic: 32.8 us -> 20.7 us
    pallas_call x4 -> x1, Pallas kernels: 158 us -> 103 us  [weight_grads(): pl.pallas_call(functools.partial(weights_kernel, planes, chunk), out_shap...]
    pallas_call x1, Pallas kernels: 185 us -> 156 us  [run_experts(): pl.pallas_call(functools.partial(experts_kernel, planes), out_shape=[jax....]
    dot_general x5 -> x0, matrix products: 16.8 us -> none  [the longest x1 6.5 us: on_chips(): lax.dot_general(query_low, query_weight, (((1,), (1,)), ((), ())), prefer...]
    unnamed x133 -> x100, local copies, waits for them, and re-layouts: 24.6 us -> 22.9 us
  transfers between devices with their start and end apart: 2 -> 2, of which waited for: 1 -> 1; matrix products, arithmetic and copies ran while one was open for 17% -> 13% of each run, Pallas kernels for 44% -> 43%
where the time goes in v2:
time: 525 us; the launch traced here: 517 us
  Pallas kernels  377 us (72%)
  local copies, waits for them, and re-layouts  44.1 us (8%)
  waiting for transfers between devices  38.7 us (7%)
  matrix products  21 us (4%)
  other arithmetic  20.7 us (4%)
  between operations  15 us (3%)
    pallas_call x1, Pallas kernels, run_experts(): pl.pallas_call(functools.partial(experts_kernel, planes), out_shape=[jax....  156 us
    pallas_call x1, Pallas kernels, weight_grads(): pl.pallas_call(functools.partial(weights_kernel, planes, chunk), out_shap...  103 us
    pallas_call x1, Pallas kernels, attend_back(): pl.pallas_call(functools.partial(attend_back_kernel, planes, group), out_...  80.6 us
    all_gather x1, waiting for transfers between devices, on_chips(): upstream_mine = lax.all_gather(upstream_half, 'expert')  38.7 us
    pallas_call x1, Pallas kernels, attend(): pl.pallas_call(functools.partial(attend_kernel, planes, group), out_shape...  33.8 us
    unnamed x100, local copies, waits for them, and re-layouts  22.9 us
  transfers between devices with their start and end apart: 2, of which 1 were waited for; matrix products, arithmetic and copies ran while one was open for 13% of the time, Pallas kernels for 43%

profile of v2, /device:TPU:8, one launch (start us, length us, event | category | flops | bytes accessed | tf_op | source)
XLA Modules:
  0.0 516.8 jit_solution(3189153069505309997)
XLA Ops:
  7.3 1.8 constant_dynamic-slice_fusion
  17.7 5.3 %fusion = f32[3,64,2048]{2,1,0:T(8,128)S(1)} fusion(bf16[3,64,2048]{2,1,0:T(8,128)(2,1)S(1)} %multiply_convert_fusion.1, bf16[2048,2048]{1,0:T(8,128)(2,1)} %query_w.1), kind=kOutput, calls=%fused_computation | convolution fusion | flops 1610612736 | bytes 10747904 | tf_op jit(solution)/shard_map/dot_general | solution.py:1874
  28.6 33.8 %attend.1 = (bf16[192,2048]{1,0:T(8,128)(2,1)}, bf16[16,192,512]{2,1,0:T(8,128)(2,1)}, f32[6,512,128]{2,1,0:T(8,128)}) custom-call(bf16[192,2048]{1,0:T(8,128)(2,1)} %bitcast.122, bf16[192,512]{1,0:T(8,128)(2,1)} %pad_maximum_fusion.2.x_ref), custom_call_target="tpu_custom_call" | custom-call | tf_op jit(solution)/shard_map/attend/pallas_call | solution.py:844
  62.5 6.3 %convolution_convert_fusion.1.x_ref = bf16[192,2048]{1,0:T(8,128)(2,1)} fusion(bf16[192,2048]{1,0:T(8,128)(2,1)} %get-tuple-element.31.context_ref.o_ref, bf16[2048,2048]{1,0:T(8,128)(2,1)} %param.21), kind=kOutput, calls=%fused_computation.4 | convolution fusion | flops 1611005952 | bytes 9961472 | tf_op jit(solution)/shard_map/dot_general | solution.py:1891
  68.8 3.0 swap_heads.1
  71.9 1.5 bitcast_add_fusion
  77.1 38.7 %all-gather.3.cloned.1.call-done = bf16[1536,2048]{1,0:T(8,128)(2,1)} async-done(((bf16[96,2048]{1,0:T(8,128)(2,1)}), bf16[1536,2048]{1,0:T(8,128)(2,1)}) %all-gather.3.cloned.1.call-update) | async-done | bytes 6291472 | tf_op jit(solution)/shard_map/all_gather | solution.py:1888
  115.8 156.4 %experts.1 = (bf16[16,192,2176]{2,1,0:T(8,128)(2,1)}, bf16[16,96,2048]{2,1,0:T(8,128)(2,1)}, bf16[16,192,1024]{2,1,0:T(8,128)(2,1)}, bf16[2,192,1152]{2,1,0:T(8,...) custom-call(bf16[192,2176]{1,0:T(8,128)(2,1)} %concatenate.36.parcel, ...), custom_call_target="tpu_custom_call" | custom-call | tf_op jit(solution)/shard_map/experts/pallas_call | solution.py:651
  274.9 1.7 fusion.31
  277.5 7.2 %convolution_convert_fusion.g_ref = bf16[192,2048]{1,0:T(8,128)(2,1)} fusion(bf16[192,2048]{1,0:T(8,128)(2,1)S(1)} %get-tuple-element.154, bf16[2048,2048]{1,0:T(8,128)(2,1)} %param.21), kind=kOutput, calls=%fused_computation.3 | convolution fusion | flops 1611005952 | bytes 9961472 | tf_op jit(solution)/shard_map/dot_general | solution.py:1936
  284.7 80.6 %attend_back.1 = (f32[192,2048]{1,0:T(8,128)}, f32[192,512]{1,0:T(8,128)}, bf16[4,128,2048]{2,1,0:T(8,128)(2,1)}) custom-call(bf16[192,2048]{1,0:T(8,128)(2,1)} %bitcast.123, bf16[192,2048]{1,0:T(8,128)(2,1)} %convolution_convert_fusion.g_ref, bf16[192,2048]{1,0:T(8,128)(2,1)} %get-tuple-element.31.context_ref.o_ref, ...), custom_call_target="tpu_custom_call" | custom-call | tf_op jit(solution)/shard_map/attend_back/pallas_call | solution.py:1059
  365.3 1.7 slice.106
  367.0 1.6 slice.71
  368.6 1.6 dynamic-slice_dynamic-update-slice_fusion
  370.3 2.3 copy.111
  377.1 2.5 multiply_add_fusion.1
  381.4 2.8 fusion.3
  387.3 103.2 %weight_grads.1 = (f32[128,2560]{1,0:T(8,128)}, f32[192,2048]{1,0:T(8,128)}, f32[32,2048]{1,0:T(8,128)}, f32[128,2048]{1,0:T(8,128)}) custom-call(bf16[192,2560]{1,0:T(8,128)(2,1)} %pad_maximum_fusion.low_ref, bf16[512,768]{1,0:T(8,128)(2,1)} %bitcast.134, bf16[2048,2048]{1,0:T(8,128)(2,1)} %query_w.1, bf16[2048,256]{1,0:T(8,128)(2,1)} %key_w.1, ...), custom_call_target="tpu_custom_call" | custom-call | tf_op jit(solution)/shard_map/weight_grads/pallas_call | solution.py:1386
  490.6 2.6 copy.112
  494.8 1.7 fusion.33
  497.7 1.8 fusion.10
  502.0 1.7 copy.164
  505.1 1.7 copy.165
  508.1 1.7 copy.166
  (176 shorter events, 38.6 us)
Async XLA Ops:
  7.2 67.8 %copy-start = (bf16[2048,16]{0,1:T(8,128)(2,1)S(1)}, bf16[2048,16]{0,1:T(8,128)(2,1)}, u32[]{:S(2)}) copy-start(bf16[2048,16]{0,1:T(8,128)(2,1)} %param.25) | copy-start | bytes 196612
  7.2 4.1 copy-start.8
  7.2 4.4 copy-start.32
  7.2 108.6 %all-gather.3.cloned.1.call-start = ((), (), s32[]{:S(2)}) async-start(), calls=%async_computation.2 | async-start | bytes 6684672 | tf_op jit(solution)/shard_map/all_gather | solution.py:1888
  9.1 488.6 %reduce-scatter.2.cloned.1.call-start = ((), (), s32[]{:S(2)}) async-start(), calls=%async_computation.1 | async-start | bytes 6684672 | tf_op jit(solution)/shard_map/reduce_scatter | solution.py:1918
  12.8 1.8 copy-start.39
  23.3 1.8 copy-start.2
  68.8 3.0 copy-start.9
  68.8 3.0 copy-start.15
  74.9 2.1 copy-start.6
  365.3 7.2 %copy-start.18 = (f32[192,2048]{1,0:T(8,128)S(1)}, f32[192,2048]{1,0:T(8,128)}, u32[]{:S(2)}) copy-start(f32[192,2048]{1,0:T(8,128)} %get-tuple-element.37) | copy-start | bytes 4718596
  372.6 2.5 copy-start.25
  372.6 2.8 copy-start.40
  374.0 2.2 copy-start.34
  377.0 2.5 copy-start.3
  377.1 2.5 copy-start.20
  377.1 2.5 copy-start.42
  379.6 1.7 copy-start.29
  384.2 2.1 copy-start.27
  490.6 2.6 copy-start.21
  494.3 5.3 %copy-start.17 = (f32[192,2048]{1,0:T(8,128)S(1)}, f32[192,2048]{1,0:T(8,128)}, u32[]{:S(2)}) copy-start(f32[192,2048]{1,0:T(8,128)} %get-tuple-element.41) | copy-start | bytes 4718596
  499.6 2.5 copy-start.14
  502.0 3.0 copy-start.13
  505.1 3.0 copy-start.12
  (22 other events, 24.2 us)
Sparse Core Ops, SparseCore 0:
  11.4 104.3 all-gather.2
  272.3 201.2 reduce-scatter.1

commit v3 on v2

--- a/solution.py
+++ b/solution.py
@@ -486,16 +486,17 @@
         row = jnp.where(mark == me.e, high, jnp.where(mark == me.e + count, total - high, 0.0))
         rbuf[:, side:] = row.astype(bf16)
 
-    def store(idx, q):
-        return pltpu.make_async_copy(stage.at[lax.rem(q, 2)], share_ref.at[idx], osem.at[lax.rem(q, 2)])
+    def store(sa, q):
+        sb, sc = side_of(q)
+        there = share_ref.at[sc * 2 * planes + sa * 2 + sb]
+        return pltpu.make_async_copy(stage.at[lax.rem(q, 2)], there, osem.at[lax.rem(q, 2)])
 
     def spread_rows(q, sa):
         at = pl.ds(pl.multiple_of(q * slots, slots), slots)
-        idx = sa * 4 + q
 
         @pl.when((q >= 2) | (sa != near(1)))
         def _():
-            store(idx, q).wait()
+            store(sa, q).wait()
 
         for n in range(0, side, 512):
             cut = slice(n, n + 512)
@@ -514,7 +515,7 @@
             outgoing[slot] = rbuf[at, :]
             send_c(sa, sb).start()
 
-        store(idx, q).start()
+        store(sa, q).start()
         return sa
 
     me.greet(planes, True, True, True, True, True)
@@ -532,6 +533,8 @@
     across(me.a, True)
     for i in range(2, planes):
         relay_a(near(i), True, False)
+        if i == planes - 1:
+            context_pass(0, True)
         relay_b(near(i - 1), True)
     across(near(1), True)
     fetch_rows(near(1))
@@ -564,9 +567,14 @@
         @pl.when(i == 0)
         def _():
             relay_b(near(planes - 1), True)
-            context_pass(0, True)
             for k in range(3):
                 cut_to(k).start()
+
+        for k in range(1, planes):
+
+            @pl.when(i == k - 1)
+            def _(k=k):
+                context_pass(k, True)
 
         @pl.when(i > 0)
         def _():
@@ -591,19 +599,13 @@
         def _():
             along(near(i))
 
-        for k in range(1, planes):
-
-            @pl.when(i == k)
-            def _(k=k):
-                context_pass(k, True)
-
         return c
 
     lax.fori_loop(0, planes, step, 0)
     from_c(me.a)
     finish()
-    store(0, 0).wait()
-    store(0, 1).wait()
+    store(me.a, 0).wait()
+    store(me.a, 1).wait()
     done = push(home_ref.at[me.t], home_ref.at[me.t], esem.at[0], esem.at[1], me.core())
     done.start()
 
@@ -873,9 +875,14 @@
     log_ref,
     cut_ref,
     column_ref,
-    query_grad,
+    query_raw,
+    key_raw,
+    gain_ref,
+    turn_ref,
+    low_ref,
+    gain_grad,
+    mixing_ref,
     pair_grad,
-    mixing_ref,
     cut_all,
     column,
     qs,
@@ -1020,9 +1027,31 @@
         return c
 
     lax.fori_loop(0, me.a + 1, step, 0)
-    for item in range(items):
-        spread_heads(query_grad, item, qacc[item] * factor, group, keys)
     mix()
+
+    def unturned(grads, raw, gain):
+        turned = grads * turn_ref[0] + pltpu.roll(grads, size // 2, 1) * turn_ref[1]
+        scale = lax.rsqrt(jnp.mean(raw * raw, axis=1, keepdims=True) + epsilon)
+        scaled = gain * turned
+        level = jnp.mean(scaled * raw, axis=1, keepdims=True)
+        return scale * scaled - raw * (scale * scale * scale * level), jnp.sum(turned * raw * scale, axis=0, keepdims=True)
+
+    seg = rows // group
+    gain_grad[...] = jnp.zeros_like(gain_grad)
+
+    def query_item(item, c):
+        at = pl.ds(pl.multiple_of(lax.div(item, keys) * seg, seg), seg)
+        total = jnp.zeros((1, size), f32)
+        for h in range(group):
+            cols = pl.ds(pl.multiple_of((lax.rem(item, keys) * group + h) * size, size), size)
+            grads = qacc[item, h * seg : (h + 1) * seg, :] * factor
+            value, part = unturned(grads, query_raw[at, cols], gain_ref[0:1, :])
+            low_ref[at, cols] = value.astype(bf16)
+            total = total + part
+        gain_grad[0:1, :] += total
+        return c
+
+    lax.fori_loop(0, items, query_item, 0)
     from_c(me.a)
 
     @pl.when(me.a > 0)
@@ -1030,6 +1059,15 @@
         along(me.a - 1)
 
     finish()
+    width = query_raw.shape[1]
+    for item in range(items):
+        s, k = item // keys, item % keys
+        at = slice(s * seg, (s + 1) * seg)
+        cols = slice(k * size, (k + 1) * size)
+        value, part = unturned(pair_grad[at, cols], key_raw[at, cols], gain_ref[1:2, :])
+        low_ref[at, width + k * size : width + (k + 1) * size] = value.astype(bf16)
+        gain_grad[1:2, :] += part
+    low_ref[:, width + keys * size :] = pair_grad[:, keys * size :].astype(bf16)
 
     def settle(sa, c):
         for sb in (1 - me.b, me.b):
@@ -1047,7 +1085,7 @@
         cut_to(k).wait_send()
 
 
-def attend_back(query, grads, context, pairs_all, logs, cut, column, planes, group, size, cid):
+def attend_back(query, grads, context, pairs_all, logs, cut, column, raws, gains, turns, planes, group, size, cid):
     f32, bf16 = jnp.float32, jnp.bfloat16
     tokens, width = query.shape
     items = logs.shape[0]
@@ -1059,13 +1097,14 @@
     return pl.pallas_call(
         functools.partial(attend_back_kernel, planes, group),
         out_shape=[
-            jax.ShapeDtypeStruct((tokens, width), f32),
-            jax.ShapeDtypeStruct(block, f32),
+            jax.ShapeDtypeStruct((tokens, width + block[1]), bf16),
+            jax.ShapeDtypeStruct((8, size), f32),
             jax.ShapeDtypeStruct((4, share, width), bf16),
         ],
-        in_specs=[inside] * 5 + [anywhere] * 2,
+        in_specs=[inside] * 5 + [anywhere] * 2 + [inside] * 4,
         out_specs=[inside] * 3,
         scratch_shapes=[
+            pltpu.VMEM(block, f32),
             pltpu.VMEM(cut.shape, bf16),
             pltpu.VMEM(column.shape, bf16),
             pltpu.VMEM(state, bf16),
@@ -1084,7 +1123,7 @@
         ],
         compiler_params=pltpu.CompilerParams(collective_id=cid, has_side_effects=True, vmem_limit_bytes=ROOM),
         name="attend_back",
-    )(query, grads, context, pairs_all, logs, cut, column)
+    )(query, grads, context, pairs_all, logs, cut, column, raws[0], raws[1], gains, turns)
 
 
 def weights_kernel(
@@ -1816,6 +1855,17 @@
         down_grad[None],
     )
 
+def partners(planes):
+    def number(a, b, c, t):
+        y, x = (b, c) if t else (c, b)
+        return (a * 4 + y * 2 + x) * 2 + t
+
+    both = (0, 1)
+    pairs = [[number(a, b, c, t) for c in both] for t in both for a in range(planes) for b in both]
+    groups = [[number(a, b, c, t) for a in range(planes) for b in both] for t in both for c in both]
+    return pairs, groups
+
+
 def lift(values, wide):
     high = lax.reduce_precision(values, 8, 7)
     both = jnp.concatenate([high, values - high], axis=-1).astype(jnp.bfloat16)
@@ -1878,13 +1928,15 @@
         seq_count, seg_len, local_keys, head_dim
     )
     value_local = jnp.dot(normed, value_weight, preferred_element_type=f32).astype(bf16)
-    query_rot, query_back = jax.vjp(rope_norm, query_raw, query_gain)
-    key_rot, key_back = jax.vjp(rope_norm, key_raw, key_gain)
+    query_rot = rope_norm(query_raw, query_gain)
+    key_rot = rope_norm(key_raw, key_gain)
     key_local = key_rot.astype(bf16).reshape(token_count, key_width)
     pairs = jnp.concatenate([key_local, value_local.reshape(token_count, key_width)], axis=1)
     upstream_low = cotangent.reshape(token_count, model_width)
     half_tokens = token_count // 2
     upstream_half = lax.dynamic_slice_in_dim(upstream_low, tensor_idx * half_tokens, half_tokens, 0)
+    axes = ("expert", "tensor")
+    pairs_of, groups_of = partners(planes)
     upstream_mine = lax.all_gather(upstream_half, "expert")
     query_rows = query_rot.astype(bf16).reshape(token_count, local_queries * head_dim)
     context, pairs_all, logs = attend(query_rows, pairs, planes, group_size, head_dim, 1)
@@ -1915,9 +1967,7 @@
     place = lax.rem(expert_idx, 4)
     own_cut = lax.dynamic_index_in_dim(normed_cut, place, 0)
     normed_cut = lax.dynamic_update_slice_in_dim(other_cuts, own_cut, place, 0)
-    out_home = lax.psum_scatter(out_share, "expert", scatter_dimension=0, tiled=True)[0]
-    residual_half = lax.dynamic_slice_in_dim(residual, tensor_idx * half_width, half_width, 1)
-    layer_output = (residual_half + out_home.astype(f32)).astype(bf16).reshape(seq_count, seg_len, half_width)
+    out_side = lax.psum_scatter(out_share, axes, scatter_dimension=0, axis_index_groups=pairs_of, tiled=True)
     home_scores = jnp.sum(row_home[:, :, half_width:].astype(f32), axis=0)
     home_scores = home_scores[:, :expert_count] + home_scores[:, expert_count : 2 * expert_count]
     gate_grads = jnp.sum(picked * home_scores[:, None, :], axis=-1)
@@ -1937,7 +1987,13 @@
         head_in, mixing_weight, (((1,), (1,)), ((), ())), preferred_element_type=f32
     ).astype(bf16)
     head_cut = head_in.reshape(token_count, planes, 4 * share_width).transpose(1, 0, 2)
-    query_rot_grad, pair_home, mixing_part = attend_back(
+    turns = jnp.stack(
+        [
+            jnp.concatenate([cosine[:, 0], cosine[:, 0]], axis=1),
+            jnp.concatenate([sine_table[:, 0], -sine_table[:, 0]], axis=1),
+        ]
+    )
+    all_low, gain_grads, mixing_part = attend_back(
         query_rows,
         context_grad,
         context,
@@ -1945,23 +2001,20 @@
         logs,
         head_cut,
         context_column,
+        (query_raw.reshape(token_count, -1), key_raw.reshape(token_count, key_width)),
+        jnp.stack([query_gain, key_gain]),
+        turns,
         planes,
         group_size,
         head_dim,
         7,
     )
-    key_raw_grad, keygain_part = key_back(
-        pair_home[:, :key_width].reshape(seq_count, seg_len, local_keys, head_dim)
-    )
-    query_raw_grad, querygain_part = query_back(
-        query_rot_grad.reshape(seq_count, seg_len, local_queries, head_dim)
-    )
-    query_low = query_raw_grad.astype(bf16).reshape(token_count, local_queries * head_dim)
-    key_low = key_raw_grad.astype(bf16).reshape(token_count, key_width)
-    value_low = pair_home[:, key_width:].astype(bf16)
-    all_low = jnp.concatenate([query_low, key_low, value_low], axis=1)
+    all_low, out_side = lax.optimization_barrier((all_low, out_side))
+    out_home = lax.psum_scatter(out_side, axes, scatter_dimension=0, axis_index_groups=groups_of, tiled=True)[0]
+    residual_half = lax.dynamic_slice_in_dim(residual, tensor_idx * half_width, half_width, 1)
+    layer_output = (residual_half + out_home.astype(f32)).astype(bf16).reshape(seq_count, seg_len, half_width)
     gain_row = jnp.pad(
-        jnp.concatenate([querygain_part, keygain_part])[None], ((0, 7), (0, model_width - 2 * head_dim))
+        gain_grads[:2].reshape(1, 2 * head_dim), ((0, 7), (0, model_width - 2 * head_dim))
     )
     small = jnp.concatenate(
         [gain_row, jnp.pad(second_grad[None], ((1, 6), (0, 0))), router_grad], axis=0

time: 525 us -> 477 us (0.909); the launches traced: 517 us -> 476 us
  Pallas kernels: 377 us -> 353 us
  local copies, waits for them, and re-layouts: 44.1 us -> 33 us
  other arithmetic: 20.7 us -> 12.8 us
    pallas_call x1, Pallas kernels: 80.6 us -> 59.9 us  [attend_back(): pl.pallas_call(functools.partial(attend_back_kernel, planes, group), out_...]
    pallas_call x1, Pallas kernels: 156 us -> 150 us  [run_experts(): pl.pallas_call(functools.partial(experts_kernel, planes), out_shape=[jax....]
    unnamed x100 -> x51, local copies, waits for them, and re-layouts: 22.9 us -> 17.6 us
  transfers between devices with their start and end apart: 2 -> 3, of which waited for: 1 -> 1; matrix products, arithmetic and copies ran while one was open for 13% -> 11% of each run, Pallas kernels for 43% -> 43%
where the time goes in v3:
time: 477 us; the launch traced here: 476 us
  Pallas kernels  353 us (74%)
  waiting for transfers between devices  41.9 us (9%)
  local copies, waits for them, and re-layouts  33 us (7%)
  matrix products  20.9 us (4%)
  between operations  14.3 us (3%)
  other arithmetic  12.8 us (3%)
    pallas_call x1, Pallas kernels, run_experts(): pl.pallas_call(functools.partial(experts_kernel, planes), out_shape=[jax....  150 us
    pallas_call x1, Pallas kernels, weight_grads(): pl.pallas_call(functools.partial(weights_kernel, planes, chunk), out_shap...  106 us
    pallas_call x1, Pallas kernels, attend_back(): pl.pallas_call(functools.partial(attend_back_kernel, planes, group), out_...  59.9 us
    all_gather x1, waiting for transfers between devices, on_chips(): upstream_mine = lax.all_gather(upstream_half, 'expert')  41.8 us
    pallas_call x1, Pallas kernels, attend(): pl.pallas_call(functools.partial(attend_kernel, planes, group), out_shape...  34.1 us
    unnamed x51, local copies, waits for them, and re-layouts  17.6 us
  transfers between devices with their start and end apart: 3, of which 1 were waited for; matrix products, arithmetic and copies ran while one was open for 11% of the time, Pallas kernels for 43%

profile of v3, /device:TPU:8, one launch (start us, length us, event | category | flops | bytes accessed | tf_op | source)
XLA Modules:
  0.0 476.3 jit_solution(15155268032647529781)
XLA Ops:
  7.3 1.8 constant_dynamic-slice_fusion
  14.6 1.2 reshape.278.cut_ref
  15.7 5.2 %fusion = f32[3,64,2048]{2,1,0:T(8,128)S(1)} fusion(bf16[3,64,2048]{2,1,0:T(8,128)(2,1)S(1)} %multiply_convert_fusion.1, bf16[2048,2048]{1,0:T(8,128)(2,1)} %query_w.1), kind=kOutput, calls=%fused_computation | convolution fusion | flops 1610612736 | bytes 10747904 | tf_op jit(solution)/shard_map/dot_general | solution.py:1924
  24.3 1.1 copy.130
  26.4 34.1 %attend.1 = (bf16[192,2048]{1,0:T(8,128)(2,1)}, bf16[16,192,512]{2,1,0:T(8,128)(2,1)}, f32[6,512,128]{2,1,0:T(8,128)}) custom-call(bf16[192,2048]{1,0:T(8,128)(2,1)} %bitcast.106, bf16[192,512]{1,0:T(8,128)(2,1)} %pad_maximum_fusion.1.x_ref), custom_call_target="tpu_custom_call" | custom-call | tf_op jit(solution)/shard_map/attend/pallas_call | solution.py:846
  60.6 6.3 %convolution_convert_fusion.1.x_ref = bf16[192,2048]{1,0:T(8,128)(2,1)} fusion(bf16[192,2048]{1,0:T(8,128)(2,1)} %get-tuple-element.33.context_ref.o_ref, bf16[2048,2048]{1,0:T(8,128)(2,1)} %param.21), kind=kOutput, calls=%fused_computation.4 | convolution fusion | flops 1611005952 | bytes 9961472 | tf_op jit(solution)/shard_map/dot_general | solution.py:1943
  66.9 2.6 swap_heads.1
  69.5 1.7 bitcast_add_fusion
  74.3 41.8 %all-gather.3.cloned.1.call-done = bf16[1536,2048]{1,0:T(8,128)(2,1)} async-done(((bf16[96,2048]{1,0:T(8,128)(2,1)}), bf16[1536,2048]{1,0:T(8,128)(2,1)}) %all-gather.3.cloned.1.call-update) | async-done | bytes 6291472 | tf_op jit(solution)/shard_map/all_gather | solution.py:1940
  116.2 150.0 %experts.1 = (bf16[16,192,2176]{2,1,0:T(8,128)(2,1)}, bf16[16,96,2048]{2,1,0:T(8,128)(2,1)}, bf16[16,192,1024]{2,1,0:T(8,128)(2,1)}, bf16[2,192,1152]{2,1,0:T(8,...) custom-call(bf16[192,2176]{1,0:T(8,128)(2,1)} %concatenate.36.parcel, ...), custom_call_target="tpu_custom_call" | custom-call | tf_op jit(solution)/shard_map/experts/pallas_call | solution.py:653
  269.4 1.7 fusion.27
  272.0 7.2 %convolution_convert_fusion.g_ref = bf16[192,2048]{1,0:T(8,128)(2,1)} fusion(bf16[192,2048]{1,0:T(8,128)(2,1)S(1)} %get-tuple-element.154, bf16[2048,2048]{1,0:T(8,128)(2,1)} %param.21), kind=kOutput, calls=%fused_computation.3 | convolution fusion | flops 1611005952 | bytes 9961472 | tf_op jit(solution)/shard_map/dot_general | solution.py:1986
  279.2 59.9 %attend_back.1 = (bf16[192,2560]{1,0:T(8,128)(2,1)}, f32[8,128]{1,0:T(8,128)}, bf16[4,128,2048]{2,1,0:T(8,128)(2,1)}) custom-call(bf16[192,2048]{1,0:T(8,128)(2,1)} %bitcast.107, bf16[192,2048]{1,0:T(8,128)(2,1)} %convolution_convert_fusion.g_ref, bf16[192,2048]{1,0:T(8,128)(2,1)} %get-tuple-element.33.context_ref.o_ref, ...), custom_call_target="tpu_custom_call" | custom-call | tf_op jit(solution)/shard_map/attend_back/pallas_call | solution.py:1097
  339.1 1.7 dynamic-slice_dynamic-update-slice_fusion
  340.8 2.3 copy.102
  344.7 106.4 %weight_grads.1 = (f32[128,2560]{1,0:T(8,128)}, f32[192,2048]{1,0:T(8,128)}, f32[32,2048]{1,0:T(8,128)}, f32[128,2048]{1,0:T(8,128)}) custom-call(bf16[192,2560]{1,0:T(8,128)(2,1)} %get-tuple-element.41.low_ref, bf16[512,768]{1,0:T(8,128)(2,1)} %bitcast.116, bf16[2048,2048]{1,0:T(8,128)(2,1)} %query_w.1, bf16[2048,256]{1,0:T(8,128)(2,1)} %key_w.1, ...), custom_call_target="tpu_custom_call" | custom-call | tf_op jit(solution)/shard_map/weight_grads/pallas_call | solution.py:1425
  451.1 2.6 copy.103
  457.3 1.8 fusion.8
  459.2 2.9 copy.140
  462.0 1.7 copy.141
  463.7 1.4 copy-done.10
  465.0 1.7 copy.142
  466.7 1.4 copy-done.9
  468.1 1.7 copy.143
  (113 shorter events, 21.9 us)
Async XLA Ops:
  7.2 65.0 %copy-start = (bf16[2048,16]{0,1:T(8,128)(2,1)S(1)}, bf16[2048,16]{0,1:T(8,128)(2,1)}, u32[]{:S(2)}) copy-start(bf16[2048,16]{0,1:T(8,128)(2,1)} %param.25) | copy-start | bytes 196612
  7.2 3.6 copy-start.5
  7.2 3.8 copy-start.18
  7.2 109.0 %all-gather.3.cloned.1.call-start = ((), (), s32[]{:S(2)}) async-start(), calls=%async_computation.4 | async-start | bytes 6684672 | tf_op jit(solution)/shard_map/all_gather | solution.py:1940
  9.1 329.9 %reduce-scatter.3.cloned.1.call-start = ((), (), s32[]{:S(2)}) async-start(), calls=%async_computation.2 | async-start | bytes 9437184 | tf_op jit(solution)/shard_map/reduce_scatter | solution.py:1970
  11.0 1.2 copy-start.7
  12.2 1.1 copy-start.19
  12.6 1.9 copy-start.13
  20.9 1.1 copy-start.2
  22.1 0.7 copy-start.20
  23.8 1.5 copy-start.8
  66.9 2.7 copy-start.6
  71.3 0.7 copy-start.17
  72.2 2.1 copy-start.3
  266.2 1.6 copy-start.15
  266.3 191.1 %reduce-scatter.5.cloned.1.call-start = ((), (), s32[]{:S(2)}) async-start(), calls=%async_computation.3 | async-start | bytes 3538944 | tf_op jit(solution)/shard_map/reduce_scatter | solution.py:2013
  268.2 1.1 copy-start.12
  339.1 4.7 copy-start.4
  451.1 2.6 copy-start.14
  453.8 1.0 copy-start.16
  459.2 2.9 copy-start.11
  462.0 3.0 copy-start.10
  465.0 3.0 copy-start.9
  468.1 1.7 copy-start.1
Sparse Core Ops, SparseCore 0:
  11.4 104.7 all-gather.2
  266.4 59.1 reduce-scatter.2
  339.2 68.6 reduce-scatter.4

commit v4 on v3

--- a/solution.py
+++ b/solution.py
@@ -162,6 +162,8 @@
     gates,
     scores,
     stage,
+    given,
+    taken,
     mine,
     outgoing,
     partner,
@@ -182,6 +184,8 @@
     rsem,
     lsem,
     osem,
+    osend,
+    orecv,
     esem,
     xsend,
     xrecv,
@@ -486,21 +490,27 @@
         row = jnp.where(mark == me.e, high, jnp.where(mark == me.e + count, total - high, 0.0))
         rbuf[:, side:] = row.astype(bf16)
 
-    def store(sa, q):
-        sb, sc = side_of(q)
-        there = share_ref.at[sc * 2 * planes + sa * 2 + sb]
-        return pltpu.make_async_copy(stage.at[lax.rem(q, 2)], there, osem.at[lax.rem(q, 2)])
+    def send_out(sa, sb):
+        slot = sa * 2 + sb
+        there = me.at(me.a, me.b, 1 - me.c)
+        return push(given.at[slot], taken.at[slot], osend.at[slot], orecv.at[slot], there)
+
+    def store(sa, sb):
+        slot = sa * 2 + sb
+        return pltpu.make_async_copy(stage.at[slot], share_ref.at[slot], osem.at[slot])
+
+    def out_from_c(sa):
+        for sb in (0, 1):
+            slot = sa * 2 + sb
+            send_out(sa, sb).wait_recv()
+            for n in range(0, side, 512):
+                cut = slice(n, n + 512)
+                spread = over(partner[slot], taken[slot, :, cut], NN)
+                stage[slot, :, cut] = (stage[slot, :, cut].astype(f32) + spread).astype(bf16)
+            store(sa, sb).start()
 
     def spread_rows(q, sa):
         at = pl.ds(pl.multiple_of(q * slots, slots), slots)
-
-        @pl.when((q >= 2) | (sa != near(1)))
-        def _():
-            store(sa, q).wait()
-
-        for n in range(0, side, 512):
-            cut = slice(n, n + 512)
-            stage[lax.rem(q, 2), :, cut] = over(sbuf[q], wbuf[at, cut], NN).astype(bf16)
         sb, sc = side_of(q)
         slot = sa * 2 + sb
 
@@ -509,13 +519,16 @@
             for n in range(0, mine.shape[2], 384):
                 cut = slice(n, n + 384)
                 mine[slot, :, cut] = over(sbuf[q], rbuf[at, cut], NN).astype(bf16)
+            for n in range(0, side, 512):
+                cut = slice(n, n + 512)
+                stage[slot, :, cut] = over(sbuf[q], wbuf[at, cut], NN).astype(bf16)
 
         @pl.when(sc != me.c)
         def _():
             outgoing[slot] = rbuf[at, :]
             send_c(sa, sb).start()
-
-        store(sa, q).start()
+            given[slot] = wbuf[at, :]
+
         return sa
 
     me.greet(planes, True, True, True, True, True)
@@ -584,6 +597,8 @@
         lax.fori_loop(0, side // 512, out_rows, slot)
         note_scores()
         lax.fori_loop(0, 4, spread_rows, sa)
+        for sb in (0, 1):
+            send_out(sa, sb).start()
 
         @pl.when(i + 2 < planes)
         def _():
@@ -598,14 +613,14 @@
         @pl.when(i > 0)
         def _():
             along(near(i))
+            out_from_c(near(i))
 
         return c
 
     lax.fori_loop(0, planes, step, 0)
     from_c(me.a)
+    out_from_c(me.a)
     finish()
-    store(me.a, 0).wait()
-    store(me.a, 1).wait()
     done = push(home_ref.at[me.t], home_ref.at[me.t], esem.at[0], esem.at[1], me.core())
     done.start()
 
@@ -623,6 +638,8 @@
         across(sa, False)
         for sb in (1 - me.b, me.b):
             send_c(sa, sb).wait_send()
+            send_out(sa, sb).wait_send()
+            store(sa, sb).wait()
         send_b(sa).wait_send()
         upstream(sa).wait_send()
         return c
@@ -655,7 +672,7 @@
         out_shape=[
             jax.ShapeDtypeStruct((count, tokens, packed), bf16),
             jax.ShapeDtypeStruct((count, half, width), bf16),
-            jax.ShapeDtypeStruct((count, tokens, side), bf16),
+            jax.ShapeDtypeStruct((2 * planes, tokens, side), bf16),
             jax.ShapeDtypeStruct((2, tokens, block), bf16),
             jax.ShapeDtypeStruct((planes,) + context.shape, bf16),
             jax.ShapeDtypeStruct(cut.shape, bf16),
@@ -682,7 +699,9 @@
             pltpu.VMEM((2, rows, 4 * hidden), bf16),
             pltpu.VMEM((rows, 128), f32),
             pltpu.VMEM((rows, 128), f32),
-            pltpu.VMEM((2, tokens, side), bf16),
+            pltpu.VMEM((2 * planes, tokens, side), bf16),
+            pltpu.VMEM((2 * planes, slots, side), bf16),
+            pltpu.VMEM((2 * planes, slots, side), bf16),
             pltpu.VMEM((2 * planes, tokens, block), bf16),
             pltpu.VMEM((2 * planes, slots, block), bf16),
             pltpu.VMEM((2 * planes, tokens, slots), bf16),
@@ -702,7 +721,9 @@
             pltpu.SemaphoreType.DMA((3, 2 * planes)),
             pltpu.SemaphoreType.DMA((3, 2 * planes)),
             pltpu.SemaphoreType.DMA((7,)),
-            pltpu.SemaphoreType.DMA((2,)),
+            pltpu.SemaphoreType.DMA((2 * planes,)),
+            pltpu.SemaphoreType.DMA((2 * planes,)),
+            pltpu.SemaphoreType.DMA((2 * planes,)),
             pltpu.SemaphoreType.DMA((2,)),
             pltpu.SemaphoreType.DMA((planes, 2)),
             pltpu.SemaphoreType.DMA((planes,)),
@@ -1861,9 +1882,7 @@
         return (a * 4 + y * 2 + x) * 2 + t
 
     both = (0, 1)
-    pairs = [[number(a, b, c, t) for c in both] for t in both for a in range(planes) for b in both]
-    groups = [[number(a, b, c, t) for a in range(planes) for b in both] for t in both for c in both]
-    return pairs, groups
+    return [[number(a, b, c, t) for a in range(planes) for b in both] for t in both for c in both]
 
 
 def lift(values, wide):
@@ -1936,7 +1955,7 @@
     half_tokens = token_count // 2
     upstream_half = lax.dynamic_slice_in_dim(upstream_low, tensor_idx * half_tokens, half_tokens, 0)
     axes = ("expert", "tensor")
-    pairs_of, groups_of = partners(planes)
+    groups_of = partners(planes)
     upstream_mine = lax.all_gather(upstream_half, "expert")
     query_rows = query_rot.astype(bf16).reshape(token_count, local_queries * head_dim)
     context, pairs_all, logs = attend(query_rows, pairs, planes, group_size, head_dim, 1)
@@ -1967,7 +1986,7 @@
     place = lax.rem(expert_idx, 4)
     own_cut = lax.dynamic_index_in_dim(normed_cut, place, 0)
     normed_cut = lax.dynamic_update_slice_in_dim(other_cuts, own_cut, place, 0)
-    out_side = lax.psum_scatter(out_share, axes, scatter_dimension=0, axis_index_groups=pairs_of, tiled=True)
+    out_home = lax.psum_scatter(out_share, axes, scatter_dimension=0, axis_index_groups=groups_of, tiled=True)[0]
     home_scores = jnp.sum(row_home[:, :, half_width:].astype(f32), axis=0)
     home_scores = home_scores[:, :expert_count] + home_scores[:, expert_count : 2 * expert_count]
     gate_grads = jnp.sum(picked * home_scores[:, None, :], axis=-1)
@@ -2009,8 +2028,6 @@
         head_dim,
         7,
     )
-    all_low, out_side = lax.optimization_barrier((all_low, out_side))
-    out_home = lax.psum_scatter(out_side, axes, scatter_dimension=0, axis_index_groups=groups_of, tiled=True)[0]
     residual_half = lax.dynamic_slice_in_dim(residual, tensor_idx * half_width, half_width, 1)
     layer_output = (residual_half + out_home.astype(f32)).astype(bf16).reshape(seq_count, seg_len, half_width)
     gain_row = jnp.pad(

time: 477 us -> 461 us (0.966)
  Pallas kernels: 353 us -> 337 us
    pallas_call x1, Pallas kernels: 106 us -> 90.2 us  [weight_grads(): pl.pallas_call(functools.partial(weights_kernel, planes, chunk), out_shap...]
  transfers between devices with their start and end apart: 3 -> 2, of which waited for: 1 -> 1; matrix products, arithmetic and copies ran while one was open for 11% -> 11% of each run, Pallas kernels for 43% -> 41%
where the time goes in v4:
time: 461 us
  Pallas kernels  337 us (73%)
  waiting for transfers between devices  41.8 us (9%)
  local copies, waits for them, and re-layouts  33 us (7%)
  matrix products  21.2 us (5%)
  between operations  14.5 us (3%)
  other arithmetic  12.8 us (3%)
    pallas_call x1, Pallas kernels, run_experts(): pl.pallas_call(functools.partial(experts_kernel, planes), out_shape=[jax....  148 us
    pallas_call x1, Pallas kernels, weight_grads(): pl.pallas_call(functools.partial(weights_kernel, planes, chunk), out_shap...  90.2 us
    pallas_call x1, Pallas kernels, attend_back(): pl.pallas_call(functools.partial(attend_back_kernel, planes, group), out_...  62.1 us
    all_gather x1, waiting for transfers between devices, on_chips(): upstream_mine = lax.all_gather(upstream_half, 'expert')  41.7 us
    pallas_call x1, Pallas kernels, attend(): pl.pallas_call(functools.partial(attend_kernel, planes, group), out_shape...  34.1 us
    unnamed x51, local copies, waits for them, and re-layouts  17.6 us
  transfers between devices with their start and end apart: 2, of which 1 were waited for; matrix products, arithmetic and copies ran while one was open for 11% of the time, Pallas kernels for 41%

profile of v4, /device:TPU:8, one launch (start us, length us, event | category | flops | bytes accessed | tf_op | source)
XLA Modules:
  0.0 460.7 jit_solution(2941356139542193800)
XLA Ops:
  7.3 1.8 constant_dynamic-slice_fusion
  14.6 1.2 reshape.278.cut_ref
  15.7 5.2 %fusion = f32[3,64,2048]{2,1,0:T(8,128)S(1)} fusion(bf16[3,64,2048]{2,1,0:T(8,128)(2,1)S(1)} %multiply_convert_fusion.1, bf16[2048,2048]{1,0:T(8,128)(2,1)} %query_w.1), kind=kOutput, calls=%fused_computation | convolution fusion | flops 1610612736 | bytes 10747904 | tf_op jit(solution)/shard_map/dot_general | solution.py:1943
  24.3 1.1 copy.130
  26.4 34.1 %attend.1 = (bf16[192,2048]{1,0:T(8,128)(2,1)}, bf16[16,192,512]{2,1,0:T(8,128)(2,1)}, f32[6,512,128]{2,1,0:T(8,128)}) custom-call(bf16[192,2048]{1,0:T(8,128)(2,1)} %bitcast.106, bf16[192,512]{1,0:T(8,128)(2,1)} %pad_maximum_fusion.1.x_ref), custom_call_target="tpu_custom_call" | custom-call | tf_op jit(solution)/shard_map/attend/pallas_call | solution.py:867
  60.6 6.3 %convolution_convert_fusion.1.x_ref = bf16[192,2048]{1,0:T(8,128)(2,1)} fusion(bf16[192,2048]{1,0:T(8,128)(2,1)} %get-tuple-element.31.context_ref.o_ref, bf16[2048,2048]{1,0:T(8,128)(2,1)} %param.21), kind=kOutput, calls=%fused_computation.4 | convolution fusion | flops 1611005952 | bytes 9961472 | tf_op jit(solution)/shard_map/dot_general | solution.py:1962
  66.9 2.6 swap_heads.1
  69.6 1.7 bitcast_add_fusion
  74.4 41.7 %all-gather.3.cloned.1.call-done = bf16[1536,2048]{1,0:T(8,128)(2,1)} async-done(((bf16[96,2048]{1,0:T(8,128)(2,1)}), bf16[1536,2048]{1,0:T(8,128)(2,1)}) %all-gather.3.cloned.1.call-update) | async-done | bytes 6291472 | tf_op jit(solution)/shard_map/all_gather | solution.py:1959
  116.1 148.2 %experts.1 = (bf16[16,192,2176]{2,1,0:T(8,128)(2,1)}, bf16[16,96,2048]{2,1,0:T(8,128)(2,1)}, bf16[8,192,1024]{2,1,0:T(8,128)(2,1)}, bf16[2,192,1152]{2,1,0:T(8,1...) custom-call(bf16[192,2176]{1,0:T(8,128)(2,1)} %concatenate.36.parcel, ...), custom_call_target="tpu_custom_call" | custom-call | tf_op jit(solution)/shard_map/experts/pallas_call | solution.py:670
  265.7 1.6 dynamic-slice_dynamic-update-slice_fusion
  267.3 2.3 copy.102
  271.2 1.7 fusion.27
  273.8 7.5 %convolution_convert_fusion.g_ref = bf16[192,2048]{1,0:T(8,128)(2,1)} fusion(bf16[192,2048]{1,0:T(8,128)(2,1)S(1)} %get-tuple-element.150, bf16[2048,2048]{1,0:T(8,128)(2,1)} %param.21), kind=kOutput, calls=%fused_computation.3 | convolution fusion | flops 1611005952 | bytes 9961472 | tf_op jit(solution)/shard_map/dot_general | solution.py:2005
  281.3 62.1 %attend_back.1 = (bf16[192,2560]{1,0:T(8,128)(2,1)}, f32[8,128]{1,0:T(8,128)}, bf16[4,128,2048]{2,1,0:T(8,128)(2,1)}) custom-call(bf16[192,2048]{1,0:T(8,128)(2,1)} %bitcast.107, bf16[192,2048]{1,0:T(8,128)(2,1)} %convolution_convert_fusion.g_ref, bf16[192,2048]{1,0:T(8,128)(2,1)} %get-tuple-element.31.context_ref.o_ref, ...), custom_call_target="tpu_custom_call" | custom-call | tf_op jit(solution)/shard_map/attend_back/pallas_call | solution.py:1118
  345.0 90.2 %weight_grads.1 = (f32[128,2560]{1,0:T(8,128)}, f32[192,2048]{1,0:T(8,128)}, f32[32,2048]{1,0:T(8,128)}, f32[128,2048]{1,0:T(8,128)}) custom-call(bf16[192,2560]{1,0:T(8,128)(2,1)} %get-tuple-element.37.low_ref, bf16[512,768]{1,0:T(8,128)(2,1)} %bitcast.116, bf16[2048,2048]{1,0:T(8,128)(2,1)} %query_w.1, bf16[2048,256]{1,0:T(8,128)(2,1)} %key_w.1, ...), custom_call_target="tpu_custom_call" | custom-call | tf_op jit(solution)/shard_map/weight_grads/pallas_call | solution.py:1446
  435.2 2.6 copy.103
  441.4 1.8 fusion.8
  443.3 2.9 copy.140
  446.1 1.7 copy.141
  447.8 1.4 copy-done.10
  449.1 1.7 copy.142
  450.8 1.4 copy-done.9
  452.2 1.7 copy.143
  (110 shorter events, 21.6 us)
Async XLA Ops:
  7.2 65.1 %copy-start = (bf16[2048,16]{0,1:T(8,128)(2,1)S(1)}, bf16[2048,16]{0,1:T(8,128)(2,1)}, u32[]{:S(2)}) copy-start(bf16[2048,16]{0,1:T(8,128)(2,1)} %param.25) | copy-start | bytes 196612
  7.2 3.6 copy-start.5
  7.2 3.8 copy-start.18
  7.2 108.9 %all-gather.3.cloned.1.call-start = ((), (), s32[]{:S(2)}) async-start(), calls=%async_computation.2 | async-start | bytes 6684672 | tf_op jit(solution)/shard_map/all_gather | solution.py:1959
  9.1 432.3 %reduce-scatter.2.cloned.1.call-start = ((), (), s32[]{:S(2)}) async-start(), calls=%async_computation.1 | async-start | bytes 3538944 | tf_op jit(solution)/shard_map/reduce_scatter | solution.py:1989
  11.0 1.2 copy-start.7
  12.2 1.0 copy-start.19
  12.6 1.9 copy-start.13
  20.9 1.1 copy-start.2
  22.1 0.7 copy-start.20
  23.8 1.5 copy-start.8
  66.9 2.7 copy-start.6
  71.3 0.7 copy-start.17
  72.2 2.1 copy-start.3
  264.4 5.2 %copy-start.15 = (bf16[2,192,1152]{2,1,0:T(8,128)(2,1)S(1)}, bf16[2,192,1152]{2,1,0:T(8,128)(2,1)}, u32[]{:S(2)}) copy-start(bf16[2,192,1152]{2,1,0:T(8,128)(2,1)} %get-tuple-element.33) | copy-start | bytes 2654212
  270.0 1.1 copy-start.12
  281.3 62.8 %copy-start.4 = (bf16[192,2048]{1,0:T(8,128)(2,1)S(1)}, bf16[192,2048]{1,0:T(8,128)(2,1)}, u32[]{:S(2)}) copy-start(bf16[192,2048]{1,0:T(8,128)(2,1)} %copy-done.3) | copy-start | bytes 2359300
  435.2 2.6 copy-start.14
  437.9 1.0 copy-start.16
  443.2 2.9 copy-start.11
  446.1 3.0 copy-start.10
  449.1 3.0 copy-start.9
  452.2 1.7 copy-start.1
Sparse Core Ops, SparseCore 0:
  11.4 104.6 all-gather.2
  264.5 67.9 reduce-scatter.1

commit v5 on v4

--- a/solution.py
+++ b/solution.py
@@ -509,9 +509,10 @@
                 stage[slot, :, cut] = (stage[slot, :, cut].astype(f32) + spread).astype(bf16)
             store(sa, sb).start()
 
-    def spread_rows(q, sa):
+    def spread_rows(j, sa):
+        sb, sc = lax.rem(j, 2), jnp.where(j < 2, 1 - me.c, me.c)
+        q = 2 * (sc + me.t * (sb - sc)) + sb + me.t * (sc - sb)
         at = pl.ds(pl.multiple_of(q * slots, slots), slots)
-        sb, sc = side_of(q)
         slot = sa * 2 + sb
 
         @pl.when(sc == me.c)
@@ -608,11 +609,14 @@
         def _():
             fetch_rows(after)
 
+        @pl.when(i > 0)
+        def _():
+            along(near(i))
+
         lax.fori_loop(0, width // 512, weight_sums, slot)
 
         @pl.when(i > 0)
         def _():
-            along(near(i))
             out_from_c(near(i))
 
         return c

time: 461 us -> 460 us (level)
  no operation moved by 1% of the time
where the time goes in v5:
time: 460 us; the launch traced here: 459 us
  Pallas kernels  336 us (73%)
  waiting for transfers between devices  41.8 us (9%)
  local copies, waits for them, and re-layouts  33 us (7%)
  matrix products  20.9 us (5%)
  between operations  14.5 us (3%)
  other arithmetic  12.8 us (3%)
    pallas_call x1, Pallas kernels, run_experts(): pl.pallas_call(functools.partial(experts_kernel, planes), out_shape=[jax....  150 us
    pallas_call x1, Pallas kernels, weight_grads(): pl.pallas_call(functools.partial(weights_kernel, planes, chunk), out_shap...  88.9 us
    pallas_call x1, Pallas kernels, attend_back(): pl.pallas_call(functools.partial(attend_back_kernel, planes, group), out_...  60.4 us
    all_gather x1, waiting for transfers between devices, on_chips(): upstream_mine = lax.all_gather(upstream_half, 'expert')  41.7 us
    pallas_call x1, Pallas kernels, attend(): pl.pallas_call(functools.partial(attend_kernel, planes, group), out_shape...  34.1 us
    unnamed x51, local copies, waits for them, and re-layouts  17.6 us
  transfers between devices with their start and end apart: 2, of which 1 were waited for; matrix products, arithmetic and copies ran while one was open for 11% of the time, Pallas kernels for 41%

profile of v5, /device:TPU:8, one launch (start us, length us, event | category | flops | bytes accessed | tf_op | source)
XLA Modules:
  0.0 459.1 jit_solution(7686130749424591642)
XLA Ops:
  7.3 1.8 constant_dynamic-slice_fusion
  14.6 1.2 reshape.278.cut_ref
  15.7 5.2 %fusion = f32[3,64,2048]{2,1,0:T(8,128)S(1)} fusion(bf16[3,64,2048]{2,1,0:T(8,128)(2,1)S(1)} %multiply_convert_fusion.1, bf16[2048,2048]{1,0:T(8,128)(2,1)} %query_w.1), kind=kOutput, calls=%fused_computation | convolution fusion | flops 1610612736 | bytes 10747904 | tf_op jit(solution)/shard_map/dot_general | solution.py:1947
  24.3 1.1 copy.130
  26.4 34.1 %attend.1 = (bf16[192,2048]{1,0:T(8,128)(2,1)}, bf16[16,192,512]{2,1,0:T(8,128)(2,1)}, f32[6,512,128]{2,1,0:T(8,128)}) custom-call(bf16[192,2048]{1,0:T(8,128)(2,1)} %bitcast.106, bf16[192,512]{1,0:T(8,128)(2,1)} %pad_maximum_fusion.1.x_ref), custom_call_target="tpu_custom_call" | custom-call | tf_op jit(solution)/shard_map/attend/pallas_call | solution.py:871
  60.6 6.3 %convolution_convert_fusion.1.x_ref = bf16[192,2048]{1,0:T(8,128)(2,1)} fusion(bf16[192,2048]{1,0:T(8,128)(2,1)} %get-tuple-element.31.context_ref.o_ref, bf16[2048,2048]{1,0:T(8,128)(2,1)} %param.21), kind=kOutput, calls=%fused_computation.4 | convolution fusion | flops 1611005952 | bytes 9961472 | tf_op jit(solution)/shard_map/dot_general | solution.py:1966
  66.9 2.6 swap_heads.1
  69.6 1.7 bitcast_add_fusion
  74.4 41.7 %all-gather.3.cloned.1.call-done = bf16[1536,2048]{1,0:T(8,128)(2,1)} async-done(((bf16[96,2048]{1,0:T(8,128)(2,1)}), bf16[1536,2048]{1,0:T(8,128)(2,1)}) %all-gather.3.cloned.1.call-update) | async-done | bytes 6291472 | tf_op jit(solution)/shard_map/all_gather | solution.py:1963
  116.1 150.0 %experts.1 = (bf16[16,192,2176]{2,1,0:T(8,128)(2,1)}, bf16[16,96,2048]{2,1,0:T(8,128)(2,1)}, bf16[8,192,1024]{2,1,0:T(8,128)(2,1)}, bf16[2,192,1152]{2,1,0:T(8,1...) custom-call(bf16[192,2176]{1,0:T(8,128)(2,1)} %concatenate.36.parcel, ...), custom_call_target="tpu_custom_call" | custom-call | tf_op jit(solution)/shard_map/experts/pallas_call | solution.py:674
  267.5 1.6 dynamic-slice_dynamic-update-slice_fusion
  269.2 2.3 copy.102
  273.0 1.7 fusion.27
  275.6 7.2 %convolution_convert_fusion.g_ref = bf16[192,2048]{1,0:T(8,128)(2,1)} fusion(bf16[192,2048]{1,0:T(8,128)(2,1)S(1)} %get-tuple-element.150, bf16[2048,2048]{1,0:T(8,128)(2,1)} %param.21), kind=kOutput, calls=%fused_computation.3 | convolution fusion | flops 1611005952 | bytes 9961472 | tf_op jit(solution)/shard_map/dot_general | solution.py:2009
  282.8 60.4 %attend_back.1 = (bf16[192,2560]{1,0:T(8,128)(2,1)}, f32[8,128]{1,0:T(8,128)}, bf16[4,128,2048]{2,1,0:T(8,128)(2,1)}) custom-call(bf16[192,2048]{1,0:T(8,128)(2,1)} %bitcast.107, bf16[192,2048]{1,0:T(8,128)(2,1)} %convolution_convert_fusion.g_ref, bf16[192,2048]{1,0:T(8,128)(2,1)} %get-tuple-element.31.context_ref.o_ref, ...), custom_call_target="tpu_custom_call" | custom-call | tf_op jit(solution)/shard_map/attend_back/pallas_call | solution.py:1122
  344.8 88.9 %weight_grads.1 = (f32[128,2560]{1,0:T(8,128)}, f32[192,2048]{1,0:T(8,128)}, f32[32,2048]{1,0:T(8,128)}, f32[128,2048]{1,0:T(8,128)}) custom-call(bf16[192,2560]{1,0:T(8,128)(2,1)} %get-tuple-element.37.low_ref, bf16[512,768]{1,0:T(8,128)(2,1)} %bitcast.116, bf16[2048,2048]{1,0:T(8,128)(2,1)} %query_w.1, bf16[2048,256]{1,0:T(8,128)(2,1)} %key_w.1, ...), custom_call_target="tpu_custom_call" | custom-call | tf_op jit(solution)/shard_map/weight_grads/pallas_call | solution.py:1450
  433.7 2.6 copy.103
  439.9 1.8 fusion.8
  441.7 2.9 copy.140
  444.6 1.7 copy.141
  446.2 1.4 copy-done.10
  447.6 1.7 copy.142
  449.3 1.4 copy-done.9
  450.6 1.7 copy.143
  (110 shorter events, 21.6 us)
Async XLA Ops:
  7.2 65.1 %copy-start = (bf16[2048,16]{0,1:T(8,128)(2,1)S(1)}, bf16[2048,16]{0,1:T(8,128)(2,1)}, u32[]{:S(2)}) copy-start(bf16[2048,16]{0,1:T(8,128)(2,1)} %param.25) | copy-start | bytes 196612
  7.2 3.6 copy-start.5
  7.2 3.8 copy-start.18
  7.2 108.9 %all-gather.3.cloned.1.call-start = ((), (), s32[]{:S(2)}) async-start(), calls=%async_computation.2 | async-start | bytes 6684672 | tf_op jit(solution)/shard_map/all_gather | solution.py:1963
  9.1 430.8 %reduce-scatter.2.cloned.1.call-start = ((), (), s32[]{:S(2)}) async-start(), calls=%async_computation.1 | async-start | bytes 3538944 | tf_op jit(solution)/shard_map/reduce_scatter | solution.py:1993
  11.0 1.2 copy-start.7
  12.2 1.0 copy-start.19
  12.6 1.9 copy-start.13
  20.9 1.1 copy-start.2
  22.1 0.7 copy-start.20
  23.8 1.5 copy-start.8
  66.9 2.7 copy-start.6
  71.3 0.7 copy-start.17
  72.2 2.1 copy-start.3
  266.2 5.2 %copy-start.15 = (bf16[2,192,1152]{2,1,0:T(8,128)(2,1)S(1)}, bf16[2,192,1152]{2,1,0:T(8,128)(2,1)}, u32[]{:S(2)}) copy-start(bf16[2,192,1152]{2,1,0:T(8,128)(2,1)} %get-tuple-element.33) | copy-start | bytes 2654212
  271.8 1.1 copy-start.12
  282.8 61.1 %copy-start.4 = (bf16[192,2048]{1,0:T(8,128)(2,1)S(1)}, bf16[192,2048]{1,0:T(8,128)(2,1)}, u32[]{:S(2)}) copy-start(bf16[192,2048]{1,0:T(8,128)(2,1)} %copy-done.3) | copy-start | bytes 2359300
  433.7 2.6 copy-start.14
  436.3 1.0 copy-start.16
  441.7 2.9 copy-start.11
  444.6 3.0 copy-start.10
  447.6 3.0 copy-start.9
  450.6 1.7 copy-start.1
Sparse Core Ops, SparseCore 0:
  11.4 104.6 all-gather.2
  266.3 59.1 reduce-scatter.1
